TPU v7x, 128 devices: a whole 4x4x4 slice. The times are simulated.
128 devices in a mesh: ens: 4 (over x), cols: 32 (over z, y, core).
Axes of the slice: x: 4, y: 4, z: 4, core: 2. Of those that a mesh axis runs over, the one named last changes fastest.
Arguments:
- static_control: float32 [16, 64, 4096], P(None, 'cols'), may hold values from -6 to 6
- ensemble_control: float32 [32, 16, 64, 4096], P('ens', None, 'cols'), may hold values from -6 to 6
- perturbations: bfloat16 [32, 16, 64, 4096], P('ens', None, 'cols'), may hold values from -6 to 6
- vertical_root: float32 [16, 16], replicated, may hold values from 0 to 1.5
- vertical_local: float32 [16, 16], replicated, may hold values from 0 to 1.5
- face_north: float32 [64, 4096], P('cols'), may hold values from 0.02 to 0.24
- face_east: float32 [64, 4096], P('cols'), may hold values from 0.02 to 0.24
- innovation: float32 [2097152], P('cols'), may hold values from -6 to 6
- obs_weight: float32 [2097152], P('cols'), may hold values from 0.5 to 4
- obs_slot: int32 [2097152], P('cols'), may hold values from 0 to 32767
- send_index: int32 [1024, 1024], P('cols'), may hold values from 0 to 131071
- send_count: int32 [1024], P('cols'), may hold values from 256 to 1024, as said below
Outputs:
- static_grad: float32 [16, 64, 4096], P(None, 'cols')
- ensemble_grad: float32 [32, 16, 64, 4096], P('ens', None, 'cols')
Inputs may be any that keep to these rules, and one draw needn't show every extreme that they name: `send_count`: in every draw one observation owner, drawn from the seed, receives full lists (count 1024) from every column owner; all other counts are drawn independently.
All inputs are finite; a program needn't handle non-finite values.
Results may differ from a plain program's by a relative error of at most 0.0003.
Values sent between devices are 32-bit elements; how exact they have to be, the bound alone decides.
A program may use at most 128 MiB of HBM per device.

v0:
```python
import math

import jax
import jax.numpy as jnp
from jax import lax
from jax.sharding import PartitionSpec as P

NDIFF = 4


precise = lax.Precision.HIGHEST


def shifted(shard, axis, by):
    length = lax.axis_size(axis)
    pairs = [(i, i + by) for i in range(length) if 0 <= i + by < length]
    return lax.ppermute(shard, axis, pairs)


def with_halo(cells, sides, width):
    for axis, dim in sides:
        count = lax.axis_size(axis)
        ends = count - 1
        head = lax.slice_in_dim(cells, 0, width, axis=dim)
        tail = lax.slice_in_dim(cells, cells.shape[dim] - width, cells.shape[dim], axis=dim)
        cells = jnp.concatenate(
            [
                lax.ppermute(tail, axis, [(i, (i + 1) % count) for i in range(ends)]),
                cells,
                lax.ppermute(head, axis, [((i + 1) % count, i) for i in range(ends)]),
            ],
            axis=dim,
        )
    return cells


def smooth(source, padded, k_north, k_south, k_east):
    upper_rows = padded[:, :-2]
    lower_rows = padded[:, 2:]
    eastern = jnp.roll(source, -1, axis=2)
    western = jnp.roll(source, 1, axis=2)
    k_west = jnp.roll(k_east, 1, axis=1)
    return (
        source
        + k_north * (upper_rows - source)
        + k_south * (lower_rows - source)
        + k_east * (eastern - source)
        + k_west * (western - source)
    )


def vertical(matrix, source):
    return jnp.einsum("lm,mrc->lrc", matrix, source, precision=precise)


def lane_count(total):
    return math.gcd(total, 128)


def lane_select(index, lanes):
    return (index % lanes)[..., None] == jnp.arange(lanes, dtype=jnp.int32)


def pick(table, index):
    lanes = lane_count(table.size)
    grid = table.reshape(-1, lanes)
    rows = jnp.take(grid, index // lanes, axis=0)
    return jnp.sum(jnp.where(lane_select(index, lanes), rows, 0.0), axis=-1)


def spread(amounts, index, total):
    lanes = lane_count(total)
    rows = jnp.where(lane_select(index, lanes), amounts[..., None], 0.0).reshape(-1, lanes)
    grid = jnp.zeros((total // lanes, lanes), jnp.float32)
    return grid.at[(index // lanes).reshape(-1)].add(rows).reshape(-1)


def local(
    static_control,
    ensemble_control,
    perturbations,
    vertical_root,
    vertical_local,
    face_north,
    face_east,
    innovation,
    obs_weight,
    obs_slot,
    send_index,
    send_count,
):
    south_rim = shifted(face_north[:1], "cols", -1)
    k_south = jnp.concatenate([face_north[1:], south_rim], axis=0)

    def diffuse(source):
        for repeat in range(NDIFF):
            padded = with_halo(source, (("cols", 1),), 1)
            source = smooth(source, padded, face_north, k_south, face_east)
        return source

    members = ensemble_control.shape[0] * lax.axis_size("ens")
    member_scale = 1.0 / math.sqrt(members - 1)
    localized = jnp.einsum("lm,kmrc->klrc", vertical_local, ensemble_control, precision=precise)
    ens_part = member_scale * jnp.sum(perturbations.astype(jnp.float32) * localized, axis=0)
    static_increment = diffuse(vertical(vertical_root, static_control))
    peer_count = lax.axis_size("cols")
    capacity = send_index.shape[1]
    live_mask = (jnp.arange(capacity, dtype=jnp.int32)[None, :] < send_count[:, None]).astype(
        jnp.float32
    )
    increment = lax.psum(ens_part, "ens")
    increment = static_increment + increment
    outgoing = pick(increment, send_index) * live_mask
    incoming = lax.all_to_all(outgoing, "cols", split_axis=0, concat_axis=0, tiled=True)
    slot_total = peer_count * capacity
    lanes = lane_count(slot_total)
    slot_grid = incoming.reshape(-1, lanes)
    row_onehot = (
        (obs_slot // lanes)[:, None] == jnp.arange(slot_total // lanes, dtype=jnp.int32)[None, :]
    ).astype(jnp.float32)
    lane_mask = lane_select(obs_slot, lanes)
    picked_rows = jnp.dot(row_onehot, slot_grid, precision=precise)
    model_eq = jnp.sum(jnp.where(lane_mask, picked_rows, 0.0), axis=1)
    weighted = obs_weight * (model_eq - innovation)
    weighted_rows = jnp.where(lane_mask, weighted[:, None], 0.0)
    returned = jnp.dot(row_onehot.T, weighted_rows, precision=precise).reshape(peer_count, capacity)
    arrived = lax.all_to_all(returned, "cols", split_axis=0, concat_axis=0, tiled=True) * live_mask
    cell_total = static_control.size
    adjoint = spread(arrived, send_index, cell_total).reshape(static_control.shape)
    smoothed = diffuse(adjoint)
    static_grad = static_control + vertical(vertical_root.T, smoothed)
    weighted_perts = perturbations.astype(jnp.float32) * adjoint[None]
    ensemble_grad = ensemble_control + member_scale * jnp.einsum(
        "ml,kmrc->klrc", vertical_local, weighted_perts, precision=precise
    )
    return (static_grad, ensemble_grad)


def solution(mesh):
    placed = (
        P(None, "cols", None),
        P("ens", None, "cols", None),
        P("ens", None, "cols", None),
        P(),
        P(),
        P("cols", None),
        P("cols", None),
        P("cols"),
        P("cols"),
        P("cols"),
        P("cols", None),
        P("cols"),
    )
    return jax.shard_map(
        local,
        mesh=mesh,
        in_specs=placed,
        out_specs=(P(None, "cols", None), P("ens", None, "cols", None)),
        check_vma=False,
    )
```

profile of v0, /device:TPU:32, one launch (start us, length us, event | category | flops | bytes accessed | tf_op | source)
XLA Modules:
  0.0 624.0 jit_solution(7357855661467922733)
XLA Ops:
  8.1 3.9 collective-permute-start.1
  15.9 5.8 collective-permute-start.2
  21.7 10.6 %fusion.22 = f32[16,2,4096]{2,0,1:T(8,128)S(1)} fusion(f32[8,16,2,4096]{3,2,1,0:T(2,128)} %param.13, bf16[8,16,2,4096]{3,2,1,0:T(2,128)(2,1)} %param.14, f32[16,16]{1,0:T(8,128)S(1)} %copy-done), kind=kOutput, calls=%fused_computation.33 | convolution fusion | flops 204341248 | bytes 6816768 | tf_op jit(solution)/shard_map/lm,kmrc->klrc/dot_general | solution.py:103
  41.8 5.8 collective-permute-start.4
  53.7 6.1 collective-permute-start.6
  65.8 5.9 collective-permute-start.8
  72.0 3.9 all-reduce.2.cloned.1.call-done
  78.2 108.2 %gather_fusion = f32[32768,128]{1,0:T(8,128)} fusion(f32[1024,128]{1,0:T(8,128)S(1)} %reshape.124, s32[32768]{0:T(1024)S(1)} %broadcast_clamp_fusion), kind=kCustom, calls=%fused_computation | custom fusion | bytes 33685504 | tf_op jit(solution)/shard_map/jit(_take)/gather | solution.py:67
  186.4 18.0 %select_reduce_fusion = f32[32,1024]{1,0:T(8,128)S(1)} fusion(f32[32,1024,128]{2,1,0:T(8,128)} %bitcast.50, s32[32,1024]{1,0:T(8,128)S(1)} %get-tuple-element.58, pred[32,1024]{1,0:T(8,128)(4,1)S(1)} %copy-done.8), kind=kLoop, calls=%fused_computation.14 | loop fusion | flops 16744448 | bytes 17072128 | tf_op jit(solution)/shard_map/reduce_sum | solution.py:68
  205.2 9.0 %all-to-all-start = ((f32[32,1,1024]{2,1,0:T(1,128)}), f32[32,1,1024]{2,1,0:T(1,128)S(1)}, u32[]{:S(2)}, u32[]{:S(2)}) async-start(f32[32,1,1024]{2,1,0:T(1,128)} %compare_select_fusion.1), calls=%async_computation | async-start | bytes 262144 | tf_op jit(solution)/shard_map/all_to_all | solution.py:114
  214.4 6.4 %all-to-all-done = f32[32,1,1024]{2,1,0:T(1,128)S(1)} async-done(((f32[32,1,1024]{2,1,0:T(1,128)}), f32[32,1,1024]{2,1,0:T(1,128)S(1)}, u32[]{:S(2)}, u32[]{:S(2)}) %all-to-all-start) | async-done | bytes 131104 | tf_op jit(solution)/shard_map/all_to_all | solution.py:114
  220.8 41.6 %fusion.14 = f32[65536]{0:T(1024)S(1)} fusion(f32[256,128]{1,0:T(8,128)S(1)} %bitcast.59, s32[65536]{0:T(1024)S(1)} %get-tuple-element.57, s32[65536]{0:T(1024)S(1)} %get-tuple-element.56), kind=kOutput, calls=%fused_computation.21 | convolution fusion | flops 25811681280 | bytes 917504 | tf_op jit(solution)/shard_map/dot_general | solution.py:122
  262.5 3.3 fusion.169
  265.8 84.3 %fusion.1 = f32[256,128]{1,0:T(8,128)} fusion(s32[65536]{0:T(1024)S(1)} %get-tuple-element.57, f32[65536,128]{0,1:T(8,128)S(1)} %fusion.169), kind=kOutput, calls=%fused_computation.5 | convolution fusion | flops 25803358208 | bytes 33947648 | tf_op jit(solution)/shard_map/dot_general | solution.py:126
  350.2 5.0 all-to-all-start.1
  355.3 6.5 %all-to-all-done.1 = f32[32,1,1024]{2,1,0:T(1,128)S(1)} async-done(((f32[32,1,1024]{2,1,0:T(1,128)}), f32[32,1,1024]{2,1,0:T(1,128)S(1)}, u32[]{:S(2)}, u32[]{:S(2)}) %all-to-all-start.1) | async-done | bytes 131104 | tf_op jit(solution)/shard_map/all_to_all | solution.py:127
  361.8 195.2 %scatter_custom_fusion = f32[1024,128]{1,0:T(8,128)S(1)} fusion(s32[32768]{0:T(1024)} %bitcast.58, f32[]{:T(128)} %constant.64.clone.1, f32[32768]{0:T(1024)S(1)} %broadcast_select_fusion, s32[32768]{0:T(1024)S(1)} %bitcast.56), kind=kCustom, calls=%fused_computation.10 | custom fusion | flops 12582912 | bytes 787456 | tf_op jit(solution)/shard_map/scatter-add | solution.py:75
  557.9 3.8 collective-permute-start.10
  561.7 2.3 collective-permute-start.9
  564.0 9.5 %fusion.16 = f32[8,16,2,4096]{3,1,2,0:T(8,128)S(1)} fusion(f32[8,16,2,4096]{3,2,1,0:T(2,128)} %param.13, f32[16,2,4096]{2,0,1:T(8,128)S(1)} %copy.55, bf16[8,16,2,4096]{3,2,1,0:T(2,128)(2,1)S(1)} %copy-done.1, f32[16,16]{1,0:T(8,128)S(1)} %copy-done), kind=kOutput, calls=%fused_computation.24 | convolution fusion | flops 205520896 | bytes 11011072 | tf_op jit(solution)/shard_map/ml,kmrc->klrc/dot_general | solution.py:133
  573.4 5.3 copy.71
  581.1 5.8 collective-permute-start.12
  593.0 5.9 collective-permute-start.14
  605.1 5.9 collective-permute-start.16
  (104 shorter events, 51.6 us)
Async XLA Ops:
  7.2 68.7 %all-reduce.2.cloned.1.call-start = ((), (), s32[]{:S(2)}) async-start(), calls=%async_computation.2 | async-start | bytes 1048576 | tf_op jit(solution)/shard_map/psum | solution.py:111
  8.1 30.6 %collective-permute-start.1 = (f32[1,4096]{1,0:T(1,128)S(1)}, f32[1,4096]{1,0:T(1,128)S(1)}, u32[]{:S(2)}, u32[]{:S(2)}) collective-permute-start(f32[1,4096]{1,0:T(1,128)S(1)} %get-tuple-element.62), channel_id=1, source_target_pairs={{1,0},{2,1},{3,2},{4,3},{5,4},{6,5},{7,6},{8,7},{9,8},{10,9},{11,1... | collective-permute-start | bytes 49160 | tf_op jit(solution)/shard_map/ppermute | solution.py:17
  14.0 24.8 %collective-permute-start = (f32[16,1,4096]{2,0,1:T(8,128)S(1)}, f32[16,1,4096]{2,0,1:T(8,128)S(1)}, u32[]{:S(2)}, u32[]{:S(2)}) collective-permute-start(f32[16,1,4096]{2,0,1:T(8,128)S(1)} %get-tuple-element.54), channel_id=1, source_target_pairs={{0,1},{1,2},{2,3},{3,4},{4,5},{5,6},{6,7},{7,8},{8,9},{9,10},{10,1... | collective-permute-start | bytes 786440 | tf_op jit(solution)/shard_map/ppermute | solution.py:28
  15.9 22.9 %collective-permute-start.2 = (f32[16,1,4096]{2,0,1:T(8,128)S(1)}, f32[16,1,4096]{2,0,1:T(8,128)S(1)}, u32[]{:S(2)}, u32[]{:S(2)}) collective-permute-start(f32[16,1,4096]{2,0,1:T(8,128)S(1)} %get-tuple-element.55), channel_id=1, source_target_pairs={{1,0},{2,1},{3,2},{4,3},{5,4},{6,5},{7,6},{8,7},{9,8},{10,9},{11,1... | collective-permute-start | bytes 786440 | tf_op jit(solution)/shard_map/ppermute | solution.py:30
  39.9 9.8 %collective-permute-start.3 = (f32[16,1,4096]{2,0,1:T(8,128)S(1)}, f32[16,1,4096]{2,0,1:T(8,128)S(1)}, u32[]{:S(2)}, u32[]{:S(2)}) collective-permute-start(f32[16,1,4096]{2,0,1:T(8,128)S(1)} %get-tuple-element.48), channel_id=1, source_target_pairs={{0,1},{1,2},{2,3},{3,4},{4,5},{5,6},{6,7},{7,8},{8,9},{9,10},{10,1... | collective-permute-start | bytes 786440 | tf_op jit(solution)/shard_map/ppermute | solution.py:28
  41.8 9.6 %collective-permute-start.4 = (f32[16,1,4096]{2,0,1:T(8,128)S(1)}, f32[16,1,4096]{2,0,1:T(8,128)S(1)}, u32[]{:S(2)}, u32[]{:S(2)}) collective-permute-start(f32[16,1,4096]{2,0,1:T(8,128)S(1)} %get-tuple-element.49), channel_id=1, source_target_pairs={{1,0},{2,1},{3,2},{4,3},{5,4},{6,5},{7,6},{8,7},{9,8},{10,9},{11,1... | collective-permute-start | bytes 786440 | tf_op jit(solution)/shard_map/ppermute | solution.py:30
  51.8 10.0 %collective-permute-start.5 = (f32[16,1,4096]{2,0,1:T(8,128)S(1)}, f32[16,1,4096]{2,0,1:T(8,128)S(1)}, u32[]{:S(2)}, u32[]{:S(2)}) collective-permute-start(f32[16,1,4096]{2,0,1:T(8,128)S(1)} %get-tuple-element.42), channel_id=1, source_target_pairs={{0,1},{1,2},{2,3},{3,4},{4,5},{5,6},{6,7},{7,8},{8,9},{9,10},{10,1... | collective-permute-start | bytes 786440 | tf_op jit(solution)/shard_map/ppermute | solution.py:28
  53.7 9.8 %collective-permute-start.6 = (f32[16,1,4096]{2,0,1:T(8,128)S(1)}, f32[16,1,4096]{2,0,1:T(8,128)S(1)}, u32[]{:S(2)}, u32[]{:S(2)}) collective-permute-start(f32[16,1,4096]{2,0,1:T(8,128)S(1)} %get-tuple-element.43), channel_id=1, source_target_pairs={{1,0},{2,1},{3,2},{4,3},{5,4},{6,5},{7,6},{8,7},{9,8},{10,9},{11,1... | collective-permute-start | bytes 786440 | tf_op jit(solution)/shard_map/ppermute | solution.py:30
  63.9 12.1 %collective-permute-start.7 = (f32[16,1,4096]{2,0,1:T(8,128)S(1)}, f32[16,1,4096]{2,0,1:T(8,128)S(1)}, u32[]{:S(2)}, u32[]{:S(2)}) collective-permute-start(f32[16,1,4096]{2,0,1:T(8,128)S(1)} %get-tuple-element.36), channel_id=1, source_target_pairs={{0,1},{1,2},{2,3},{3,4},{4,5},{5,6},{6,7},{7,8},{8,9},{9,10},{10,1... | collective-permute-start | bytes 786440 | tf_op jit(solution)/shard_map/ppermute | solution.py:28
  65.8 10.1 %collective-permute-start.8 = (f32[16,1,4096]{2,0,1:T(8,128)S(1)}, f32[16,1,4096]{2,0,1:T(8,128)S(1)}, u32[]{:S(2)}, u32[]{:S(2)}) collective-permute-start(f32[16,1,4096]{2,0,1:T(8,128)S(1)} %get-tuple-element.37), channel_id=1, source_target_pairs={{1,0},{2,1},{3,2},{4,3},{5,4},{6,5},{7,6},{8,7},{9,8},{10,9},{11,1... | collective-permute-start | bytes 786440 | tf_op jit(solution)/shard_map/ppermute | solution.py:30
  78.2 108.2 %copy-start.8 = (pred[32,1024]{1,0:T(8,128)(4,1)S(1)}, pred[32,1024]{1,0:T(8,128)(4,1)}, u32[]{:S(2)}) copy-start(pred[32,1024]{1,0:T(8,128)(4,1)} %compare_and_fusion) | copy-start | bytes 98308
  205.2 15.6 %all-to-all-start = ((f32[32,1,1024]{2,1,0:T(1,128)}), f32[32,1,1024]{2,1,0:T(1,128)S(1)}, u32[]{:S(2)}, u32[]{:S(2)}) async-start(f32[32,1,1024]{2,1,0:T(1,128)} %compare_select_fusion.1), calls=%async_computation | async-start | bytes 262144 | tf_op jit(solution)/shard_map/all_to_all | solution.py:114
  265.8 298.1 %copy-start.1 = (bf16[8,16,2,4096]{3,2,1,0:T(2,128)(2,1)S(1)}, bf16[8,16,2,4096]{3,2,1,0:T(2,128)(2,1)}, u32[]{:S(2)}) copy-start(bf16[8,16,2,4096]{3,2,1,0:T(2,128)(2,1)} %param.14) | copy-start | bytes 6291460
  350.2 11.7 %all-to-all-start.1 = ((f32[32,1,1024]{2,1,0:T(1,128)}), f32[32,1,1024]{2,1,0:T(1,128)S(1)}, u32[]{:S(2)}, u32[]{:S(2)}) async-start(f32[32,1,1024]{2,1,0:T(1,128)} %bitcast.7), calls=%async_computation.1 | async-start | bytes 262144 | tf_op jit(solution)/shard_map/all_to_all | solution.py:127
  557.9 20.9 %collective-permute-start.10 = (f32[16,1,4096]{2,0,1:T(8,128)S(1)}, f32[16,1,4096]{2,0,1:T(8,128)S(1)}, u32[]{:S(2)}, u32[]{:S(2)}) collective-permute-start(f32[16,1,4096]{2,0,1:T(8,128)S(1)} %get-tuple-element.31), channel_id=1, source_target_pairs={{1,0},{2,1},{3,2},{4,3},{5,4},{6,5},{7,6},{8,7},{9,8},{10,9},{11,1... | collective-permute-start | bytes 786440 | tf_op jit(solution)/shard_map/ppermute | solution.py:30
  561.6 53.2 %copy-start.4 = (f32[16,2,4096]{2,1,0:T(2,128)S(1)}, f32[16,2,4096]{2,1,0:T(2,128)}, u32[]{:S(2)}) copy-start(f32[16,2,4096]{2,1,0:T(2,128)} %param.12) | copy-start | bytes 1572868
  561.6 53.2 %copy-start.9 = (f32[16,16]{1,0:T(8,128)S(1)}, f32[16,16]{1,0:T(8,128)}, u32[]{:S(2)}) copy-start(f32[16,16]{1,0:T(8,128)} %param.15) | copy-start | bytes 3076
  561.7 17.1 %collective-permute-start.9 = (f32[16,1,4096]{2,0,1:T(8,128)S(1)}, f32[16,1,4096]{2,0,1:T(8,128)S(1)}, u32[]{:S(2)}, u32[]{:S(2)}) collective-permute-start(f32[16,1,4096]{2,0,1:T(8,128)S(1)} %get-tuple-element.30), channel_id=1, source_target_pairs={{0,1},{1,2},{2,3},{3,4},{4,5},{5,6},{6,7},{7,8},{8,9},{9,10},{10,1... | collective-permute-start | bytes 786440 | tf_op jit(solution)/shard_map/ppermute | solution.py:28
  579.2 9.8 %collective-permute-start.11 = (f32[16,1,4096]{2,0,1:T(8,128)S(1)}, f32[16,1,4096]{2,0,1:T(8,128)S(1)}, u32[]{:S(2)}, u32[]{:S(2)}) collective-permute-start(f32[16,1,4096]{2,0,1:T(8,128)S(1)} %get-tuple-element.24), channel_id=1, source_target_pairs={{0,1},{1,2},{2,3},{3,4},{4,5},{5,6},{6,7},{7,8},{8,9},{9,10},{10,1... | collective-permute-start | bytes 786440 | tf_op jit(solution)/shard_map/ppermute | solution.py:28
  581.1 9.6 %collective-permute-start.12 = (f32[16,1,4096]{2,0,1:T(8,128)S(1)}, f32[16,1,4096]{2,0,1:T(8,128)S(1)}, u32[]{:S(2)}, u32[]{:S(2)}) collective-permute-start(f32[16,1,4096]{2,0,1:T(8,128)S(1)} %get-tuple-element.25), channel_id=1, source_target_pairs={{1,0},{2,1},{3,2},{4,3},{5,4},{6,5},{7,6},{8,7},{9,8},{10,9},{11,1... | collective-permute-start | bytes 786440 | tf_op jit(solution)/shard_map/ppermute | solution.py:30
  591.1 10.0 %collective-permute-start.13 = (f32[16,1,4096]{2,0,1:T(8,128)S(1)}, f32[16,1,4096]{2,0,1:T(8,128)S(1)}, u32[]{:S(2)}, u32[]{:S(2)}) collective-permute-start(f32[16,1,4096]{2,0,1:T(8,128)S(1)} %get-tuple-element.18), channel_id=1, source_target_pairs={{0,1},{1,2},{2,3},{3,4},{4,5},{5,6},{6,7},{7,8},{8,9},{9,10},{10,1... | collective-permute-start | bytes 786440 | tf_op jit(solution)/shard_map/ppermute | solution.py:28
  593.0 9.8 %collective-permute-start.14 = (f32[16,1,4096]{2,0,1:T(8,128)S(1)}, f32[16,1,4096]{2,0,1:T(8,128)S(1)}, u32[]{:S(2)}, u32[]{:S(2)}) collective-permute-start(f32[16,1,4096]{2,0,1:T(8,128)S(1)} %get-tuple-element.19), channel_id=1, source_target_pairs={{1,0},{2,1},{3,2},{4,3},{5,4},{6,5},{7,6},{8,7},{9,8},{10,9},{11,1... | collective-permute-start | bytes 786440 | tf_op jit(solution)/shard_map/ppermute | solution.py:30
  603.2 10.0 %collective-permute-start.15 = (f32[16,1,4096]{2,0,1:T(8,128)S(1)}, f32[16,1,4096]{2,0,1:T(8,128)S(1)}, u32[]{:S(2)}, u32[]{:S(2)}) collective-permute-start(f32[16,1,4096]{2,0,1:T(8,128)S(1)} %get-tuple-element.12), channel_id=1, source_target_pairs={{0,1},{1,2},{2,3},{3,4},{4,5},{5,6},{6,7},{7,8},{8,9},{9,10},{10,1... | collective-permute-start | bytes 786440 | tf_op jit(solution)/shard_map/ppermute | solution.py:28
  605.1 9.8 %collective-permute-start.16 = (f32[16,1,4096]{2,0,1:T(8,128)S(1)}, f32[16,1,4096]{2,0,1:T(8,128)S(1)}, u32[]{:S(2)}, u32[]{:S(2)}) collective-permute-start(f32[16,1,4096]{2,0,1:T(8,128)S(1)} %get-tuple-element.13), channel_id=1, source_target_pairs={{1,0},{2,1},{3,2},{4,3},{5,4},{6,5},{7,6},{8,7},{9,8},{10,9},{11,1... | collective-permute-start | bytes 786440 | tf_op jit(solution)/shard_map/ppermute | solution.py:30
  (7 other events, 232.0 us)
Sparse Core Ops, SparseCore 0:
  33.3 42.5 all-reduce.1
where the time goes:
time: 627 us; the launch traced here: 624 us
  other arithmetic  227 us (36%)
  matrix products  149 us (24%)
  local copies, waits for them, and re-layouts  121 us (19%)
  starting transfers between devices  78.6 us (13%)
  waiting for transfers between devices  34.6 us (6%)
  between operations  14.6 us (2%)
    scatter-add x1, other arithmetic, spread(): return grid.at[(index // lanes).reshape(-1)].add(rows).reshape(-1)  195 us
    gather x1, local copies, waits for them, and re-layouts, pick(): rows = jnp.take(grid, index // lanes, axis=0)  108 us
    dot_general x1, matrix products, local(): jnp.dot(row_onehot.T, weighted_rows, precision=precise)  84.3 us
    ppermute x8, starting transfers between devices, with_halo(): lax.ppermute(head, axis, [((i + 1) % count, i) for i in range(ends)])  44.9 us
    dot_general x1, matrix products, local(): picked_rows = jnp.dot(row_onehot, slot_grid, precision=precise)  41.6 us
    reduce_sum x1, other arithmetic, pick(): return jnp.sum(jnp.where(lane_select(index, lanes), rows, 0.0), axis=-1)  18 us
    ppermute x8, starting transfers between devices, with_halo(): lax.ppermute(tail, axis, [(i, (i + 1) % count) for i in range(ends)])  15.7 us
  transfers between devices with their start and end apart: 20, of which 13 were waited for; matrix products, arithmetic and copies ran while one was open for 6% of the time, Pallas kernels for 0%

commit v1 on v0

v1 whole, which is shorter than its diff:
```python
import functools
import math

import jax
import jax.numpy as jnp
from jax import lax
from jax.experimental import pallas as pl
from jax.experimental.pallas import tpu as pltpu
from jax.sharding import PartitionSpec as P

NDIFF = 4
LANES = 128
VMEM_LIMIT = 48 * 1024 * 1024

precise = lax.Precision.HIGHEST

SMEM = pl.BlockSpec(memory_space=pltpu.SMEM)
VMEM = pl.BlockSpec(memory_space=pltpu.VMEM)


def params(**more):
    return pltpu.CompilerParams(vmem_limit_bytes=VMEM_LIMIT, **more)


def to_tiles(cells):
    lead = cells.shape[:-2]
    rows, length = cells.shape[-2:]
    split = cells.reshape(lead + (rows, length // LANES, LANES))
    return jnp.swapaxes(split, -3, -2).reshape(lead + (rows * length // LANES, LANES))


def from_tiles(tiles, rows):
    lead = tiles.shape[:-2]
    count = tiles.shape[-2] // rows
    split = tiles.reshape(lead + (count, rows, LANES))
    return jnp.swapaxes(split, -3, -2).reshape(lead + (rows, count * LANES))


def ens_kernel(scale, root_ref, control_ref, pert_ref, out_ref):
    levels = control_ref.shape[1]

    @pl.when(pl.program_id(0) == 0)
    def _():
        out_ref[...] = jnp.zeros_like(out_ref)

    def chunk(c, carry):
        rows = pl.ds(pl.multiple_of(c * 16, 16), 16)
        source = [control_ref[0, m, rows, :] for m in range(levels)]
        for l in range(levels):
            total = root_ref[l, 0] * source[0]
            for m in range(1, levels):
                total = total + root_ref[l, m] * source[m]
            out_ref[l, rows, :] += pert_ref[0, l, rows, :].astype(jnp.float32) * total * scale
        return carry

    lax.fori_loop(0, control_ref.shape[2] // 16, chunk, 0)


def ens_part(control, pert, root, scale):
    members, levels, rows, lanes = control.shape
    block = pl.BlockSpec((1, levels, rows, lanes), lambda k: (k, 0, 0, 0))
    return pl.pallas_call(
        functools.partial(ens_kernel, scale),
        grid=(members,),
        in_specs=[SMEM, block, block],
        out_specs=pl.BlockSpec((levels, rows, lanes), lambda k: (0, 0, 0)),
        out_shape=jax.ShapeDtypeStruct((levels, rows, lanes), jnp.float32),
        compiler_params=params(),
        name="ens_part",
    )(root, control, pert)


def grad_kernel(scale, root_ref, adjoint_ref, control_ref, pert_ref, out_ref):
    levels = control_ref.shape[1]

    def chunk(c, carry):
        rows = pl.ds(pl.multiple_of(c * 16, 16), 16)
        source = [
            pert_ref[0, m, rows, :].astype(jnp.float32) * adjoint_ref[m, rows, :] for m in range(levels)
        ]
        for l in range(levels):
            total = root_ref[0, l] * source[0]
            for m in range(1, levels):
                total = total + root_ref[m, l] * source[m]
            out_ref[0, l, rows, :] = control_ref[0, l, rows, :] + total * scale
        return carry

    lax.fori_loop(0, control_ref.shape[2] // 16, chunk, 0)


def ens_grad(adjoint, control, pert, root, scale):
    members, levels, rows, lanes = control.shape
    block = pl.BlockSpec((1, levels, rows, lanes), lambda k: (k, 0, 0, 0))
    return pl.pallas_call(
        functools.partial(grad_kernel, scale),
        grid=(members,),
        in_specs=[SMEM, pl.BlockSpec((levels, rows, lanes), lambda k: (0, 0, 0)), block, block],
        out_specs=block,
        out_shape=jax.ShapeDtypeStruct(control.shape, jnp.float32),
        compiler_params=params(),
        name="ens_grad",
    )(root, adjoint, control, pert)


def row_lookup(table_ref, row_ids, lane_ids):
    count = len(row_ids)

    def step(i, found):
        found = list(found)
        base = pl.multiple_of(i * 8, 8)
        rows = table_ref[pl.ds(base, 8), :]
        for s in range(8):
            row = jnp.broadcast_to(rows[s : s + 1, :], (8, LANES))
            for n in range(count):
                value = jnp.take_along_axis(row, lane_ids[n], axis=1)
                found[n] = jnp.where(row_ids[n] == base + s, value, found[n])
        return tuple(found)

    zero = jnp.zeros((8, LANES), jnp.float32)
    return lax.fori_loop(0, table_ref.shape[0] // 8, step, (zero,) * count)


def cell_place(index, first_cell, cells):
    inside = index - first_cell
    level = inside >> 13
    row = (level << 6) + (((inside >> 7) & 31) << 1) + ((inside >> 12) & 1)
    mine = (inside >= 0) & (inside < cells)
    return jnp.where(mine, row, -1), inside & (LANES - 1)


def live(counts_ref, first_list, slot0):
    rows = lax.broadcasted_iota(jnp.int32, (8, LANES), 0)
    limit = jnp.zeros((8, LANES), jnp.int32)
    for i in range(8):
        limit = jnp.where(rows == i, counts_ref[first_list + i], limit)
    slots = slot0 + lax.broadcasted_iota(jnp.int32, (8, LANES), 1)
    return slots < limit


def pick_kernel(first_ref, counts_ref, table_ref, index_ref, out_ref):
    lists, capacity = index_ref.shape
    cells = table_ref.shape[0] * LANES
    tiles = capacity // LANES

    def group(g, carry):
        places = []
        for t in range(tiles):
            index = index_ref[pl.ds(pl.multiple_of(g * 8, 8), 8), t * LANES : (t + 1) * LANES]
            row, lane = cell_place(index, first_ref[0], cells)
            row = jnp.where(live(counts_ref, g * 8, t * LANES), row, -1)
            places.append((row, lane))
        found = row_lookup(table_ref, [p[0] for p in places], [p[1] for p in places])
        for t in range(tiles):
            out_ref[pl.ds(g * 8 * tiles + t, 8, stride=tiles), :] = found[t]
        return carry

    lax.fori_loop(0, lists // 8, group, 0)


def pick(table, index, counts, first_cell):
    lists, capacity = index.shape
    return pl.pallas_call(
        pick_kernel,
        in_specs=[SMEM, SMEM, VMEM, VMEM],
        out_specs=VMEM,
        out_shape=jax.ShapeDtypeStruct((lists * capacity // LANES, LANES), jnp.float32),
        compiler_params=params(),
        name="pick",
    )(first_cell, counts, table, index)


def two_parts(values):
    high = values.astype(jnp.bfloat16)
    low = (values - high.astype(jnp.float32)).astype(jnp.bfloat16)
    return high, low


def one_hot_sum(rows, lanes, values, row_total):
    width = values.shape[1]
    one = jnp.bfloat16(1)
    zero = jnp.bfloat16(0)
    row_ids = lax.broadcasted_iota(jnp.int32, (row_total, width), 0)
    lane_ids = lax.broadcasted_iota(jnp.int32, (LANES, width), 0)
    row_hot = (rows == row_ids).astype(jnp.float32).astype(jnp.bfloat16)
    lane_hot = lanes == lane_ids
    high = values.astype(jnp.bfloat16).astype(jnp.float32)
    low = values - high
    parts = jnp.concatenate(
        [jnp.where(lane_hot, high, 0.0).astype(jnp.bfloat16), jnp.where(lane_hot, low, 0.0).astype(jnp.bfloat16)],
        axis=0,
    )
    both = lax.dot_general(
        row_hot, parts, (((1,), (1,)), ((), ())), preferred_element_type=jnp.float32
    )
    return both


def as_row(block):
    return jnp.concatenate([block[i : i + 1, :] for i in range(block.shape[0])], axis=1)


def obs_kernel(first_ref, table_ref, slot_ref, innovation_ref, weight_ref, out_ref, both_ref):
    rows = table_ref.shape[0]
    both_ref[...] = jnp.zeros_like(both_ref)
    group = 4

    def step(i, carry):
        base = pl.multiple_of(i * 8 * group, 8 * group)
        row_ids, lane_ids = [], []
        for n in range(group):
            inside = slot_ref[pl.ds(base + 8 * n, 8), :] - first_ref[0]
            row_ids.append(inside >> 7)
            lane_ids.append(inside & (LANES - 1))
        found = row_lookup(table_ref, row_ids, lane_ids)
        for n in range(group):
            at = pl.ds(base + 8 * n, 8)
            mine = (row_ids[n] >= 0) & (row_ids[n] < rows)
            weighted = jnp.where(mine, weight_ref[at, :] * (found[n] - innovation_ref[at, :]), 0.0)
            both_ref[...] += one_hot_sum(as_row(row_ids[n]), as_row(lane_ids[n]), as_row(weighted), rows)
        return carry

    lax.fori_loop(0, slot_ref.shape[0] // (8 * group), step, 0)
    out_ref[...] = both_ref[:, :LANES] + both_ref[:, LANES:]


def observe(table, slots, innovation, weight, first_slot):
    rows = table.shape[0]
    shaped = [a.reshape(-1, LANES) for a in (slots, innovation, weight)]
    return pl.pallas_call(
        obs_kernel,
        in_specs=[SMEM, VMEM, VMEM, VMEM, VMEM],
        out_specs=VMEM,
        out_shape=jax.ShapeDtypeStruct((rows, LANES), jnp.float32),
        scratch_shapes=[pltpu.VMEM((rows, 2 * LANES), jnp.float32)],
        compiler_params=params(),
        name="observe",
    )(first_slot, table, *shaped)


def spread_kernel(first_ref, counts_ref, arrived_ref, index_ref, out_ref, both_ref):
    lists, capacity = index_ref.shape
    tiles = capacity // LANES
    rows = out_ref.shape[0]
    cells = rows * LANES
    both_ref[...] = jnp.zeros_like(both_ref)

    def step(q, carry):
        values = as_row(arrived_ref[pl.ds(pl.multiple_of(q * tiles, tiles), tiles), :])
        index = index_ref[pl.ds(q, 1), :]
        row, lane = cell_place(index, first_ref[0], cells)
        slots = lax.broadcasted_iota(jnp.int32, (1, capacity), 1)
        values = jnp.where(slots < counts_ref[q], values, 0.0)
        both_ref[...] += one_hot_sum(row, lane, values, rows)
        return carry

    lax.fori_loop(0, lists, step, 0)
    out_ref[...] = both_ref[:, :LANES] + both_ref[:, LANES:]


def spread(arrived, index, counts, first_cell, rows):
    return pl.pallas_call(
        spread_kernel,
        in_specs=[SMEM, SMEM, VMEM, VMEM],
        out_specs=VMEM,
        out_shape=jax.ShapeDtypeStruct((rows, LANES), jnp.float32),
        scratch_shapes=[pltpu.VMEM((rows, 2 * LANES), jnp.float32)],
        compiler_params=params(),
        name="spread",
    )(first_cell, counts, arrived, index)


def shifted(shard, axis, by):
    length = lax.axis_size(axis)
    pairs = [(i, i + by) for i in range(length) if 0 <= i + by < length]
    return lax.ppermute(shard, axis, pairs)


def smooth(source, padded, k_north, k_south, k_east):
    upper_rows = padded[:, :-2]
    lower_rows = padded[:, 2:]
    eastern = jnp.roll(source, -1, axis=2)
    western = jnp.roll(source, 1, axis=2)
    k_west = jnp.roll(k_east, 1, axis=1)
    return (
        source
        + k_north * (upper_rows - source)
        + k_south * (lower_rows - source)
        + k_east * (eastern - source)
        + k_west * (western - source)
    )


def local(
    static_control,
    ensemble_control,
    perturbations,
    vertical_root,
    vertical_local,
    face_north,
    face_east,
    innovation,
    obs_weight,
    obs_slot,
    send_index,
    send_count,
):
    south_rim = shifted(face_north[:1], "cols", -1)
    k_south = jnp.concatenate([face_north[1:], south_rim], axis=0)

    def diffuse(source):
        for repeat in range(NDIFF):
            padded = jnp.concatenate(
                [shifted(source[:, -1:], "cols", 1), source, shifted(source[:, :1], "cols", -1)], axis=1
            )
            source = smooth(source, padded, face_north, k_south, face_east)
        return source

    levels, grid_rows, length = static_control.shape
    ens = lax.axis_size("ens")
    me = lax.axis_index("ens")
    own_levels = levels // ens
    member_scale = 1.0 / math.sqrt(ensemble_control.shape[0] * ens - 1)
    first_level = me * own_levels
    first_cell = (first_level * grid_rows * length).astype(jnp.int32).reshape(1)
    lists, capacity = send_index.shape
    list_rows = capacity // LANES
    own_lists = lists // ens

    control = to_tiles(ensemble_control)
    pert = to_tiles(perturbations)

    part = ens_part(control, pert, vertical_local, member_scale)
    own_root = lax.dynamic_slice_in_dim(vertical_root, first_level, own_levels, 0)
    static_increment = diffuse(jnp.einsum("lm,mrc->lrc", own_root, static_control, precision=precise))
    increment = lax.psum_scatter(part, "ens", scatter_dimension=0, tiled=True) + to_tiles(static_increment)
    picked = pick(increment.reshape(-1, LANES), send_index, send_count, first_cell)
    picked = lax.psum(picked, "ens").reshape(lists, list_rows, LANES)
    table = lax.all_to_all(picked, "cols", split_axis=0, concat_axis=0, tiled=True)
    table = lax.dynamic_slice_in_dim(table, me * own_lists, own_lists, 0).reshape(-1, LANES)
    first_slot = (me * own_lists * capacity).astype(jnp.int32).reshape(1)
    returned = observe(table, obs_slot, innovation, obs_weight, first_slot)
    sent = lax.dynamic_update_slice_in_dim(
        jnp.zeros((lists, list_rows, LANES), jnp.float32),
        returned.reshape(own_lists, list_rows, LANES),
        me * own_lists,
        0,
    )
    arrived = lax.psum(lax.all_to_all(sent, "cols", split_axis=0, concat_axis=0, tiled=True), "ens")
    adjoint = spread(arrived.reshape(-1, LANES), send_index, send_count, first_cell, own_levels * 64)
    adjoint = adjoint.reshape(own_levels, 64, LANES)
    whole = lax.all_gather(adjoint, "ens", axis=0, tiled=True)
    smoothed = diffuse(from_tiles(adjoint, grid_rows))
    smoothed = lax.all_gather(smoothed, "ens", axis=0, tiled=True)
    static_grad = static_control + jnp.einsum("ml,mrc->lrc", vertical_root, smoothed, precision=precise)
    ensemble_grad = ens_grad(whole, control, pert, vertical_local, member_scale)
    return (static_grad, from_tiles(ensemble_grad, grid_rows))


def solution(mesh):
    placed = (
        P(None, "cols", None),
        P("ens", None, "cols", None),
        P("ens", None, "cols", None),
        P(),
        P(),
        P("cols", None),
        P("cols", None),
        P("cols"),
        P("cols"),
        P("cols"),
        P("cols", None),
        P("cols"),
    )
    return jax.shard_map(
        local,
        mesh=mesh,
        in_specs=placed,
        out_specs=(P(None, "cols", None), P("ens", None, "cols", None)),
        check_vma=False,
    )
```

time: 627 us -> 336 us (0.54)
  other arithmetic: 227 us -> 2.37 us
  matrix products: 149 us -> 2.8 us
  local copies, waits for them, and re-layouts: 121 us -> 7.47 us
  Pallas kernels: 0 us -> 96.5 us
  waiting for transfers between devices: 34.6 us -> 101 us
  blocking collectives: 0 us -> 37.3 us
    scatter-add x1 -> x0, other arithmetic: 195 us -> none  [spread(): return grid.at[(index // lanes).reshape(-1)].add(rows).reshape(-1)]
    dot_general x6 -> x2, matrix products: 149 us -> 2.8 us  [the longest x1 1.68 us: local(): jnp.einsum('lm,mrc->lrc', own_root, static_control, precision=precise)]
    gather x1 -> x0, local copies, waits for them, and re-layouts: 108 us -> none  [pick(): rows = jnp.take(grid, index // lanes, axis=0)]
    pallas_call x0 -> x5, Pallas kernels: none -> 96.5 us  [the longest x1 32.6 us: pick(): pl.pallas_call(pick_kernel, in_specs=[SMEM, SMEM, VMEM, VMEM], out_specs=...]
    psum x1 -> x2, waiting for transfers between devices: 3.92 us -> 83.4 us  [the longest x1 44.3 us: local(): picked = lax.psum(picked, 'ens').reshape(lists, list_rows, LANES)]
    ppermute x1 -> x17, starting transfers between devices: 3.91 us -> 65.6 us  [shifted(): return lax.ppermute(shard, axis, pairs)]
    ppermute x16 -> x0, starting transfers between devices: 60.6 us -> none  [the longest x8 44.9 us: with_halo(): lax.ppermute(head, axis, [((i + 1) % count, i) for i in range(ends)])]
    all_gather x0 -> x2, blocking collectives: none -> 25.8 us  [the longest x1 13.1 us: local(): smoothed = lax.all_gather(smoothed, 'ens', axis=0, tiled=True)]
  transfers between devices with their start and end apart: 20 -> 21, of which waited for: 13 -> 9; matrix products, arithmetic and copies ran while one was open for 6% -> 1% of each run, Pallas kernels for 0% -> 6%
where the time goes in v1:
time: 336 us; the launch traced here: 335 us
  waiting for transfers between devices  101 us (30%)
  Pallas kernels  96.5 us (29%)
  starting transfers between devices  73.2 us (22%)
  blocking collectives  37.3 us (11%)
  between operations  14.3 us (4%)
  local copies, waits for them, and re-layouts  7.47 us (2%)
    ppermute x17, starting transfers between devices, shifted(): return lax.ppermute(shard, axis, pairs)  65.6 us
    psum x1, waiting for transfers between devices, local(): picked = lax.psum(picked, 'ens').reshape(lists, list_rows, LANES)  44.3 us
    psum x1, waiting for transfers between devices, local(): lax.psum(lax.all_to_all(sent, 'cols', split_axis=0, concat_axis=0, tiled=...  39.1 us
    pallas_call x1, Pallas kernels, pick(): pl.pallas_call(pick_kernel, in_specs=[SMEM, SMEM, VMEM, VMEM], out_specs=...  32.6 us
    pallas_call x1, Pallas kernels, observe(): pl.pallas_call(obs_kernel, in_specs=[SMEM, VMEM, VMEM, VMEM, VMEM], out_s...  32.2 us
    all_gather x1, blocking collectives, local(): smoothed = lax.all_gather(smoothed, 'ens', axis=0, tiled=True)  13.1 us
    all_gather x1, blocking collectives, local(): whole = lax.all_gather(adjoint, 'ens', axis=0, tiled=True)  12.8 us
    pallas_call x1, Pallas kernels, spread(): pl.pallas_call(spread_kernel, in_specs=[SMEM, SMEM, VMEM, VMEM], out_spec...  12.4 us
  transfers between devices with their start and end apart: 21, of which 9 were waited for; matrix products, arithmetic and copies ran while one was open for 1% of the time, Pallas kernels for 6%

profile of v1, /device:TPU:32, one launch (start us, length us, event | category | flops | bytes accessed | tf_op | source)
XLA Modules:
  0.0 334.8 jit_solution(11872022894367421973)
XLA Ops:
  8.1 3.9 %collective-permute-start.1 = (f32[1,4096]{1,0:T(1,128)S(1)}, f32[1,4096]{1,0:T(1,128)S(1)}, u32[]{:S(2)}, u32[]{:S(2)}) collective-permute-start(f32[1,4096]{1,0:T(1,128)S(1)} %get-tuple-element.55), channel_id=1, source_target_pairs={{1,0},{2,1},{3,2},{4,3},{5,4},{6,5},{7,6},{8,7},{9,8},{10,9},{11,1... | collective-permute-start | bytes 49160 | tf_op jit(solution)/shard_map/ppermute | solution.py:275
  13.8 1.9 collective-permute-start
  15.7 5.8 %collective-permute-start.2 = (f32[4,1,4096]{2,0,1:T(4,128)S(1)}, f32[4,1,4096]{2,0,1:T(4,128)S(1)}, u32[]{:S(2)}, u32[]{:S(2)}) collective-permute-start(f32[4,1,4096]{2,0,1:T(4,128)S(1)} %get-tuple-element.53), channel_id=1, source_target_pairs={{1,0},{2,1},{3,2},{4,3},{5,4},{6,5},{7,6},{8,7},{9,8},{10,9},{11,1... | collective-permute-start | bytes 196616 | tf_op jit(solution)/shard_map/ppermute | solution.py:275
  23.7 9.2 %ens_part.1 = f32[16,64,128]{2,1,0:T(8,128)} custom-call(f32[16,16]{1,0:T(8,128)S(1)} %copy-done.8, f32[8,16,64,128]{3,2,1,0:T(8,128)} %bitcast.59, bf16[8,16,64,128]{3,2,1,0:T(8,128)(2,1)S(1)} %bitcast.51), custom_call_target="tpu_custom_call" | custom-call | tf_op jit(solution)/shard_map/ens_part/pallas_call | solution.py:62
  35.8 5.8 %collective-permute-start.4 = (f32[4,1,4096]{2,0,1:T(4,128)S(1)}, f32[4,1,4096]{2,0,1:T(4,128)S(1)}, u32[]{:S(2)}, u32[]{:S(2)}) collective-permute-start(f32[4,1,4096]{2,0,1:T(4,128)S(1)} %get-tuple-element.47), channel_id=1, source_target_pairs={{1,0},{2,1},{3,2},{4,3},{5,4},{6,5},{7,6},{8,7},{9,8},{10,9},{11,1... | collective-permute-start | bytes 196616 | tf_op jit(solution)/shard_map/ppermute | solution.py:275
  43.8 2.1 collective-permute-start.5
  45.9 5.8 %collective-permute-start.6 = (f32[4,1,4096]{2,0,1:T(4,128)S(1)}, f32[4,1,4096]{2,0,1:T(4,128)S(1)}, u32[]{:S(2)}, u32[]{:S(2)}) collective-permute-start(f32[4,1,4096]{2,0,1:T(4,128)S(1)} %get-tuple-element.41), channel_id=1, source_target_pairs={{1,0},{2,1},{3,2},{4,3},{5,4},{6,5},{7,6},{8,7},{9,8},{10,9},{11,1... | collective-permute-start | bytes 196616 | tf_op jit(solution)/shard_map/ppermute | solution.py:275
  53.9 1.9 collective-permute-start.7
  55.8 5.8 %collective-permute-start.8 = (f32[4,1,4096]{2,0,1:T(4,128)S(1)}, f32[4,1,4096]{2,0,1:T(4,128)S(1)}, u32[]{:S(2)}, u32[]{:S(2)}) collective-permute-start(f32[4,1,4096]{2,0,1:T(4,128)S(1)} %get-tuple-element.35), channel_id=1, source_target_pairs={{1,0},{2,1},{3,2},{4,3},{5,4},{6,5},{7,6},{8,7},{9,8},{10,9},{11,1... | collective-permute-start | bytes 196616 | tf_op jit(solution)/shard_map/ppermute | solution.py:275
  64.8 32.6 %pick.1 = f32[256,128]{1,0:T(8,128)} custom-call(s32[1]{0:T(128)} %bitcast.first_ref, s32[32]{0:T(128)S(1)} %copy-done.10, f32[256,128]{1,0:T(8,128)S(1)} %bitcast.55, s32[32,1024]{1,0:T(8,128)S(1)} %copy-done.3), custom_call_target="tpu_custom_call" | custom-call | tf_op jit(solution)/shard_map/pick/pallas_call | solution.py:162
  97.5 44.3 %all-reduce.3.cloned.1.call-done = f32[32,8,128]{2,1,0:T(8,128)} async-done(((f32[32,8,128]{2,1,0:T(8,128)}), f32[32,8,128]{2,1,0:T(8,128)}) %all-reduce.3.cloned.1.call-update) | async-done | bytes 131088 | tf_op jit(solution)/shard_map/psum | solution.py:337
  141.8 7.5 %all-to-all-start = ((f32[32,8,128]{2,1,0:T(8,128)}), f32[32,8,128]{2,1,0:T(8,128)S(1)}, u32[]{:S(2)}, u32[]{:S(2)}) async-start(f32[32,8,128]{2,1,0:T(8,128)} %all-reduce.3.cloned.1.call-done), calls=%async_computation.1 | async-start | bytes 262144 | tf_op jit(solution)/shard_map/all_to_all | solution.py:338
  149.4 6.5 %all-to-all-done = f32[32,8,128]{2,1,0:T(8,128)S(1)} async-done(((f32[32,8,128]{2,1,0:T(8,128)}), f32[32,8,128]{2,1,0:T(8,128)S(1)}, u32[]{:S(2)}, u32[]{:S(2)}) %all-to-all-start) | async-done | bytes 131104 | tf_op jit(solution)/shard_map/all_to_all | solution.py:338
  155.9 32.2 %observe.1 = f32[64,128]{1,0:T(8,128)S(1)} custom-call(s32[1]{0:T(128)} %bitcast.1.first_ref, f32[64,128]{1,0:T(8,128)S(1)} %dynamic-slice_bitcast_fusion.table_ref, s32[512,128]{1,0:T(8,128)S(1)} %bitcast.56, f32[512,128]{1,0:T(8,128)S(1)} %bitcast.57, f32[512,128]{1,0:T(8,128)S(1)} %bitcast.58), custom_call_target="tpu_custom_call" | custom-call | tf_op jit(solution)/shard_map/observe/pallas_call | solution.py:229
  188.2 11.5 %all_to_all.10 = f32[32,8,128]{2,1,0:T(8,128)} all-to-all(f32[32,8,128]{2,1,0:T(8,128)S(1)} %bitcast_dynamic-update-slice_fusion), channel_id=1, replica_groups=mesh['ens'=4,'cols'=32] {'cols'}, dimensions={0} | all-to-all | bytes 262144 | tf_op jit(solution)/shard_map/all_to_all | solution.py:348
  199.7 39.1 %all-reduce.5.cloned.1.call-done.arrived_ref = f32[256,128]{1,0:T(8,128)} async-done(((f32[256,128]{1,0:T(8,128)}), f32[256,128]{1,0:T(8,128)}) %all-reduce.5.cloned.1.call-update) | async-done | bytes 131088 | tf_op jit(solution)/shard_map/psum | solution.py:348
  239.7 12.4 %spread.1 = f32[256,128]{1,0:T(8,128)S(1)} custom-call(s32[1]{0:T(128)} %bitcast.first_ref, s32[32]{0:T(128)S(1)} %copy-done.10, f32[256,128]{1,0:T(8,128)S(1)} %copy-done.7, s32[32,1024]{1,0:T(8,128)S(1)} %copy-done.3), custom_call_target="tpu_custom_call" | custom-call | tf_op jit(solution)/shard_map/spread/pallas_call | solution.py:261
  254.3 5.8 %collective-permute-start.10 = (f32[4,1,4096]{2,0,1:T(4,128)S(1)}, f32[4,1,4096]{2,0,1:T(4,128)S(1)}, u32[]{:S(2)}, u32[]{:S(2)}) collective-permute-start(f32[4,1,4096]{2,0,1:T(4,128)S(1)} %get-tuple-element.29), channel_id=1, source_target_pairs={{1,0},{2,1},{3,2},{4,3},{5,4},{6,5},{7,6},{8,7},{9,8},{10,9},{11,1... | collective-permute-start | bytes 196616 | tf_op jit(solution)/shard_map/ppermute | solution.py:275
  260.1 12.8 %all_gather.7.adjoint_ref = f32[16,64,128]{2,1,0:T(8,128)S(1)} all-gather(f32[4,64,128]{2,1,0:T(8,128)S(1)} %bitcast.54), channel_id=1, replica_groups=mesh['ens'=4,'cols'=32] {'ens'}, dimensions={0}, use_global_device_ids=true | all-gather | bytes 655360 | tf_op jit(solution)/shard_map/all_gather | solution.py:351
  272.9 10.0 %ens_grad.1 = f32[8,16,64,128]{3,2,1,0:T(8,128)} custom-call(f32[16,16]{1,0:T(8,128)S(1)} %copy-done.9, f32[16,64,128]{2,1,0:T(8,128)S(1)} %all_gather.7.adjoint_ref, f32[8,16,64,128]{3,2,1,0:T(8,128)} %bitcast.60, bf16[8,16,64,128]{3,2,1,0:T(8,128)(2,1)S(1)} %bitcast.52), custom_call_target="tpu_custom_call" | custom-call | tf_op jit(solution)/shard_map/ens_grad/pallas_call | solution.py:94
  285.1 5.8 %collective-permute-start.12 = (f32[4,1,4096]{2,0,1:T(4,128)S(1)}, f32[4,1,4096]{2,0,1:T(4,128)S(1)}, u32[]{:S(2)}, u32[]{:S(2)}) collective-permute-start(f32[4,1,4096]{2,0,1:T(4,128)S(1)} %get-tuple-element.23), channel_id=1, source_target_pairs={{1,0},{2,1},{3,2},{4,3},{5,4},{6,5},{7,6},{8,7},{9,8},{10,9},{11,1... | collective-permute-start | bytes 196616 | tf_op jit(solution)/shard_map/ppermute | solution.py:275
  295.0 5.8 %collective-permute-start.14 = (f32[4,1,4096]{2,0,1:T(4,128)S(1)}, f32[4,1,4096]{2,0,1:T(4,128)S(1)}, u32[]{:S(2)}, u32[]{:S(2)}) collective-permute-start(f32[4,1,4096]{2,0,1:T(4,128)S(1)} %get-tuple-element.17), channel_id=1, source_target_pairs={{1,0},{2,1},{3,2},{4,3},{5,4},{6,5},{7,6},{8,7},{9,8},{10,9},{11,1... | collective-permute-start | bytes 196616 | tf_op jit(solution)/shard_map/ppermute | solution.py:275
  304.9 5.8 %collective-permute-start.16 = (f32[4,1,4096]{2,0,1:T(4,128)S(1)}, f32[4,1,4096]{2,0,1:T(4,128)S(1)}, u32[]{:S(2)}, u32[]{:S(2)}) collective-permute-start(f32[4,1,4096]{2,0,1:T(4,128)S(1)} %get-tuple-element.11), channel_id=1, source_target_pairs={{1,0},{2,1},{3,2},{4,3},{5,4},{6,5},{7,6},{8,7},{9,8},{10,9},{11,1... | collective-permute-start | bytes 196616 | tf_op jit(solution)/shard_map/ppermute | solution.py:275
  312.9 13.1 %all_gather.6 = f32[16,2,4096]{2,1,0:T(2,128)S(1)} all-gather(f32[4,2,4096]{2,1,0:T(2,128)S(1)} %copy.28), channel_id=1, replica_groups=mesh['ens'=4,'cols'=32] {'ens'}, dimensions={0}, use_global_device_ids=true | all-gather | bytes 655360 | tf_op jit(solution)/shard_map/all_gather | solution.py:353
  (105 shorter events, 33.3 us)
Async XLA Ops:
  7.2 56.7 %reduce-scatter.2.cloned.1.call-start = ((), (), s32[]{:S(2)}) async-start(), calls=%async_computation.3 | async-start | bytes 655360 | tf_op jit(solution)/shard_map/reduce_scatter | solution.py:335
  8.1 25.4 %collective-permute-start.1 = (f32[1,4096]{1,0:T(1,128)S(1)}, f32[1,4096]{1,0:T(1,128)S(1)}, u32[]{:S(2)}, u32[]{:S(2)}) collective-permute-start(f32[1,4096]{1,0:T(1,128)S(1)} %get-tuple-element.55), channel_id=1, source_target_pairs={{1,0},{2,1},{3,2},{4,3},{5,4},{6,5},{7,6},{8,7},{9,8},{10,9},{11,1... | collective-permute-start | bytes 49160 | tf_op jit(solution)/shard_map/ppermute | solution.py:275
  13.8 19.8 %collective-permute-start = (f32[4,1,4096]{2,0,1:T(4,128)S(1)}, f32[4,1,4096]{2,0,1:T(4,128)S(1)}, u32[]{:S(2)}, u32[]{:S(2)}) collective-permute-start(f32[4,1,4096]{2,0,1:T(4,128)S(1)} %get-tuple-element.52), channel_id=1, source_target_pairs={{0,1},{1,2},{2,3},{3,4},{4,5},{5,6},{6,7},{7,8},{8,9},{9,10},{10,1... | collective-permute-start | bytes 196616 | tf_op jit(solution)/shard_map/ppermute | solution.py:275
  15.7 17.8 %collective-permute-start.2 = (f32[4,1,4096]{2,0,1:T(4,128)S(1)}, f32[4,1,4096]{2,0,1:T(4,128)S(1)}, u32[]{:S(2)}, u32[]{:S(2)}) collective-permute-start(f32[4,1,4096]{2,0,1:T(4,128)S(1)} %get-tuple-element.53), channel_id=1, source_target_pairs={{1,0},{2,1},{3,2},{4,3},{5,4},{6,5},{7,6},{8,7},{9,8},{10,9},{11,1... | collective-permute-start | bytes 196616 | tf_op jit(solution)/shard_map/ppermute | solution.py:275
  33.0 122.9 %copy-start.5 = (f32[65536]{0:T(1024)S(1)}, f32[65536]{0:T(1024)}, u32[]{:S(2)}) copy-start(f32[65536]{0:T(1024)} %param.19) | copy-start | bytes 786436
  33.0 108.8 %all-reduce.3.cloned.1.call-start = ((), (), s32[]{:S(2)}) async-start(), calls=%async_computation.4 | async-start | bytes 262144 | tf_op jit(solution)/shard_map/psum | solution.py:337
  33.9 7.8 %collective-permute-start.3 = (f32[4,1,4096]{2,0,1:T(4,128)S(1)}, f32[4,1,4096]{2,0,1:T(4,128)S(1)}, u32[]{:S(2)}, u32[]{:S(2)}) collective-permute-start(f32[4,1,4096]{2,0,1:T(4,128)S(1)} %get-tuple-element.46), channel_id=1, source_target_pairs={{0,1},{1,2},{2,3},{3,4},{4,5},{5,6},{6,7},{7,8},{8,9},{9,10},{10,1... | collective-permute-start | bytes 196616 | tf_op jit(solution)/shard_map/ppermute | solution.py:275
  35.8 7.6 %collective-permute-start.4 = (f32[4,1,4096]{2,0,1:T(4,128)S(1)}, f32[4,1,4096]{2,0,1:T(4,128)S(1)}, u32[]{:S(2)}, u32[]{:S(2)}) collective-permute-start(f32[4,1,4096]{2,0,1:T(4,128)S(1)} %get-tuple-element.47), channel_id=1, source_target_pairs={{1,0},{2,1},{3,2},{4,3},{5,4},{6,5},{7,6},{8,7},{9,8},{10,9},{11,1... | collective-permute-start | bytes 196616 | tf_op jit(solution)/shard_map/ppermute | solution.py:275
  43.6 229.2 %copy-start.2 = (bf16[8,16,2,4096]{3,2,1,0:T(2,128)(2,1)S(1)}, bf16[8,16,2,4096]{3,2,1,0:T(2,128)(2,1)}, u32[]{:S(2)}) copy-start(bf16[8,16,2,4096]{3,2,1,0:T(2,128)(2,1)} %param.14) | copy-start | bytes 6291460
  43.6 229.2 %copy-start.9 = (f32[16,16]{1,0:T(8,128)S(1)}, f32[16,16]{1,0:T(8,128)}, u32[]{:S(2)}) copy-start(f32[16,16]{1,0:T(8,128)} %root_ref.3) | copy-start | bytes 3076
  43.8 7.9 %collective-permute-start.5 = (f32[4,1,4096]{2,0,1:T(4,128)S(1)}, f32[4,1,4096]{2,0,1:T(4,128)S(1)}, u32[]{:S(2)}, u32[]{:S(2)}) collective-permute-start(f32[4,1,4096]{2,0,1:T(4,128)S(1)} %get-tuple-element.40), channel_id=1, source_target_pairs={{0,1},{1,2},{2,3},{3,4},{4,5},{5,6},{6,7},{7,8},{8,9},{9,10},{10,1... | collective-permute-start | bytes 196616 | tf_op jit(solution)/shard_map/ppermute | solution.py:275
  45.9 7.7 %collective-permute-start.6 = (f32[4,1,4096]{2,0,1:T(4,128)S(1)}, f32[4,1,4096]{2,0,1:T(4,128)S(1)}, u32[]{:S(2)}, u32[]{:S(2)}) collective-permute-start(f32[4,1,4096]{2,0,1:T(4,128)S(1)} %get-tuple-element.41), channel_id=1, source_target_pairs={{1,0},{2,1},{3,2},{4,3},{5,4},{6,5},{7,6},{8,7},{9,8},{10,9},{11,1... | collective-permute-start | bytes 196616 | tf_op jit(solution)/shard_map/ppermute | solution.py:275
  53.9 7.8 %collective-permute-start.7 = (f32[4,1,4096]{2,0,1:T(4,128)S(1)}, f32[4,1,4096]{2,0,1:T(4,128)S(1)}, u32[]{:S(2)}, u32[]{:S(2)}) collective-permute-start(f32[4,1,4096]{2,0,1:T(4,128)S(1)} %get-tuple-element.34), channel_id=1, source_target_pairs={{0,1},{1,2},{2,3},{3,4},{4,5},{5,6},{6,7},{7,8},{8,9},{9,10},{10,1... | collective-permute-start | bytes 196616 | tf_op jit(solution)/shard_map/ppermute | solution.py:275
  55.8 7.7 %collective-permute-start.8 = (f32[4,1,4096]{2,0,1:T(4,128)S(1)}, f32[4,1,4096]{2,0,1:T(4,128)S(1)}, u32[]{:S(2)}, u32[]{:S(2)}) collective-permute-start(f32[4,1,4096]{2,0,1:T(4,128)S(1)} %get-tuple-element.35), channel_id=1, source_target_pairs={{1,0},{2,1},{3,2},{4,3},{5,4},{6,5},{7,6},{8,7},{9,8},{10,9},{11,1... | collective-permute-start | bytes 196616 | tf_op jit(solution)/shard_map/ppermute | solution.py:275
  141.8 14.1 %all-to-all-start = ((f32[32,8,128]{2,1,0:T(8,128)}), f32[32,8,128]{2,1,0:T(8,128)S(1)}, u32[]{:S(2)}, u32[]{:S(2)}) async-start(f32[32,8,128]{2,1,0:T(8,128)} %all-reduce.3.cloned.1.call-done), calls=%async_computation.1 | async-start | bytes 262144 | tf_op jit(solution)/shard_map/all_to_all | solution.py:338
  149.3 89.4 %all-reduce.5.cloned.1.call-start = ((), (), s32[]{:S(2)}) async-start(), calls=%async_computation.5 | async-start | bytes 262144 | tf_op jit(solution)/shard_map/psum | solution.py:348
  252.4 30.5 %collective-permute-start.9 = (f32[4,1,4096]{2,0,1:T(4,128)S(1)}, f32[4,1,4096]{2,0,1:T(4,128)S(1)}, u32[]{:S(2)}, u32[]{:S(2)}) collective-permute-start(f32[4,1,4096]{2,0,1:T(4,128)S(1)} %get-tuple-element.28), channel_id=1, source_target_pairs={{0,1},{1,2},{2,3},{3,4},{4,5},{5,6},{6,7},{7,8},{8,9},{9,10},{10,1... | collective-permute-start | bytes 196616 | tf_op jit(solution)/shard_map/ppermute | solution.py:275
  254.3 28.5 %collective-permute-start.10 = (f32[4,1,4096]{2,0,1:T(4,128)S(1)}, f32[4,1,4096]{2,0,1:T(4,128)S(1)}, u32[]{:S(2)}, u32[]{:S(2)}) collective-permute-start(f32[4,1,4096]{2,0,1:T(4,128)S(1)} %get-tuple-element.29), channel_id=1, source_target_pairs={{1,0},{2,1},{3,2},{4,3},{5,4},{6,5},{7,6},{8,7},{9,8},{10,9},{11,1... | collective-permute-start | bytes 196616 | tf_op jit(solution)/shard_map/ppermute | solution.py:275
  283.2 7.8 %collective-permute-start.11 = (f32[4,1,4096]{2,0,1:T(4,128)S(1)}, f32[4,1,4096]{2,0,1:T(4,128)S(1)}, u32[]{:S(2)}, u32[]{:S(2)}) collective-permute-start(f32[4,1,4096]{2,0,1:T(4,128)S(1)} %get-tuple-element.22), channel_id=1, source_target_pairs={{0,1},{1,2},{2,3},{3,4},{4,5},{5,6},{6,7},{7,8},{8,9},{9,10},{10,1... | collective-permute-start | bytes 196616 | tf_op jit(solution)/shard_map/ppermute | solution.py:275
  285.1 7.6 %collective-permute-start.12 = (f32[4,1,4096]{2,0,1:T(4,128)S(1)}, f32[4,1,4096]{2,0,1:T(4,128)S(1)}, u32[]{:S(2)}, u32[]{:S(2)}) collective-permute-start(f32[4,1,4096]{2,0,1:T(4,128)S(1)} %get-tuple-element.23), channel_id=1, source_target_pairs={{1,0},{2,1},{3,2},{4,3},{5,4},{6,5},{7,6},{8,7},{9,8},{10,9},{11,1... | collective-permute-start | bytes 196616 | tf_op jit(solution)/shard_map/ppermute | solution.py:275
  293.1 7.8 %collective-permute-start.13 = (f32[4,1,4096]{2,0,1:T(4,128)S(1)}, f32[4,1,4096]{2,0,1:T(4,128)S(1)}, u32[]{:S(2)}, u32[]{:S(2)}) collective-permute-start(f32[4,1,4096]{2,0,1:T(4,128)S(1)} %get-tuple-element.16), channel_id=1, source_target_pairs={{0,1},{1,2},{2,3},{3,4},{4,5},{5,6},{6,7},{7,8},{8,9},{9,10},{10,1... | collective-permute-start | bytes 196616 | tf_op jit(solution)/shard_map/ppermute | solution.py:275
  295.0 7.7 %collective-permute-start.14 = (f32[4,1,4096]{2,0,1:T(4,128)S(1)}, f32[4,1,4096]{2,0,1:T(4,128)S(1)}, u32[]{:S(2)}, u32[]{:S(2)}) collective-permute-start(f32[4,1,4096]{2,0,1:T(4,128)S(1)} %get-tuple-element.17), channel_id=1, source_target_pairs={{1,0},{2,1},{3,2},{4,3},{5,4},{6,5},{7,6},{8,7},{9,8},{10,9},{11,1... | collective-permute-start | bytes 196616 | tf_op jit(solution)/shard_map/ppermute | solution.py:275
  303.0 7.8 %collective-permute-start.15 = (f32[4,1,4096]{2,0,1:T(4,128)S(1)}, f32[4,1,4096]{2,0,1:T(4,128)S(1)}, u32[]{:S(2)}, u32[]{:S(2)}) collective-permute-start(f32[4,1,4096]{2,0,1:T(4,128)S(1)} %get-tuple-element.10), channel_id=1, source_target_pairs={{0,1},{1,2},{2,3},{3,4},{4,5},{5,6},{6,7},{7,8},{8,9},{9,10},{10,1... | collective-permute-start | bytes 196616 | tf_op jit(solution)/shard_map/ppermute | solution.py:275
  304.9 7.7 %collective-permute-start.16 = (f32[4,1,4096]{2,0,1:T(4,128)S(1)}, f32[4,1,4096]{2,0,1:T(4,128)S(1)}, u32[]{:S(2)}, u32[]{:S(2)}) collective-permute-start(f32[4,1,4096]{2,0,1:T(4,128)S(1)} %get-tuple-element.11), channel_id=1, source_target_pairs={{1,0},{2,1},{3,2},{4,3},{5,4},{6,5},{7,6},{8,7},{9,8},{10,9},{11,1... | collective-permute-start | bytes 196616 | tf_op jit(solution)/shard_map/ppermute | solution.py:275
  (11 other events, 400.1 us)
Sparse Core Ops, SparseCore 0:
  33.1 21.0 reduce-scatter.1
  97.6 44.1 all-reduce.2
  199.8 38.9 all-reduce.4

commit v2 on v1

--- a/solution.py
+++ b/solution.py
@@ -70,8 +70,21 @@
     )(root, control, pert)
 
 
-def grad_kernel(scale, root_ref, adjoint_ref, control_ref, pert_ref, out_ref):
+def grad_kernel(
+    scale,
+    local_ref,
+    root_ref,
+    adjoint_ref,
+    smooth_ref,
+    static_ref,
+    control_ref,
+    pert_ref,
+    out_ref,
+    static_out_ref,
+):
     levels = control_ref.shape[1]
+    k = pl.program_id(0)
+    share_of = levels // pl.num_programs(0)
 
     def chunk(c, carry):
         rows = pl.ds(pl.multiple_of(c * 16, 16), 16)
@@ -79,27 +92,37 @@
             pert_ref[0, m, rows, :].astype(jnp.float32) * adjoint_ref[m, rows, :] for m in range(levels)
         ]
         for l in range(levels):
-            total = root_ref[0, l] * source[0]
+            total = local_ref[0, l] * source[0]
             for m in range(1, levels):
-                total = total + root_ref[m, l] * source[m]
+                total = total + local_ref[m, l] * source[m]
             out_ref[0, l, rows, :] = control_ref[0, l, rows, :] + total * scale
+        for n in range(2):
+            l = k * share_of + n
+            total = static_ref[l, rows, :]
+            for m in range(levels):
+                total = total + root_ref[m, l] * smooth_ref[m, rows, :]
+            static_out_ref[l, rows, :] = total
         return carry
 
     lax.fori_loop(0, control_ref.shape[2] // 16, chunk, 0)
 
 
-def ens_grad(adjoint, control, pert, root, scale):
+def gradients(adjoint, smoothed, control, pert, static, local_root, root, scale):
     members, levels, rows, lanes = control.shape
     block = pl.BlockSpec((1, levels, rows, lanes), lambda k: (k, 0, 0, 0))
+    fixed = pl.BlockSpec((levels, rows, lanes), lambda k: (0, 0, 0))
     return pl.pallas_call(
         functools.partial(grad_kernel, scale),
         grid=(members,),
-        in_specs=[SMEM, pl.BlockSpec((levels, rows, lanes), lambda k: (0, 0, 0)), block, block],
-        out_specs=block,
-        out_shape=jax.ShapeDtypeStruct(control.shape, jnp.float32),
+        in_specs=[SMEM, SMEM, fixed, fixed, fixed, block, block],
+        out_specs=[block, fixed],
+        out_shape=[
+            jax.ShapeDtypeStruct(control.shape, jnp.float32),
+            jax.ShapeDtypeStruct(static.shape, jnp.float32),
+        ],
         compiler_params=params(),
-        name="ens_grad",
-    )(root, adjoint, control, pert)
+        name="gradients",
+    )(local_root, root, adjoint, smoothed, static, control, pert)
 
 
 def row_lookup(table_ref, row_ids, lane_ids):
@@ -269,25 +292,438 @@
     )(first_cell, counts, arrived, index)
 
 
-def shifted(shard, axis, by):
-    length = lax.axis_size(axis)
-    pairs = [(i, i + by) for i in range(length) if 0 <= i + by < length]
-    return lax.ppermute(shard, axis, pairs)
-
-
-def smooth(source, padded, k_north, k_south, k_east):
-    upper_rows = padded[:, :-2]
-    lower_rows = padded[:, 2:]
-    eastern = jnp.roll(source, -1, axis=2)
-    western = jnp.roll(source, 1, axis=2)
-    k_west = jnp.roll(k_east, 1, axis=1)
+MESH = pl.DeviceIdType.MESH
+
+
+def spot(ens, cols):
+    return {"ens": ens, "cols": cols}
+
+
+def places():
+    return (lax.axis_index("ens"), lax.axis_index("cols"), lax.axis_size("ens"), lax.axis_size("cols"))
+
+
+def greet(barrier, target):
+    pl.semaphore_signal(barrier, inc=1, device_id=target, device_id_type=MESH)
+
+
+def send(source, landing, send_sem, recv_sem, target):
+    copy = pltpu.make_async_remote_copy(
+        src_ref=source,
+        dst_ref=landing,
+        send_sem=send_sem,
+        recv_sem=recv_sem,
+        device_id=target,
+        device_id_type=MESH,
+    )
+    copy.start()
+    return copy
+
+
+def to_observers_kernel(picked_ref, out_ref, landing, send_sem, recv_sem):
+    e, c, ens, cols = places()
+    group = cols // ens
+    z = c // group
+    barrier = pltpu.get_barrier_semaphore()
+
+    def hello(n, carry):
+        e2 = n // group
+        p = group * e + n % group
+
+        @pl.when((e2 != e) | (p != c))
+        def _():
+            greet(barrier, spot(e2, p))
+
+        return carry
+
+    lax.fori_loop(0, cols, hello, 0)
+
+    @pl.when(z == e)
+    def _():
+        pl.semaphore_wait(barrier, cols - 1)
+        landing[e, c % group] = picked_ref[c]
+
+    @pl.when(z != e)
+    def _():
+        pl.semaphore_wait(barrier, cols)
+        send(picked_ref.at[c], landing.at[e, c % group], send_sem, recv_sem, spot(z, c))
+
+    def step(d, carry):
+        q = (c + d) % cols
+        send(picked_ref.at[q], landing.at[e, c % group], send_sem, recv_sem, spot(z, q))
+        return carry
+
+    lax.fori_loop(1, cols, step, 0)
+    wait_lists(z == e, picked_ref, send_sem, recv_sem, cols)
+    total = landing[0]
+    for n in range(1, ens):
+        total = total + landing[n]
+    out_ref[...] = total
+
+
+def wait_lists(short, whole_ref, send_sem, recv_sem, count):
+    few = whole_ref.at[pl.ds(0, count - 1)]
+
+    @pl.when(short)
+    def _():
+        pltpu.make_async_copy(few, few, send_sem).wait()
+        pltpu.make_async_copy(few, few, recv_sem).wait()
+
+    @pl.when(jnp.logical_not(short))
+    def _():
+        pltpu.make_async_copy(whole_ref, whole_ref, send_sem).wait()
+        pltpu.make_async_copy(whole_ref, whole_ref, recv_sem).wait()
+
+
+def to_observers(picked, ens):
+    lists, rows, lanes = picked.shape
+    return pl.pallas_call(
+        to_observers_kernel,
+        in_specs=[VMEM],
+        out_specs=VMEM,
+        out_shape=jax.ShapeDtypeStruct((lists // ens, rows, lanes), jnp.float32),
+        scratch_shapes=[
+            pltpu.VMEM((ens, lists // ens, rows, lanes), jnp.float32),
+            pltpu.SemaphoreType.DMA,
+            pltpu.SemaphoreType.DMA,
+        ],
+        compiler_params=params(collective_id=1, has_side_effects=True),
+        name="to_observers",
+    )(picked)
+
+
+def to_columns_kernel(returned_ref, out_ref, send_sem, recv_sem):
+    e, c, ens, cols = places()
+    group = cols // ens
+    z = c // group
+    barrier = pltpu.get_barrier_semaphore()
+
+    def hello(d, carry):
+        greet(barrier, spot(z, (c + d) % cols))
+        return carry
+
+    lax.fori_loop(1, cols, hello, 0)
+
+    @pl.when(z == e)
+    def _():
+        pl.semaphore_wait(barrier, cols - 1)
+        out_ref[c] = returned_ref[c % group]
+
+    @pl.when(z != e)
+    def _():
+        greet(barrier, spot(z, c))
+        pl.semaphore_wait(barrier, cols)
+
+    def step(n, carry):
+        e2 = n // group
+        i = (c + n) % group
+
+        @pl.when((e2 != e) | (group * e + i != c))
+        def _():
+            send(returned_ref.at[i], out_ref.at[c], send_sem, recv_sem, spot(e2, group * e + i))
+
+        return carry
+
+    lax.fori_loop(0, cols, step, 0)
+    wait_lists(z == e, out_ref, send_sem, recv_sem, cols)
+
+
+def to_columns(returned, ens):
+    lists, rows, lanes = returned.shape
+    return pl.pallas_call(
+        to_columns_kernel,
+        in_specs=[VMEM],
+        out_specs=VMEM,
+        out_shape=jax.ShapeDtypeStruct((lists * ens, rows, lanes), jnp.float32),
+        scratch_shapes=[pltpu.SemaphoreType.DMA, pltpu.SemaphoreType.DMA],
+        compiler_params=params(collective_id=2, has_side_effects=True),
+        name="to_columns",
+    )(returned)
+
+
+def odd_rows():
+    return (lax.broadcasted_iota(jnp.int32, (64, LANES), 0) & 1) == 1
+
+
+def swapped(tile):
+    return jnp.where(odd_rows(), pltpu.roll(tile, 1, 0), pltpu.roll(tile, 63, 0))
+
+
+def east_of(tile):
+    near = pltpu.roll(tile, LANES - 1, 1)
+    lane = lax.broadcasted_iota(jnp.int32, (64, LANES), 1)
+    return jnp.where(lane == LANES - 1, pltpu.roll(near, 62, 0), near)
+
+
+def west_of(tile):
+    near = pltpu.roll(tile, 1, 1)
+    lane = lax.broadcasted_iota(jnp.int32, (64, LANES), 1)
+    return jnp.where(lane == 0, pltpu.roll(near, 2, 0), near)
+
+
+COEFS = 10
+
+
+def make_coefs(coef_ref, north, east, north_up, east_up, north_down, east_down, has_up, has_down):
+    odd = odd_rows()
+    keep_up = has_up.astype(jnp.float32)
+    keep_down = has_down.astype(jnp.float32)
+    north_down = north_down * keep_down
+    pair = jnp.where(odd, north, swapped(north))
+    outer = jnp.where(odd, swapped(north_down), north)
+    east_rim = jnp.where(odd, east_up, east_down)
+    west = west_of(east)
+    west_rim = west_of(east_rim)
+    inner = swapped(outer)
+    far = jnp.where(odd, north_up, swapped(north_down))
+    coef_ref[0] = 1.0 - pair - outer - east - west
+    coef_ref[1] = pair
+    coef_ref[2] = outer * jnp.where(odd, keep_down, keep_up)
+    coef_ref[3] = east
+    coef_ref[4] = west
+    coef_ref[5] = 1.0 - inner - far - east_rim - west_rim
+    coef_ref[6] = inner
+    coef_ref[7] = far
+    coef_ref[8] = east_rim
+    coef_ref[9] = west_rim
+
+
+def two_steps(coef_ref, own, up, down):
+    odd = odd_rows()
+    rim = jnp.where(odd, up, down)
+    far = jnp.where(odd, down, up)
+    own_swap = swapped(own)
+    first = (
+        coef_ref[0] * own
+        + coef_ref[1] * own_swap
+        + coef_ref[2] * swapped(rim)
+        + coef_ref[3] * east_of(own)
+        + coef_ref[4] * west_of(own)
+    )
+    rim = (
+        coef_ref[5] * rim
+        + coef_ref[6] * own_swap
+        + coef_ref[7] * swapped(far)
+        + coef_ref[8] * east_of(rim)
+        + coef_ref[9] * west_of(rim)
+    )
     return (
-        source
-        + k_north * (upper_rows - source)
-        + k_south * (lower_rows - source)
-        + k_east * (eastern - source)
-        + k_west * (western - source)
-    )
+        coef_ref[0] * first
+        + coef_ref[1] * swapped(first)
+        + coef_ref[2] * swapped(rim)
+        + coef_ref[3] * east_of(first)
+        + coef_ref[4] * west_of(first)
+    )
+
+
+def neighbours():
+    e, c, ens, cols = places()
+    return spot(e, (c + cols - 1) % cols), spot(e, (c + 1) % cols)
+
+
+def exchange_tiles(source, landing, send_sems, recv_sems):
+    upper, lower = neighbours()
+    return [
+        send(source, landing.at[0], send_sems.at[0], recv_sems.at[0], lower),
+        send(source, landing.at[1], send_sems.at[1], recv_sems.at[1], upper),
+    ]
+
+
+def increment_kernel(
+    root_ref,
+    static_ref,
+    part_ref,
+    north_ref,
+    east_ref,
+    out_ref,
+    coef_ref,
+    faces,
+    fields,
+    halos,
+    terms,
+    face_send,
+    face_recv,
+    halo_send,
+    halo_recv,
+    term_send,
+    term_recv,
+):
+    e, c, ens, cols = places()
+    levels = static_ref.shape[0]
+    own = levels // ens
+    upper, lower = neighbours()
+    barrier = pltpu.get_barrier_semaphore()
+    for target in (upper, lower):
+        greet(barrier, target)
+    for d in range(1, ens):
+        greet(barrier, spot((e + d) % ens, c))
+    pl.semaphore_wait(barrier, ens + 1)
+
+    copies = []
+    for side, target in enumerate((lower, upper)):
+        for n, source in enumerate((north_ref, east_ref)):
+            copies.append(
+                send(source, faces.at[side, n], face_send.at[side, n], face_recv.at[side, n], target)
+            )
+    sums = []
+    for d in (2, 1, 3):
+        peer = (e + d) % ens
+        sums.append(
+            send(
+                part_ref.at[pl.ds(peer * own, own)],
+                terms.at[d - 1],
+                term_send.at[d - 1],
+                term_recv.at[d - 1],
+                spot(peer, c),
+            )
+        )
+
+    def product(i, carry):
+        l = i // 4
+        rows = pl.ds(pl.multiple_of((i % 4) * 16, 16), 16)
+        total = root_ref[e * own + l, 0] * static_ref[0, rows, :]
+        for m in range(1, levels):
+            total = total + root_ref[e * own + l, m] * static_ref[m, rows, :]
+        fields[0, l, rows, :] = total
+        return carry
+
+    lax.fori_loop(0, own * 4, product, 0)
+    halo = exchange_tiles(fields.at[0], halos.at[0], halo_send.at[0], halo_recv.at[0])
+    for copy in copies:
+        copy.wait()
+    make_coefs(
+        coef_ref,
+        north_ref[...],
+        east_ref[...],
+        faces[0, 0],
+        faces[0, 1],
+        faces[1, 0],
+        faces[1, 1],
+        c > 0,
+        c < cols - 1,
+    )
+    for copy in halo:
+        copy.wait()
+    for l in range(own):
+        fields[1, l] = two_steps(coef_ref, fields[0, l], halos[0, 0, l], halos[0, 1, l])
+    halo = exchange_tiles(fields.at[1], halos.at[1], halo_send.at[1], halo_recv.at[1])
+    for copy in sums + halo:
+        copy.wait()
+    for l in range(own):
+        total = two_steps(coef_ref, fields[1, l], halos[1, 0, l], halos[1, 1, l])
+        total = total + part_ref[e * own + l]
+        for d in range(ens - 1):
+            total = total + terms[d, l]
+        out_ref[l] = total
+
+
+def increment_of(root, static, part, north, east, ens):
+    levels, rows, lanes = static.shape
+    own = levels // ens
+    return pl.pallas_call(
+        increment_kernel,
+        in_specs=[SMEM, VMEM, VMEM, VMEM, VMEM],
+        out_specs=[VMEM, VMEM],
+        out_shape=[
+            jax.ShapeDtypeStruct((own, rows, lanes), jnp.float32),
+            jax.ShapeDtypeStruct((COEFS, rows, lanes), jnp.float32),
+        ],
+        scratch_shapes=[
+            pltpu.VMEM((2, 2, rows, lanes), jnp.float32),
+            pltpu.VMEM((2, own, rows, lanes), jnp.float32),
+            pltpu.VMEM((2, 2, own, rows, lanes), jnp.float32),
+            pltpu.VMEM((ens - 1, own, rows, lanes), jnp.float32),
+            pltpu.SemaphoreType.DMA((2, 2)),
+            pltpu.SemaphoreType.DMA((2, 2)),
+            pltpu.SemaphoreType.DMA((2, 2)),
+            pltpu.SemaphoreType.DMA((2, 2)),
+            pltpu.SemaphoreType.DMA((ens - 1,)),
+            pltpu.SemaphoreType.DMA((ens - 1,)),
+        ],
+        compiler_params=params(collective_id=3, has_side_effects=True),
+        name="increment",
+    )(root, static, part, north, east)
+
+
+def share(own_ref, whole_ref, send_sems, recv_sems):
+    e, c, ens, cols = places()
+    own = own_ref.shape[0]
+    return [
+        send(
+            own_ref,
+            whole_ref.at[pl.ds(e * own, own)],
+            send_sems.at[d - 1],
+            recv_sems.at[d - 1],
+            spot((e + d) % ens, c),
+        )
+        for d in (2, 1, 3)
+    ]
+
+
+def smooth_kernel(
+    adjoint_ref,
+    coef_ref,
+    whole_ref,
+    smooth_ref,
+    fields,
+    halos,
+    halo_send,
+    halo_recv,
+    whole_send,
+    whole_recv,
+    smooth_send,
+    smooth_recv,
+):
+    e, c, ens, cols = places()
+    own = adjoint_ref.shape[0]
+    upper, lower = neighbours()
+    barrier = pltpu.get_barrier_semaphore()
+    for target in (upper, lower):
+        greet(barrier, target)
+    for d in range(1, ens):
+        greet(barrier, spot((e + d) % ens, c))
+    pl.semaphore_wait(barrier, ens + 1)
+    halo = exchange_tiles(adjoint_ref, halos.at[0], halo_send.at[0], halo_recv.at[0])
+    wholes = share(adjoint_ref, whole_ref, whole_send, whole_recv)
+    for l in range(own):
+        whole_ref[e * own + l] = adjoint_ref[l]
+    for copy in halo:
+        copy.wait()
+    for l in range(own):
+        fields[0, l] = two_steps(coef_ref, adjoint_ref[l], halos[0, 0, l], halos[0, 1, l])
+    halo = exchange_tiles(fields.at[0], halos.at[1], halo_send.at[1], halo_recv.at[1])
+    for copy in halo:
+        copy.wait()
+    for l in range(own):
+        fields[1, l] = two_steps(coef_ref, fields[0, l], halos[1, 0, l], halos[1, 1, l])
+    smooths = share(fields.at[1], smooth_ref, smooth_send, smooth_recv)
+    for l in range(own):
+        smooth_ref[e * own + l] = fields[1, l]
+    for copy in wholes + smooths:
+        copy.wait()
+
+
+def smooth_of(adjoint, coefs, ens):
+    own, rows, lanes = adjoint.shape
+    whole = jax.ShapeDtypeStruct((own * ens, rows, lanes), jnp.float32)
+    return pl.pallas_call(
+        smooth_kernel,
+        in_specs=[VMEM, VMEM],
+        out_specs=[VMEM, VMEM],
+        out_shape=[whole, whole],
+        scratch_shapes=[
+            pltpu.VMEM((2, own, rows, lanes), jnp.float32),
+            pltpu.VMEM((2, 2, own, rows, lanes), jnp.float32),
+            pltpu.SemaphoreType.DMA((2, 2)),
+            pltpu.SemaphoreType.DMA((2, 2)),
+            pltpu.SemaphoreType.DMA((ens - 1,)),
+            pltpu.SemaphoreType.DMA((ens - 1,)),
+            pltpu.SemaphoreType.DMA((ens - 1,)),
+            pltpu.SemaphoreType.DMA((ens - 1,)),
+        ],
+        compiler_params=params(collective_id=4, has_side_effects=True),
+        name="smooth",
+    )(adjoint, coefs)
 
 
 def local(
@@ -304,56 +740,35 @@
     send_index,
     send_count,
 ):
-    south_rim = shifted(face_north[:1], "cols", -1)
-    k_south = jnp.concatenate([face_north[1:], south_rim], axis=0)
-
-    def diffuse(source):
-        for repeat in range(NDIFF):
-            padded = jnp.concatenate(
-                [shifted(source[:, -1:], "cols", 1), source, shifted(source[:, :1], "cols", -1)], axis=1
-            )
-            source = smooth(source, padded, face_north, k_south, face_east)
-        return source
-
     levels, grid_rows, length = static_control.shape
     ens = lax.axis_size("ens")
     me = lax.axis_index("ens")
     own_levels = levels // ens
     member_scale = 1.0 / math.sqrt(ensemble_control.shape[0] * ens - 1)
-    first_level = me * own_levels
-    first_cell = (first_level * grid_rows * length).astype(jnp.int32).reshape(1)
+    first_cell = (me * own_levels * grid_rows * length).astype(jnp.int32).reshape(1)
     lists, capacity = send_index.shape
     list_rows = capacity // LANES
     own_lists = lists // ens
-
+    first_slot = (me * own_lists * capacity).astype(jnp.int32).reshape(1)
+
+    static = to_tiles(static_control)
     control = to_tiles(ensemble_control)
     pert = to_tiles(perturbations)
 
     part = ens_part(control, pert, vertical_local, member_scale)
-    own_root = lax.dynamic_slice_in_dim(vertical_root, first_level, own_levels, 0)
-    static_increment = diffuse(jnp.einsum("lm,mrc->lrc", own_root, static_control, precision=precise))
-    increment = lax.psum_scatter(part, "ens", scatter_dimension=0, tiled=True) + to_tiles(static_increment)
+    increment, coefs = increment_of(
+        vertical_root, static, part, to_tiles(face_north), to_tiles(face_east), ens
+    )
     picked = pick(increment.reshape(-1, LANES), send_index, send_count, first_cell)
-    picked = lax.psum(picked, "ens").reshape(lists, list_rows, LANES)
-    table = lax.all_to_all(picked, "cols", split_axis=0, concat_axis=0, tiled=True)
-    table = lax.dynamic_slice_in_dim(table, me * own_lists, own_lists, 0).reshape(-1, LANES)
-    first_slot = (me * own_lists * capacity).astype(jnp.int32).reshape(1)
+    table = to_observers(picked.reshape(lists, list_rows, LANES), ens).reshape(-1, LANES)
     returned = observe(table, obs_slot, innovation, obs_weight, first_slot)
-    sent = lax.dynamic_update_slice_in_dim(
-        jnp.zeros((lists, list_rows, LANES), jnp.float32),
-        returned.reshape(own_lists, list_rows, LANES),
-        me * own_lists,
-        0,
-    )
-    arrived = lax.psum(lax.all_to_all(sent, "cols", split_axis=0, concat_axis=0, tiled=True), "ens")
+    arrived = to_columns(returned.reshape(own_lists, list_rows, LANES), ens)
     adjoint = spread(arrived.reshape(-1, LANES), send_index, send_count, first_cell, own_levels * 64)
-    adjoint = adjoint.reshape(own_levels, 64, LANES)
-    whole = lax.all_gather(adjoint, "ens", axis=0, tiled=True)
-    smoothed = diffuse(from_tiles(adjoint, grid_rows))
-    smoothed = lax.all_gather(smoothed, "ens", axis=0, tiled=True)
-    static_grad = static_control + jnp.einsum("ml,mrc->lrc", vertical_root, smoothed, precision=precise)
-    ensemble_grad = ens_grad(whole, control, pert, vertical_local, member_scale)
-    return (static_grad, from_tiles(ensemble_grad, grid_rows))
+    whole, smoothed = smooth_of(adjoint.reshape(own_levels, 64, LANES), coefs, ens)
+    ensemble_grad, static_grad = gradients(
+        whole, smoothed, control, pert, static, vertical_local, vertical_root, member_scale
+    )
+    return (from_tiles(static_grad, grid_rows), from_tiles(ensemble_grad, grid_rows))
 
 
 def solution(mesh):

time: 336 us -> 163 us (0.49)
  waiting for transfers between devices: 101 us -> 0 us
  starting transfers between devices: 73.2 us -> 0 us
  Pallas kernels: 96.5 us -> 157 us
  blocking collectives: 37.3 us -> 0 us
  between operations: 14.3 us -> 0.85 us
  local copies, waits for them, and re-layouts: 7.47 us -> 2.33 us
    psum x2 -> x0, waiting for transfers between devices: 83.4 us -> none  [the longest x1 44.3 us: local(): picked = lax.psum(picked, 'ens').reshape(lists, list_rows, LANES)]
    ppermute x17 -> x0, starting transfers between devices: 65.6 us -> none  [shifted(): return lax.ppermute(shard, axis, pairs)]
    pallas_call x1 -> x5, Pallas kernels: 9.97 us -> 71.4 us  [the longest x1 19 us: smooth_of(): pl.pallas_call(smooth_kernel, in_specs=[VMEM, VMEM], out_specs=[VMEM, VME...]
    all_gather x2 -> x0, blocking collectives: 25.8 us -> none  [the longest x1 13.1 us: local(): smoothed = lax.all_gather(smoothed, 'ens', axis=0, tiled=True)]
    all_to_all x1 -> x0, blocking collectives: 11.5 us -> none  [local(): lax.all_to_all(sent, 'cols', split_axis=0, concat_axis=0, tiled=True)]
    ppermute x17 -> x0, waiting for transfers between devices: 10.9 us -> none  [shifted(): return lax.ppermute(shard, axis, pairs)]
    all_to_all x1 -> x0, starting transfers between devices: 7.5 us -> none  [local(): lax.all_to_all(picked, 'cols', split_axis=0, concat_axis=0, tiled=True)]
    all_to_all x1 -> x0, waiting for transfers between devices: 6.55 us -> none  [local(): lax.all_to_all(picked, 'cols', split_axis=0, concat_axis=0, tiled=True)]
  transfers between devices with their start and end apart: 21 -> 0, of which waited for: 9 -> 0; matrix products, arithmetic and copies ran while one was open for 1% -> 0% of each run, Pallas kernels for 6% -> 0%
where the time goes in v2:
time: 163 us; the launch traced here: 160 us
  Pallas kernels  157 us (96%)
  local copies, waits for them, and re-layouts  2.33 us (1%)
    pallas_call x1, Pallas kernels, observe(): pl.pallas_call(obs_kernel, in_specs=[SMEM, VMEM, VMEM, VMEM, VMEM], out_s...  32.2 us
    pallas_call x1, Pallas kernels, pick(): pl.pallas_call(pick_kernel, in_specs=[SMEM, SMEM, VMEM, VMEM], out_specs=...  32 us
    pallas_call x1, Pallas kernels, smooth_of(): pl.pallas_call(smooth_kernel, in_specs=[VMEM, VMEM], out_specs=[VMEM, VME...  19 us
    pallas_call x1, Pallas kernels, increment_of(): pl.pallas_call(increment_kernel, in_specs=[SMEM, VMEM, VMEM, VMEM, VMEM],...  14.9 us
    pallas_call x1, Pallas kernels, to_observers(): pl.pallas_call(to_observers_kernel, in_specs=[VMEM], out_specs=VMEM, out_...  14.9 us
    pallas_call x1, Pallas kernels, spread(): pl.pallas_call(spread_kernel, in_specs=[SMEM, SMEM, VMEM, VMEM], out_spec...  12.4 us
    pallas_call x1, Pallas kernels, to_columns(): pl.pallas_call(to_columns_kernel, in_specs=[VMEM], out_specs=VMEM, out_sh...  12 us
    pallas_call x1, Pallas kernels, gradients(): pl.pallas_call(functools.partial(grad_kernel, scale), grid=(members,), in...  10.7 us

profile of v2, /device:TPU:32, one launch (start us, length us, event | category | flops | bytes accessed | tf_op | source)
XLA Modules:
  0.0 159.8 jit_solution(4792479309181358941)
XLA Ops:
  0.6 0.0 copy-start.12
  0.6 0.0 copy-start.11
  0.7 0.0 copy-start
  0.7 1.6 copy-done
  2.3 0.7 copy-done.9
  3.0 0.0 copy-start.4
  3.0 0.0 copy-start.5
  3.0 0.0 copy-start.6
  3.0 0.0 copy-start.1
  3.0 0.0 copy-start.10
  3.0 8.6 %ens_part.1.part_ref = f32[16,64,128]{2,1,0:T(8,128)S(1)} custom-call(f32[16,16]{1,0:T(8,128)S(1)} %copy-done.9, f32[8,16,64,128]{3,2,1,0:T(8,128)} %bitcast.61, bf16[8,16,64,128]{3,2,1,0:T(8,128)(2,1)S(1)} %bitcast.46), custom_call_target="tpu_custom_call" | custom-call | tf_op jit(solution)/shard_map/ens_part/pallas_call | solution.py:62
  11.6 0.0 copy-done.11
  11.6 0.0 copy-done.2
  11.6 0.0 copy-done.7
  11.6 0.0 copy-done.8
  11.7 14.9 %increment.1 = (f32[4,64,128]{2,1,0:T(8,128)S(1)}, f32[10,64,128]{2,1,0:T(8,128)S(1)}) custom-call(f32[16,16]{1,0:T(8,128)S(1)} %copy-done.11, f32[16,64,128]{2,1,0:T(8,128)S(1)} %bitcast.48, f32[16,64,128]{2,1,0:T(8,128)S(1)} %ens_part.1.part_ref, f32[64,128]{1,0:T(8,128)S(1)} %bitcast.59, f32[64,128]{1,0:T(8,128)S(1)} %bitcast.60), custom_call_target="tpu_custom_call" | custom-call | tf_op jit(solution)/shard_map/increment/pallas_call | solution.py:623
  26.6 0.0 copy-done.12
  26.6 32.0 %pick.1 = f32[256,128]{1,0:T(8,128)S(1)} custom-call(s32[1]{0:T(128)} %bitcast.first_ref, s32[32]{0:T(128)S(1)} %copy-done.12, f32[256,128]{1,0:T(8,128)S(1)} %bitcast.56, s32[32,1024]{1,0:T(8,128)S(1)} %copy-done.3), custom_call_target="tpu_custom_call" | custom-call | tf_op jit(solution)/shard_map/pick/pallas_call | solution.py:185
  58.6 14.9 %to_observers.1 = f32[8,8,128]{2,1,0:T(8,128)S(1)} custom-call(f32[32,8,128]{2,1,0:T(8,128)S(1)} %bitcast.52), custom_call_target="tpu_custom_call" | custom-call | tf_op jit(solution)/shard_map/to_observers/pallas_call | solution.py:380
  73.5 32.2 %observe.1 = f32[64,128]{1,0:T(8,128)S(1)} custom-call(s32[1]{0:T(128)} %bitcast.1.first_ref, f32[64,128]{1,0:T(8,128)S(1)} %bitcast.57, s32[512,128]{1,0:T(8,128)S(1)} %bitcast.53, f32[512,128]{1,0:T(8,128)S(1)} %bitcast.54, f32[512,128]{1,0:T(8,128)S(1)} %bitcast.55), custom_call_target="tpu_custom_call" | custom-call | tf_op jit(solution)/shard_map/observe/pallas_call | solution.py:252
  105.7 12.0 %to_columns.1 = f32[32,8,128]{2,1,0:T(8,128)S(1)} custom-call(f32[8,8,128]{2,1,0:T(8,128)S(1)} %bitcast.58), custom_call_target="tpu_custom_call" | custom-call | tf_op jit(solution)/shard_map/to_columns/pallas_call | solution.py:433
  117.7 12.4 %spread.1 = f32[256,128]{1,0:T(8,128)S(1)} custom-call(s32[1]{0:T(128)} %bitcast.first_ref, s32[32]{0:T(128)S(1)} %copy-done.12, f32[256,128]{1,0:T(8,128)S(1)} %bitcast.51, s32[32,1024]{1,0:T(8,128)S(1)} %copy-done.3), custom_call_target="tpu_custom_call" | custom-call | tf_op jit(solution)/shard_map/spread/pallas_call | solution.py:284
  130.2 19.0 %smooth.1 = (f32[16,64,128]{2,1,0:T(8,128)S(1)}, f32[16,64,128]{2,1,0:T(8,128)S(1)}) custom-call(f32[4,64,128]{2,1,0:T(8,128)S(1)} %bitcast.50, f32[10,64,128]{2,1,0:T(8,128)S(1)} %get-tuple-element.9.coef_ref), custom_call_target="tpu_custom_call" | custom-call | tf_op jit(solution)/shard_map/smooth/pallas_call | solution.py:709
  149.2 10.7 %gradients.1 = (f32[8,16,64,128]{3,2,1,0:T(8,128)}, f32[16,64,128]{2,1,0:T(8,128)}) custom-call(f32[16,16]{1,0:T(8,128)S(1)} %copy-done.10, f32[16,16]{1,0:T(8,128)S(1)} %copy-done.11, f32[16,64,128]{2,1,0:T(8,128)S(1)} %get-tuple-element.10.adjoint_ref, f32[16,64,128]{2,1,0:T(8,128)S(1)} %get-tuple-element.11.smooth_ref, f32[16,64,128]{2,1,0:T(8,128)S(1)} %bitcast.49, ...), custom_call_target="tpu_custom_call" | custom-call | tf_op jit(solution)/shard_map/gradients/pallas_call | solution.py:114
  (11 shorter events, 0.0 us)
Async XLA Ops:
  0.6 25.9 %copy-start.12 = (s32[32]{0:T(128)S(1)}, s32[32]{0:T(128)}, u32[]{:S(2)}) copy-start(s32[32]{0:T(128)} %counts_ref.3) | copy-start | bytes 388
  0.6 11.0 %copy-start.11 = (f32[16,16]{1,0:T(8,128)S(1)}, f32[16,16]{1,0:T(8,128)}, u32[]{:S(2)}) copy-start(f32[16,16]{1,0:T(8,128)} %root_ref.5) | copy-start | bytes 3076
  0.7 1.6 copy-start
  2.3 0.7 copy-start.9
  3.0 8.7 %copy-start.2 = (f32[16,2,4096]{2,1,0:T(2,128)S(1)}, f32[16,2,4096]{2,1,0:T(2,128)}, u32[]{:S(2)}) copy-start(f32[16,2,4096]{2,1,0:T(2,128)} %param.12) | copy-start | bytes 1572868
  3.0 8.7 %copy-start.7 = (f32[2,4096]{1,0:T(2,128)S(1)}, f32[2,4096]{1,0:T(2,128)}, u32[]{:S(2)}) copy-start(f32[2,4096]{1,0:T(2,128)} %param.17) | copy-start | bytes 98308
  3.0 8.7 %copy-start.8 = (f32[2,4096]{1,0:T(2,128)S(1)}, f32[2,4096]{1,0:T(2,128)}, u32[]{:S(2)}) copy-start(f32[2,4096]{1,0:T(2,128)} %param.18) | copy-start | bytes 98308
  3.0 23.6 %copy-start.3 = (s32[32,1024]{1,0:T(8,128)S(1)}, s32[32,1024]{1,0:T(8,128)}, u32[]{:S(2)}) copy-start(s32[32,1024]{1,0:T(8,128)} %index_ref.3) | copy-start | bytes 393220
  3.0 70.5 %copy-start.4 = (s32[65536]{0:T(1024)S(1)}, s32[65536]{0:T(1024)}, u32[]{:S(2)}) copy-start(s32[65536]{0:T(1024)} %param.21) | copy-start | bytes 786436
  3.0 70.5 %copy-start.5 = (f32[65536]{0:T(1024)S(1)}, f32[65536]{0:T(1024)}, u32[]{:S(2)}) copy-start(f32[65536]{0:T(1024)} %param.19) | copy-start | bytes 786436
  3.0 70.5 %copy-start.6 = (f32[65536]{0:T(1024)S(1)}, f32[65536]{0:T(1024)}, u32[]{:S(2)}) copy-start(f32[65536]{0:T(1024)} %param.20) | copy-start | bytes 786436
  3.0 146.1 %copy-start.1 = (bf16[8,16,2,4096]{3,2,1,0:T(2,128)(2,1)S(1)}, bf16[8,16,2,4096]{3,2,1,0:T(2,128)(2,1)}, u32[]{:S(2)}) copy-start(bf16[8,16,2,4096]{3,2,1,0:T(2,128)(2,1)} %param.14) | copy-start | bytes 6291460
  3.0 146.1 %copy-start.10 = (f32[16,16]{1,0:T(8,128)S(1)}, f32[16,16]{1,0:T(8,128)}, u32[]{:S(2)}) copy-start(f32[16,16]{1,0:T(8,128)} %local_ref.1) | copy-start | bytes 3076

commit v3 on v2

--- a/solution.py
+++ b/solution.py
@@ -125,22 +125,46 @@
     )(local_root, root, adjoint, smoothed, static, control, pert)
 
 
-def row_lookup(table_ref, row_ids, lane_ids):
-    count = len(row_ids)
-
-    def step(i, found):
-        found = list(found)
-        base = pl.multiple_of(i * 8, 8)
-        rows = table_ref[pl.ds(base, 8), :]
-        for s in range(8):
-            row = jnp.broadcast_to(rows[s : s + 1, :], (8, LANES))
-            for n in range(count):
-                value = jnp.take_along_axis(row, lane_ids[n], axis=1)
-                found[n] = jnp.where(row_ids[n] == base + s, value, found[n])
-        return tuple(found)
-
-    zero = jnp.zeros((8, LANES), jnp.float32)
-    return lax.fori_loop(0, table_ref.shape[0] // 8, step, (zero,) * count)
+def iota(shape, dim):
+    return lax.broadcasted_iota(jnp.int32, shape, dim)
+
+
+def small(ids):
+    return ids.astype(jnp.float32).astype(jnp.bfloat16)
+
+
+def one_hot(ids, count):
+    width = ids.shape[1]
+    hit = small(iota((count, width), 0)) == small(ids)
+    return jnp.where(hit, jnp.bfloat16(1), jnp.bfloat16(0))
+
+
+def table_parts(table, parts_ref):
+    lanes = table.shape[1]
+    high = table.astype(jnp.bfloat16).astype(jnp.float32)
+    parts_ref[:lanes, :] = high.T.astype(jnp.bfloat16)
+    parts_ref[lanes:, :] = (table - high).T.astype(jnp.bfloat16)
+
+
+def look_up(parts_ref, hot, lane):
+    lanes = parts_ref.shape[0] // 2
+    found = jnp.dot(parts_ref[...], hot, preferred_element_type=jnp.float32)
+    found = found[:lanes] + found[lanes:]
+    found = jnp.where(iota(found.shape, 0) == lane, found, 0.0)
+    return jnp.sum(found, axis=0, keepdims=True)
+
+
+def sum_up(hot, lane, values, lanes):
+    high = values.astype(jnp.bfloat16)
+    low = (values - high.astype(jnp.float32)).astype(jnp.bfloat16)
+    hit = small(iota((lanes, lane.shape[1]), 0)) == small(lane)
+    zero = jnp.bfloat16(0)
+    parts = jnp.concatenate([jnp.where(hit, high, zero), jnp.where(hit, low, zero)], axis=0)
+    return lax.dot_general(hot, parts, (((1,), (1,)), ((), ())), preferred_element_type=jnp.float32)
+
+
+def as_row(block):
+    return jnp.concatenate([block[i : i + 1, :] for i in range(block.shape[0])], axis=1)
 
 
 def cell_place(index, first_cell, cells):
@@ -151,33 +175,24 @@
     return jnp.where(mine, row, -1), inside & (LANES - 1)
 
 
-def live(counts_ref, first_list, slot0):
-    rows = lax.broadcasted_iota(jnp.int32, (8, LANES), 0)
-    limit = jnp.zeros((8, LANES), jnp.int32)
-    for i in range(8):
-        limit = jnp.where(rows == i, counts_ref[first_list + i], limit)
-    slots = slot0 + lax.broadcasted_iota(jnp.int32, (8, LANES), 1)
-    return slots < limit
-
-
-def pick_kernel(first_ref, counts_ref, table_ref, index_ref, out_ref):
+def pick_kernel(first_ref, counts_ref, table_ref, index_ref, out_ref, parts_ref):
     lists, capacity = index_ref.shape
-    cells = table_ref.shape[0] * LANES
+    rows = table_ref.shape[0]
     tiles = capacity // LANES
-
-    def group(g, carry):
-        places = []
-        for t in range(tiles):
-            index = index_ref[pl.ds(pl.multiple_of(g * 8, 8), 8), t * LANES : (t + 1) * LANES]
-            row, lane = cell_place(index, first_ref[0], cells)
-            row = jnp.where(live(counts_ref, g * 8, t * LANES), row, -1)
-            places.append((row, lane))
-        found = row_lookup(table_ref, [p[0] for p in places], [p[1] for p in places])
-        for t in range(tiles):
-            out_ref[pl.ds(g * 8 * tiles + t, 8, stride=tiles), :] = found[t]
-        return carry
-
-    lax.fori_loop(0, lists // 8, group, 0)
+    table_parts(table_ref[...], parts_ref)
+    slots = iota((1, capacity), 1)
+
+    def step(i, carry):
+        for j in range(8):
+            q = i * 8 + j
+            row, lane = cell_place(index_ref[pl.ds(q, 1), :], first_ref[0], rows * LANES)
+            row = jnp.where(slots < counts_ref[q], row, -1)
+            found = look_up(parts_ref, one_hot(row, rows), lane)
+            for t in range(tiles):
+                out_ref[pl.ds(q * tiles + t, 1), :] = found[:, t * LANES : (t + 1) * LANES]
+        return carry
+
+    lax.fori_loop(0, lists // 8, step, 0)
 
 
 def pick(table, index, counts, first_cell):
@@ -187,63 +202,41 @@
         in_specs=[SMEM, SMEM, VMEM, VMEM],
         out_specs=VMEM,
         out_shape=jax.ShapeDtypeStruct((lists * capacity // LANES, LANES), jnp.float32),
+        scratch_shapes=[pltpu.VMEM((2 * LANES, table.shape[0]), jnp.bfloat16)],
         compiler_params=params(),
         name="pick",
     )(first_cell, counts, table, index)
 
 
-def two_parts(values):
-    high = values.astype(jnp.bfloat16)
-    low = (values - high.astype(jnp.float32)).astype(jnp.bfloat16)
-    return high, low
-
-
-def one_hot_sum(rows, lanes, values, row_total):
-    width = values.shape[1]
-    one = jnp.bfloat16(1)
-    zero = jnp.bfloat16(0)
-    row_ids = lax.broadcasted_iota(jnp.int32, (row_total, width), 0)
-    lane_ids = lax.broadcasted_iota(jnp.int32, (LANES, width), 0)
-    row_hot = (rows == row_ids).astype(jnp.float32).astype(jnp.bfloat16)
-    lane_hot = lanes == lane_ids
-    high = values.astype(jnp.bfloat16).astype(jnp.float32)
-    low = values - high
-    parts = jnp.concatenate(
-        [jnp.where(lane_hot, high, 0.0).astype(jnp.bfloat16), jnp.where(lane_hot, low, 0.0).astype(jnp.bfloat16)],
-        axis=0,
-    )
-    both = lax.dot_general(
-        row_hot, parts, (((1,), (1,)), ((), ())), preferred_element_type=jnp.float32
-    )
-    return both
-
-
-def as_row(block):
-    return jnp.concatenate([block[i : i + 1, :] for i in range(block.shape[0])], axis=1)
-
-
-def obs_kernel(first_ref, table_ref, slot_ref, innovation_ref, weight_ref, out_ref, both_ref):
-    rows = table_ref.shape[0]
+HALF = 64
+
+
+def obs_kernel(first_ref, table_ref, slot_ref, innovation_ref, weight_ref, out_ref, parts_ref, both_ref):
+    rows = 2 * table_ref.shape[0]
+    table = table_ref[...]
+    table_parts(jnp.concatenate([table[:, :HALF], table[:, HALF:]], axis=0), parts_ref)
     both_ref[...] = jnp.zeros_like(both_ref)
-    group = 4
+    group = 32
 
     def step(i, carry):
-        base = pl.multiple_of(i * 8 * group, 8 * group)
-        row_ids, lane_ids = [], []
-        for n in range(group):
-            inside = slot_ref[pl.ds(base + 8 * n, 8), :] - first_ref[0]
-            row_ids.append(inside >> 7)
-            lane_ids.append(inside & (LANES - 1))
-        found = row_lookup(table_ref, row_ids, lane_ids)
-        for n in range(group):
-            at = pl.ds(base + 8 * n, 8)
-            mine = (row_ids[n] >= 0) & (row_ids[n] < rows)
-            weighted = jnp.where(mine, weight_ref[at, :] * (found[n] - innovation_ref[at, :]), 0.0)
-            both_ref[...] += one_hot_sum(as_row(row_ids[n]), as_row(lane_ids[n]), as_row(weighted), rows)
-        return carry
-
-    lax.fori_loop(0, slot_ref.shape[0] // (8 * group), step, 0)
-    out_ref[...] = both_ref[:, :LANES] + both_ref[:, LANES:]
+        total = jnp.zeros(both_ref.shape, jnp.float32)
+        for j in range(2):
+            at = pl.ds(pl.multiple_of((i * 2 + j) * group, group), group)
+            inside = as_row(slot_ref[at, :]) - first_ref[0]
+            whole = inside >> 7
+            mine = (inside >= 0) & (whole < rows // 2)
+            row = jnp.where(mine, whole + ((inside >> 6) & 1) * (rows // 2), -1)
+            lane = inside & (HALF - 1)
+            hot = one_hot(row, rows)
+            found = look_up(parts_ref, hot, lane)
+            weighted = as_row(weight_ref[at, :]) * (found - as_row(innovation_ref[at, :]))
+            total = total + sum_up(hot, lane, jnp.where(mine, weighted, 0.0), HALF)
+        both_ref[...] += total
+        return carry
+
+    lax.fori_loop(0, slot_ref.shape[0] // (2 * group), step, 0)
+    sums = both_ref[:, :HALF] + both_ref[:, HALF:]
+    out_ref[...] = jnp.concatenate([sums[: rows // 2], sums[rows // 2 :]], axis=1)
 
 
 def observe(table, slots, innovation, weight, first_slot):
@@ -254,7 +247,10 @@
         in_specs=[SMEM, VMEM, VMEM, VMEM, VMEM],
         out_specs=VMEM,
         out_shape=jax.ShapeDtypeStruct((rows, LANES), jnp.float32),
-        scratch_shapes=[pltpu.VMEM((rows, 2 * LANES), jnp.float32)],
+        scratch_shapes=[
+            pltpu.VMEM((2 * HALF, 2 * rows), jnp.bfloat16),
+            pltpu.VMEM((2 * rows, 2 * HALF), jnp.float32),
+        ],
         compiler_params=params(),
         name="observe",
     )(first_slot, table, *shaped)
@@ -264,19 +260,21 @@
     lists, capacity = index_ref.shape
     tiles = capacity // LANES
     rows = out_ref.shape[0]
-    cells = rows * LANES
     both_ref[...] = jnp.zeros_like(both_ref)
-
-    def step(q, carry):
-        values = as_row(arrived_ref[pl.ds(pl.multiple_of(q * tiles, tiles), tiles), :])
-        index = index_ref[pl.ds(q, 1), :]
-        row, lane = cell_place(index, first_ref[0], cells)
-        slots = lax.broadcasted_iota(jnp.int32, (1, capacity), 1)
-        values = jnp.where(slots < counts_ref[q], values, 0.0)
-        both_ref[...] += one_hot_sum(row, lane, values, rows)
-        return carry
-
-    lax.fori_loop(0, lists, step, 0)
+    slots = iota((1, capacity), 1)
+
+    def step(i, carry):
+        total = jnp.zeros(both_ref.shape, jnp.float32)
+        for j in range(8):
+            q = i * 8 + j
+            values = as_row(arrived_ref[pl.ds(pl.multiple_of(q * tiles, tiles), tiles), :])
+            row, lane = cell_place(index_ref[pl.ds(q, 1), :], first_ref[0], rows * LANES)
+            row = jnp.where(slots < counts_ref[q], row, -1)
+            total = total + sum_up(one_hot(row, rows), lane, values, LANES)
+        both_ref[...] += total
+        return carry
+
+    lax.fori_loop(0, lists // 8, step, 0)
     out_ref[...] = both_ref[:, :LANES] + both_ref[:, LANES:]
 
 

time: 163 us -> 109 us (0.67)
  the two profiles are of different devices: /device:TPU:32 before, /device:TPU:0 now
where the time goes in v3:
time: 109 us; the launch traced here: 108 us
  Pallas kernels  105 us (96%)
  local copies, waits for them, and re-layouts  2.33 us (2%)
    pallas_call x1, Pallas kernels, smooth_of(): pl.pallas_call(smooth_kernel, in_specs=[VMEM, VMEM], out_specs=[VMEM, VME...  21 us
    pallas_call x1, Pallas kernels, increment_of(): pl.pallas_call(increment_kernel, in_specs=[SMEM, VMEM, VMEM, VMEM, VMEM],...  18.8 us
    pallas_call x1, Pallas kernels, to_observers(): pl.pallas_call(to_observers_kernel, in_specs=[VMEM], out_specs=VMEM, out_...  13.5 us
    pallas_call x1, Pallas kernels, observe(): pl.pallas_call(obs_kernel, in_specs=[SMEM, VMEM, VMEM, VMEM, VMEM], out_s...  10.7 us
    pallas_call x1, Pallas kernels, gradients(): pl.pallas_call(functools.partial(grad_kernel, scale), grid=(members,), in...  10.7 us
    pallas_call x1, Pallas kernels, to_columns(): pl.pallas_call(to_columns_kernel, in_specs=[VMEM], out_specs=VMEM, out_sh...  9.7 us
    pallas_call x1, Pallas kernels, ens_part(): pl.pallas_call(functools.partial(ens_kernel, scale), grid=(members,), in_...  8.59 us
    pallas_call x1, Pallas kernels, pick(): pl.pallas_call(pick_kernel, in_specs=[SMEM, SMEM, VMEM, VMEM], out_specs=...  6.55 us

profile of v3, /device:TPU:0, one launch (start us, length us, event | category | flops | bytes accessed | tf_op | source)
XLA Modules:
  0.0 108.5 jit_solution(11212832507184321190)
XLA Ops:
  0.6 0.0 copy-start.12
  0.6 0.0 copy-start.11
  0.7 0.0 copy-start
  0.7 1.6 %copy-done = bf16[8,16,2,4096]{3,2,1,0:T(2,128)(2,1)S(1)} copy-done((bf16[8,16,2,4096]{3,2,1,0:T(2,128)(2,1)S(1)}, bf16[8,16,2,4096]{3,2,1,0:T(2,128)(2,1)}, u32[]{:S(2)}) %copy-start) | copy-done | bytes 2097176
  2.3 0.7 copy-done.9
  3.0 0.0 copy-start.4
  3.0 8.6 %ens_part.1.part_ref = f32[16,64,128]{2,1,0:T(8,128)S(1)} custom-call(f32[16,16]{1,0:T(8,128)S(1)} %copy-done.9, f32[8,16,64,128]{3,2,1,0:T(8,128)} %bitcast.61, bf16[8,16,64,128]{3,2,1,0:T(8,128)(2,1)S(1)} %bitcast.46), custom_call_target="tpu_custom_call" | custom-call | tf_op jit(solution)/shard_map/ens_part/pallas_call | solution.py:62
  11.6 0.0 copy-done.11
  11.6 0.0 copy-done.2
  11.6 0.0 copy-done.7
  11.6 0.0 copy-done.8
  11.7 18.8 %increment.1 = (f32[4,64,128]{2,1,0:T(8,128)S(1)}, f32[10,64,128]{2,1,0:T(8,128)S(1)}) custom-call(f32[16,16]{1,0:T(8,128)S(1)} %copy-done.11, f32[16,64,128]{2,1,0:T(8,128)S(1)} %bitcast.48, f32[16,64,128]{2,1,0:T(8,128)S(1)} %ens_part.1.part_ref, f32[64,128]{1,0:T(8,128)S(1)} %bitcast.59, f32[64,128]{1,0:T(8,128)S(1)} %bitcast.60), custom_call_target="tpu_custom_call" | custom-call | tf_op jit(solution)/shard_map/increment/pallas_call | solution.py:621
  30.4 0.0 copy-done.12
  30.5 0.0 copy-done.3
  30.5 6.5 %pick.1 = f32[256,128]{1,0:T(8,128)S(1)} custom-call(s32[1]{0:T(128)} %bitcast.first_ref, s32[32]{0:T(128)S(1)} %copy-done.12, f32[256,128]{1,0:T(8,128)S(1)} %bitcast.56, s32[32,1024]{1,0:T(8,128)S(1)} %copy-done.3), custom_call_target="tpu_custom_call" | custom-call | tf_op jit(solution)/shard_map/pick/pallas_call | solution.py:200
  37.0 13.5 %to_observers.1 = f32[8,8,128]{2,1,0:T(8,128)S(1)} custom-call(f32[32,8,128]{2,1,0:T(8,128)S(1)} %bitcast.52), custom_call_target="tpu_custom_call" | custom-call | tf_op jit(solution)/shard_map/to_observers/pallas_call | solution.py:378
  50.6 0.0 copy-done.4
  50.6 0.0 copy-done.5
  50.6 0.0 copy-done.6
  50.6 10.7 %observe.1 = f32[64,128]{1,0:T(8,128)S(1)} custom-call(s32[1]{0:T(128)} %bitcast.1.first_ref, f32[64,128]{1,0:T(8,128)S(1)} %bitcast.57, s32[512,128]{1,0:T(8,128)S(1)} %bitcast.53, f32[512,128]{1,0:T(8,128)S(1)} %bitcast.54, f32[512,128]{1,0:T(8,128)S(1)} %bitcast.55), custom_call_target="tpu_custom_call" | custom-call | tf_op jit(solution)/shard_map/observe/pallas_call | solution.py:245
  61.3 9.7 %to_columns.1 = f32[32,8,128]{2,1,0:T(8,128)S(1)} custom-call(f32[8,8,128]{2,1,0:T(8,128)S(1)} %bitcast.58), custom_call_target="tpu_custom_call" | custom-call | tf_op jit(solution)/shard_map/to_columns/pallas_call | solution.py:431
  71.0 5.8 %spread.1 = f32[256,128]{1,0:T(8,128)S(1)} custom-call(s32[1]{0:T(128)} %bitcast.first_ref, s32[32]{0:T(128)S(1)} %copy-done.12, f32[256,128]{1,0:T(8,128)S(1)} %bitcast.51, s32[32,1024]{1,0:T(8,128)S(1)} %copy-done.3), custom_call_target="tpu_custom_call" | custom-call | tf_op jit(solution)/shard_map/spread/pallas_call | solution.py:282
  76.8 21.0 %smooth.1 = (f32[16,64,128]{2,1,0:T(8,128)S(1)}, f32[16,64,128]{2,1,0:T(8,128)S(1)}) custom-call(f32[4,64,128]{2,1,0:T(8,128)S(1)} %bitcast.50, f32[10,64,128]{2,1,0:T(8,128)S(1)} %get-tuple-element.9.coef_ref), custom_call_target="tpu_custom_call" | custom-call | tf_op jit(solution)/shard_map/smooth/pallas_call | solution.py:707
  97.8 10.7 %gradients.1 = (f32[8,16,64,128]{3,2,1,0:T(8,128)}, f32[16,64,128]{2,1,0:T(8,128)}) custom-call(f32[16,16]{1,0:T(8,128)S(1)} %copy-done.10, f32[16,16]{1,0:T(8,128)S(1)} %copy-done.11, f32[16,64,128]{2,1,0:T(8,128)S(1)} %get-tuple-element.10.adjoint_ref, f32[16,64,128]{2,1,0:T(8,128)S(1)} %get-tuple-element.11.smooth_ref, f32[16,64,128]{2,1,0:T(8,128)S(1)} %bitcast.49, ...), custom_call_target="tpu_custom_call" | custom-call | tf_op jit(solution)/shard_map/gradients/pallas_call | solution.py:114
  (11 shorter events, 0.0 us)
Async XLA Ops:
  0.6 29.8 %copy-start.12 = (s32[32]{0:T(128)S(1)}, s32[32]{0:T(128)}, u32[]{:S(2)}) copy-start(s32[32]{0:T(128)} %counts_ref.3) | copy-start | bytes 388
  0.6 11.0 %copy-start.11 = (f32[16,16]{1,0:T(8,128)S(1)}, f32[16,16]{1,0:T(8,128)}, u32[]{:S(2)}) copy-start(f32[16,16]{1,0:T(8,128)} %root_ref.5) | copy-start | bytes 3076
  0.7 1.6 %copy-start = (bf16[8,16,2,4096]{3,2,1,0:T(2,128)(2,1)S(1)}, bf16[8,16,2,4096]{3,2,1,0:T(2,128)(2,1)}, u32[]{:S(2)}) copy-start(bf16[8,16,2,4096]{3,2,1,0:T(2,128)(2,1)} %param.14) | copy-start | bytes 6291460
  2.3 0.7 copy-start.9
  3.0 8.7 %copy-start.2 = (f32[16,2,4096]{2,1,0:T(2,128)S(1)}, f32[16,2,4096]{2,1,0:T(2,128)}, u32[]{:S(2)}) copy-start(f32[16,2,4096]{2,1,0:T(2,128)} %param.12) | copy-start | bytes 1572868
  3.0 8.7 %copy-start.7 = (f32[2,4096]{1,0:T(2,128)S(1)}, f32[2,4096]{1,0:T(2,128)}, u32[]{:S(2)}) copy-start(f32[2,4096]{1,0:T(2,128)} %param.17) | copy-start | bytes 98308
  3.0 8.7 %copy-start.8 = (f32[2,4096]{1,0:T(2,128)S(1)}, f32[2,4096]{1,0:T(2,128)}, u32[]{:S(2)}) copy-start(f32[2,4096]{1,0:T(2,128)} %param.18) | copy-start | bytes 98308
  3.0 27.5 %copy-start.3 = (s32[32,1024]{1,0:T(8,128)S(1)}, s32[32,1024]{1,0:T(8,128)}, u32[]{:S(2)}) copy-start(s32[32,1024]{1,0:T(8,128)} %index_ref.3) | copy-start | bytes 393220
  3.0 47.6 %copy-start.4 = (s32[65536]{0:T(1024)S(1)}, s32[65536]{0:T(1024)}, u32[]{:S(2)}) copy-start(s32[65536]{0:T(1024)} %param.21) | copy-start | bytes 786436
  3.0 47.6 %copy-start.5 = (f32[65536]{0:T(1024)S(1)}, f32[65536]{0:T(1024)}, u32[]{:S(2)}) copy-start(f32[65536]{0:T(1024)} %param.19) | copy-start | bytes 786436
  3.0 47.6 %copy-start.6 = (f32[65536]{0:T(1024)S(1)}, f32[65536]{0:T(1024)}, u32[]{:S(2)}) copy-start(f32[65536]{0:T(1024)} %param.20) | copy-start | bytes 786436
  3.0 94.8 %copy-start.1 = (bf16[8,16,2,4096]{3,2,1,0:T(2,128)(2,1)S(1)}, bf16[8,16,2,4096]{3,2,1,0:T(2,128)(2,1)}, u32[]{:S(2)}) copy-start(bf16[8,16,2,4096]{3,2,1,0:T(2,128)(2,1)} %param.14) | copy-start | bytes 6291460
  3.0 94.8 %copy-start.10 = (f32[16,16]{1,0:T(8,128)S(1)}, f32[16,16]{1,0:T(8,128)}, u32[]{:S(2)}) copy-start(f32[16,16]{1,0:T(8,128)} %local_ref.1) | copy-start | bytes 3076

commit v4 on v0

v4 whole, which is shorter than its diff:
```python
import functools
import math

import jax
import jax.numpy as jnp
from jax import lax
from jax.experimental import pallas as pl
from jax.experimental.pallas import tpu as pltpu
from jax.sharding import PartitionSpec as P

NDIFF = 4
LANES = 128
VMEM_LIMIT = 48 * 1024 * 1024

precise = lax.Precision.HIGHEST

SMEM = pl.BlockSpec(memory_space=pltpu.SMEM)
VMEM = pl.BlockSpec(memory_space=pltpu.VMEM)


def params(**more):
    return pltpu.CompilerParams(vmem_limit_bytes=VMEM_LIMIT, **more)


def to_tiles(cells):
    lead = cells.shape[:-2]
    rows, length = cells.shape[-2:]
    split = cells.reshape(lead + (rows, length // LANES, LANES))
    return jnp.swapaxes(split, -3, -2).reshape(lead + (rows * length // LANES, LANES))


def from_tiles(tiles, rows):
    lead = tiles.shape[:-2]
    count = tiles.shape[-2] // rows
    split = tiles.reshape(lead + (count, rows, LANES))
    return jnp.swapaxes(split, -3, -2).reshape(lead + (rows, count * LANES))


def iota(shape, dim):
    return lax.broadcasted_iota(jnp.int32, shape, dim)


def small(ids):
    return ids.astype(jnp.float32).astype(jnp.bfloat16)


def one_hot(ids, count):
    width = ids.shape[1]
    hit = small(iota((count, width), 0)) == small(ids)
    return jnp.where(hit, jnp.bfloat16(1), jnp.bfloat16(0))


def table_parts(table, parts_ref):
    lanes = table.shape[1]
    high = table.astype(jnp.bfloat16).astype(jnp.float32)
    parts_ref[:lanes, :] = high.T.astype(jnp.bfloat16)
    parts_ref[lanes:, :] = (table - high).T.astype(jnp.bfloat16)


def look_up(parts_ref, hot, lane):
    lanes = parts_ref.shape[0] // 2
    found = jnp.dot(parts_ref[...], hot, preferred_element_type=jnp.float32)
    found = found[:lanes] + found[lanes:]
    found = jnp.where(iota(found.shape, 0) == lane, found, 0.0)
    return jnp.sum(found, axis=0, keepdims=True)


def sum_up(hot, lane, values, lanes):
    high = values.astype(jnp.bfloat16)
    low = (values - high.astype(jnp.float32)).astype(jnp.bfloat16)
    hit = small(iota((lanes, lane.shape[1]), 0)) == small(lane)
    zero = jnp.bfloat16(0)
    parts = jnp.concatenate([jnp.where(hit, high, zero), jnp.where(hit, low, zero)], axis=0)
    return lax.dot_general(hot, parts, (((1,), (1,)), ((), ())), preferred_element_type=jnp.float32)


def as_row(block):
    return jnp.concatenate([block[i : i + 1, :] for i in range(block.shape[0])], axis=1)


def cell_place(index, first_cell, cells):
    inside = index - first_cell
    level = inside >> 13
    row = (level << 6) + (((inside >> 7) & 31) << 1) + ((inside >> 12) & 1)
    mine = (inside >= 0) & (inside < cells)
    return jnp.where(mine, row, -1), inside & (LANES - 1)


MESH = pl.DeviceIdType.MESH


def spot(ens, cols):
    return {"ens": ens, "cols": cols}


def places():
    return (lax.axis_index("ens"), lax.axis_index("cols"), lax.axis_size("ens"), lax.axis_size("cols"))


def greet(barrier, target):
    pl.semaphore_signal(barrier, inc=1, device_id=target, device_id_type=MESH)


def send(source, landing, send_sem, recv_sem, target):
    copy = pltpu.make_async_remote_copy(
        src_ref=source,
        dst_ref=landing,
        send_sem=send_sem,
        recv_sem=recv_sem,
        device_id=target,
        device_id_type=MESH,
    )
    copy.start()
    return copy


def odd_rows():
    return (lax.broadcasted_iota(jnp.int32, (64, LANES), 0) & 1) == 1


def swapped(tile):
    return jnp.where(odd_rows(), pltpu.roll(tile, 1, 0), pltpu.roll(tile, 63, 0))


def east_of(tile):
    near = pltpu.roll(tile, LANES - 1, 1)
    lane = lax.broadcasted_iota(jnp.int32, (64, LANES), 1)
    return jnp.where(lane == LANES - 1, pltpu.roll(near, 62, 0), near)


def west_of(tile):
    near = pltpu.roll(tile, 1, 1)
    lane = lax.broadcasted_iota(jnp.int32, (64, LANES), 1)
    return jnp.where(lane == 0, pltpu.roll(near, 2, 0), near)


COEFS = 10


def make_coefs(coef_ref, north, east, north_up, east_up, north_down, east_down, has_up, has_down):
    odd = odd_rows()
    keep_up = has_up.astype(jnp.float32)
    keep_down = has_down.astype(jnp.float32)
    north_down = north_down * keep_down
    pair = jnp.where(odd, north, swapped(north))
    outer = jnp.where(odd, swapped(north_down), north)
    east_rim = jnp.where(odd, east_up, east_down)
    west = west_of(east)
    west_rim = west_of(east_rim)
    inner = swapped(outer)
    far = jnp.where(odd, north_up, swapped(north_down))
    coef_ref[0] = 1.0 - pair - outer - east - west
    coef_ref[1] = pair
    coef_ref[2] = outer * jnp.where(odd, keep_down, keep_up)
    coef_ref[3] = east
    coef_ref[4] = west
    coef_ref[5] = 1.0 - inner - far - east_rim - west_rim
    coef_ref[6] = inner
    coef_ref[7] = far
    coef_ref[8] = east_rim
    coef_ref[9] = west_rim


def two_steps(coef_ref, own, up, down):
    odd = odd_rows()
    rim = jnp.where(odd, up, down)
    far = jnp.where(odd, down, up)
    own_swap = swapped(own)
    first = (
        coef_ref[0] * own
        + coef_ref[1] * own_swap
        + coef_ref[2] * swapped(rim)
        + coef_ref[3] * east_of(own)
        + coef_ref[4] * west_of(own)
    )
    rim = (
        coef_ref[5] * rim
        + coef_ref[6] * own_swap
        + coef_ref[7] * swapped(far)
        + coef_ref[8] * east_of(rim)
        + coef_ref[9] * west_of(rim)
    )
    return (
        coef_ref[0] * first
        + coef_ref[1] * swapped(first)
        + coef_ref[2] * swapped(rim)
        + coef_ref[3] * east_of(first)
        + coef_ref[4] * west_of(first)
    )


def neighbours():
    e, c, ens, cols = places()
    return spot(e, (c + cols - 1) % cols), spot(e, (c + 1) % cols)


def tile_copies(source, landing, send_sems, recv_sems):
    upper, lower = neighbours()
    return [
        pltpu.make_async_remote_copy(
            src_ref=source,
            dst_ref=landing.at[side],
            send_sem=send_sems.at[side],
            recv_sem=recv_sems.at[side],
            device_id=target,
            device_id_type=MESH,
        )
        for side, target in ((0, lower), (1, upper))
    ]


def start_tiles(copies):
    e, c, ens, cols = places()

    @pl.when(c < cols - 1)
    def _():
        copies[0].start()

    @pl.when(c > 0)
    def _():
        copies[1].start()


def wait_tiles(copies):
    e, c, ens, cols = places()

    @pl.when(c < cols - 1)
    def _():
        copies[0].wait_send()
        copies[1].wait_recv()

    @pl.when(c > 0)
    def _():
        copies[1].wait_send()
        copies[0].wait_recv()


def clear_rims(refs):
    e, c, ens, cols = places()
    for ref in refs:

        @pl.when(c == 0)
        def _(ref=ref):
            ref[0] = jnp.zeros(ref.shape[1:], jnp.float32)

        @pl.when(c == cols - 1)
        def _(ref=ref):
            ref[1] = jnp.zeros(ref.shape[1:], jnp.float32)


def greet_neighbours(barrier):
    e, c, ens, cols = places()
    upper, lower = neighbours()

    @pl.when(c > 0)
    def _():
        greet(barrier, upper)

    @pl.when(c < cols - 1)
    def _():
        greet(barrier, lower)

    for d in range(1, ens):
        greet(barrier, spot((e + d) % ens, c))


def wait_barrier(barrier):
    e, c, ens, cols = places()
    has_upper = (c + cols - 1) // cols
    has_lower = 1 - (c + 1) // cols
    all_leave = ((e - c // (cols // ens) + ens) % ens + ens - 1) // ens
    pl.semaphore_wait(barrier, ens - 1 + cols - 1 + has_upper + has_lower + all_leave)


def wait_sends(lists_ref, send_sem):
    e, c, ens, cols = places()
    few = lists_ref.at[pl.ds(0, cols - 1)]

    @pl.when(e == c // (cols // ens))
    def _():
        pltpu.make_async_copy(few, few, send_sem).wait()

    @pl.when(e != c // (cols // ens))
    def _():
        pltpu.make_async_copy(lists_ref, lists_ref, send_sem).wait()


def observers_kernel(
    scale,
    local_ref,
    root_ref,
    counts_ref,
    static_ref,
    north_ref,
    east_ref,
    index_ref,
    control_hbm,
    pert_hbm,
    out_ref,
    coef_ref,
    control_ref,
    pert_ref,
    part_ref,
    faces,
    fields,
    halos,
    terms,
    table_ref,
    parts_ref,
    picked,
    landing,
    load_sems,
    face_send,
    face_recv,
    halo_send,
    halo_recv,
    term_send,
    term_recv,
    list_send,
    list_recv,
):
    e, c, ens, cols = places()
    levels = static_ref.shape[0]
    members = control_ref.shape[0]
    own = levels // ens
    group = cols // ens
    z = c // group
    loads = [
        pltpu.make_async_copy(control_hbm, control_ref, load_sems.at[0]),
        pltpu.make_async_copy(pert_hbm, pert_ref, load_sems.at[1]),
    ]
    for load in loads:
        load.start()
    barrier = pltpu.get_barrier_semaphore()
    greet_neighbours(barrier)

    def hello(n, carry):
        e2 = n // group
        p = group * e + n % group

        @pl.when((e2 != e) | (p != c))
        def _():
            greet(barrier, spot(e2, p))

        return carry

    lax.fori_loop(0, cols, hello, 0)
    clear_rims([faces, halos.at[0], halos.at[1]])

    def product(i, carry):
        rows = pl.ds(pl.multiple_of(i * 32, 32), 32)
        totals = [jnp.zeros((32, LANES), jnp.float32)] * own
        for m in range(levels):
            source = static_ref[m, rows, :]
            totals = [totals[l] + root_ref[e * own + l, m] * source for l in range(own)]
        for l in range(own):
            fields[0, l, rows, :] = totals[l]
        return carry

    lax.fori_loop(0, 2, product, 0)
    wait_barrier(barrier)
    first_halo = tile_copies(fields.at[0], halos.at[0], halo_send.at[0], halo_recv.at[0])
    start_tiles(first_halo)
    norths = tile_copies(north_ref, faces.at[:, 0], face_send.at[0], face_recv.at[0])
    easts = tile_copies(east_ref, faces.at[:, 1], face_send.at[1], face_recv.at[1])
    start_tiles(norths)
    start_tiles(easts)
    for load in loads:
        load.wait()

    def part_of(peer):
        first = peer * own

        def chunk(i, carry):
            rows = pl.ds(pl.multiple_of(i * 32, 32), 32)

            def member(k, totals):
                sums = [jnp.zeros((32, LANES), jnp.float32)] * own
                for m in range(levels):
                    source = control_ref[k, m, rows, :]
                    sums = [sums[l] + local_ref[first + l, m] * source for l in range(own)]
                return tuple(
                    totals[l] + pert_ref[k, first + l, rows, :].astype(jnp.float32) * sums[l]
                    for l in range(own)
                )

            totals = lax.fori_loop(0, members, member, (jnp.zeros((32, LANES), jnp.float32),) * own)
            for l in range(own):
                part_ref[first + l, rows, :] = totals[l] * scale
            return carry

        lax.fori_loop(0, 2, chunk, 0)

    def send_part(d):
        peer = (e + d) % ens
        return send(
            part_ref.at[pl.ds(peer * own, own)],
            terms.at[d - 1],
            term_send.at[d - 1],
            term_recv.at[d - 1],
            spot(peer, c),
        )

    part_of((e + 2) % ens)
    sums = [send_part(2)]
    wait_tiles(norths)
    wait_tiles(easts)
    make_coefs(
        coef_ref,
        north_ref[...],
        east_ref[...],
        faces[0, 0],
        faces[0, 1],
        faces[1, 0],
        faces[1, 1],
        c > 0,
        c < cols - 1,
    )
    wait_tiles(first_halo)
    for l in range(own):
        fields[1, l] = two_steps(coef_ref, fields[0, l], halos[0, 0, l], halos[0, 1, l])
    second_halo = tile_copies(fields.at[1], halos.at[1], halo_send.at[1], halo_recv.at[1])
    start_tiles(second_halo)
    part_of((e + 1) % ens)
    sums.append(send_part(1))
    part_of((e + 3) % ens)
    sums.append(send_part(3))
    part_of(e)
    wait_tiles(second_halo)
    rows = table_ref.shape[0] // own
    for l in range(own):
        total = two_steps(coef_ref, fields[1, l], halos[1, 0, l], halos[1, 1, l])
        table_ref[l * rows : (l + 1) * rows, :] = total + part_ref[e * own + l]
    for copy in sums:
        copy.wait()
    for l in range(own):
        total = table_ref[l * rows : (l + 1) * rows, :]
        for d in range(ens - 1):
            total = total + terms[d, l]
        table_ref[l * rows : (l + 1) * rows, :] = total

    table_parts(table_ref[...], parts_ref)
    capacity = index_ref.shape[1]
    slots = iota((1, capacity), 1)
    cells = table_ref.shape[0] * LANES

    def pick(i, carry):
        for j in range(8):
            q = (c + i * 8 + j) % cols
            row, lane = cell_place(index_ref[pl.ds(q, 1), :], e * cells, cells)
            row = jnp.where(slots < counts_ref[q], row, -1)
            found = look_up(parts_ref, one_hot(row, table_ref.shape[0]), lane)
            for t in range(capacity // LANES):
                picked[q, pl.ds(t, 1), :] = found[:, t * LANES : (t + 1) * LANES]
        for j in range(8):
            q = (c + i * 8 + j) % cols
            place = landing.at[e, c % group]

            @pl.when((q != c) | (e != z))
            def _(q=q, place=place):
                send(picked.at[q], place, list_send, list_recv, spot(z, q))

            @pl.when((q == c) & (e == z))
            def _(q=q, place=place):
                pltpu.make_async_copy(picked.at[q], place, list_recv).start()

        return carry

    lax.fori_loop(0, cols // 8, pick, 0)
    pltpu.make_async_copy(landing, landing, list_recv).wait()
    total = landing[0]
    for n in range(1, ens):
        total = total + landing[n]
    out_ref[...] = total
    wait_sends(picked, list_send)


def observer_lists(local_root, root, counts, static, north, east, index, control, pert, ens, scale):
    levels, rows, lanes = static.shape
    own = levels // ens
    lists, capacity = index.shape
    list_rows = capacity // LANES
    dma = pltpu.SemaphoreType.DMA
    anywhere = pl.BlockSpec(memory_space=pl.ANY)
    return pl.pallas_call(
        functools.partial(observers_kernel, scale),
        in_specs=[SMEM, SMEM, SMEM, VMEM, VMEM, VMEM, VMEM, anywhere, anywhere],
        out_specs=[VMEM, VMEM],
        out_shape=[
            jax.ShapeDtypeStruct((lists // ens, list_rows, LANES), jnp.float32),
            jax.ShapeDtypeStruct((COEFS, rows, lanes), jnp.float32),
        ],
        scratch_shapes=[
            pltpu.VMEM(control.shape, jnp.float32),
            pltpu.VMEM(pert.shape, jnp.bfloat16),
            pltpu.VMEM(static.shape, jnp.float32),
            pltpu.VMEM((2, 2, rows, lanes), jnp.float32),
            pltpu.VMEM((2, own, rows, lanes), jnp.float32),
            pltpu.VMEM((2, 2, own, rows, lanes), jnp.float32),
            pltpu.VMEM((ens - 1, own, rows, lanes), jnp.float32),
            pltpu.VMEM((own * rows, lanes), jnp.float32),
            pltpu.VMEM((2 * LANES, own * rows), jnp.bfloat16),
            pltpu.VMEM((lists, list_rows, LANES), jnp.float32),
            pltpu.VMEM((ens, lists // ens, list_rows, LANES), jnp.float32),
            dma((2,)),
            dma((2, 2)),
            dma((2, 2)),
            dma((2, 2)),
            dma((2, 2)),
            dma((ens - 1,)),
            dma((ens - 1,)),
            dma,
            dma,
        ],
        compiler_params=params(collective_id=1, has_side_effects=True),
        name="observer_lists",
    )(local_root, root, counts, static, north, east, index, control, pert)


HALF = 64


def share(own_ref, whole_ref, send_sems, recv_sems):
    e, c, ens, cols = places()
    own = own_ref.shape[0]
    return [
        send(
            own_ref,
            whole_ref.at[pl.ds(e * own, own)],
            send_sems.at[d - 1],
            recv_sems.at[d - 1],
            spot((e + d) % ens, c),
        )
        for d in (2, 1, 3)
    ]


def gradient_kernel(
    scale,
    local_ref,
    root_ref,
    counts_ref,
    lists_ref,
    coef_ref,
    slot_ref,
    innovation_ref,
    weight_ref,
    index_ref,
    static_ref,
    pert_ref,
    out_ref,
    static_out_ref,
    parts_ref,
    seen_ref,
    returned,
    arrived,
    both_ref,
    adjoint,
    whole,
    smooth,
    fields,
    halos,
    list_send,
    list_recv,
    halo_send,
    halo_recv,
    whole_send,
    whole_recv,
    smooth_send,
    smooth_recv,
):
    e, c, ens, cols = places()
    group = cols // ens
    z = c // group
    levels = static_ref.shape[0]
    own = levels // ens
    members = pert_ref.shape[0]
    barrier = pltpu.get_barrier_semaphore()
    greet_neighbours(barrier)

    def hello(d, carry):
        greet(barrier, spot(z, (c + d) % cols))
        return carry

    lax.fori_loop(1, cols, hello, 0)

    @pl.when(z != e)
    def _():
        greet(barrier, spot(z, c))

    clear_rims([halos.at[0], halos.at[1]])

    tiles = lists_ref.shape[1]
    half_rows = lists_ref.shape[0] * tiles
    table = lists_ref[...].reshape(half_rows, LANES)
    table_parts(jnp.concatenate([table[:, :HALF], table[:, HALF:]], axis=0), parts_ref)
    seen_ref[...] = jnp.zeros_like(seen_ref)
    block = 32

    def observe(i, carry):
        total = jnp.zeros(seen_ref.shape, jnp.float32)
        for j in range(2):
            at = pl.ds(pl.multiple_of((i * 2 + j) * block, block), block)
            inside = as_row(slot_ref[at, :]) - e * (half_rows * LANES)
            row = inside >> 7
            mine = (inside >= 0) & (row < half_rows)
            row = jnp.where(mine, row + ((inside >> 6) & 1) * half_rows, -1)
            lane = inside & (HALF - 1)
            hot = one_hot(row, 2 * half_rows)
            found = look_up(parts_ref, hot, lane)
            weighted = as_row(weight_ref[at, :]) * (found - as_row(innovation_ref[at, :]))
            total = total + sum_up(hot, lane, jnp.where(mine, weighted, 0.0), HALF)
        seen_ref[...] += total
        return carry

    lax.fori_loop(0, slot_ref.shape[0] // (2 * block), observe, 0)
    seen = seen_ref[:, :HALF] + seen_ref[:, HALF:]
    returned[...] = jnp.concatenate([seen[:half_rows], seen[half_rows:]], axis=1).reshape(returned.shape)
    wait_barrier(barrier)

    def give_back(n, carry):
        e2 = (e + n // group) % ens
        i = (c + n) % group
        p = group * e + i

        @pl.when((e2 != e) | (p != c))
        def _():
            send(returned.at[i], arrived.at[c], list_send, list_recv.at[z], spot(e2, p))

        @pl.when((e2 == e) & (p == c))
        def _():
            pltpu.make_async_copy(returned.at[i], arrived.at[c], list_recv.at[z]).start()

        return carry

    lax.fori_loop(0, cols, give_back, 0)

    capacity = index_ref.shape[1]
    slots = iota((1, capacity), 1)
    cell_rows = both_ref.shape[0]
    both_ref[...] = jnp.zeros_like(both_ref)

    def spread(i, carry):
        some = arrived.at[pl.ds(i * group, group)]
        pltpu.make_async_copy(some, some, list_recv.at[i]).wait()
        total = jnp.zeros(both_ref.shape, jnp.float32)
        for j in range(group):
            q = i * group + j
            values = as_row(arrived[q])
            row, lane = cell_place(index_ref[pl.ds(q, 1), :], e * (cell_rows * LANES), cell_rows * LANES)
            row = jnp.where(slots < counts_ref[q], row, -1)
            total = total + sum_up(one_hot(row, cell_rows), lane, values, LANES)
        both_ref[...] += total
        return carry

    lax.fori_loop(0, ens, spread, 0)
    adjoint[...] = (both_ref[:, :LANES] + both_ref[:, LANES:]).reshape(adjoint.shape)

    first_halo = tile_copies(adjoint, halos.at[0], halo_send.at[0], halo_recv.at[0])
    start_tiles(first_halo)
    wholes = share(adjoint, whole, whole_send, whole_recv)
    for l in range(own):
        whole[e * own + l] = adjoint[l]
    wait_sends(arrived, list_send)
    wait_tiles(first_halo)
    for l in range(own):
        fields[0, l] = two_steps(coef_ref, adjoint[l], halos[0, 0, l], halos[0, 1, l])
    second_halo = tile_copies(fields.at[0], halos.at[1], halo_send.at[1], halo_recv.at[1])
    start_tiles(second_halo)
    for copy in wholes:
        copy.wait()

    def products(k, carry):
        def chunk(i, inner):
            rows = pl.ds(pl.multiple_of((i // 2) * 32, 32), 32)
            first = (i % 2) * 8
            totals = [jnp.zeros((32, LANES), jnp.float32)] * 8
            for m in range(levels):
                source = pert_ref[k, m, rows, :].astype(jnp.float32) * whole[m, rows, :]
                totals = [totals[n] + local_ref[m, first + n] * source for n in range(8)]
            for n in range(8):
                out_ref[k, first + n, rows, :] = totals[n] * scale
            return inner

        lax.fori_loop(0, 4, chunk, 0)
        return carry

    lax.fori_loop(0, 2, products, 0)
    wait_tiles(second_halo)
    for l in range(own):
        fields[1, l] = two_steps(coef_ref, fields[0, l], halos[1, 0, l], halos[1, 1, l])
    smooths = share(fields.at[1], smooth, smooth_send, smooth_recv)
    for l in range(own):
        smooth[e * own + l] = fields[1, l]
    lax.fori_loop(2, members, products, 0)
    for copy in smooths:
        copy.wait()

    def static_product(i, carry):
        rows = pl.ds(pl.multiple_of((i // 2) * 32, 32), 32)
        first = (i % 2) * 8
        totals = [static_ref[first + n, rows, :] for n in range(8)]
        for m in range(levels):
            source = smooth[m, rows, :]
            totals = [totals[n] + root_ref[m, first + n] * source for n in range(8)]
        for n in range(8):
            static_out_ref[first + n, rows, :] = totals[n]
        return carry

    lax.fori_loop(0, 4, static_product, 0)


def gradient_terms(
    local_root, root, counts, lists, coefs, slots, innovation, weight, index, static, pert, ens, scale
):
    levels, rows, lanes = static.shape
    own = levels // ens
    all_lists = index.shape[0]
    tiles = lists.shape[1]
    half_rows = lists.shape[0] * tiles
    dma = pltpu.SemaphoreType.DMA
    shaped = [a.reshape(-1, LANES) for a in (slots, innovation, weight)]
    return pl.pallas_call(
        functools.partial(gradient_kernel, scale),
        in_specs=[SMEM, SMEM, SMEM] + [VMEM] * 8,
        out_specs=[VMEM, VMEM],
        out_shape=[
            jax.ShapeDtypeStruct(pert.shape, jnp.float32),
            jax.ShapeDtypeStruct(static.shape, jnp.float32),
        ],
        scratch_shapes=[
            pltpu.VMEM((2 * HALF, 2 * half_rows), jnp.bfloat16),
            pltpu.VMEM((2 * half_rows, 2 * HALF), jnp.float32),
            pltpu.VMEM(lists.shape, jnp.float32),
            pltpu.VMEM((all_lists, tiles, LANES), jnp.float32),
            pltpu.VMEM((own * rows, 2 * LANES), jnp.float32),
            pltpu.VMEM((own, rows, lanes), jnp.float32),
            pltpu.VMEM(static.shape, jnp.float32),
            pltpu.VMEM(static.shape, jnp.float32),
            pltpu.VMEM((2, own, rows, lanes), jnp.float32),
            pltpu.VMEM((2, 2, own, rows, lanes), jnp.float32),
            dma,
            dma((ens,)),
            dma((2, 2)),
            dma((2, 2)),
            dma((ens - 1,)),
            dma((ens - 1,)),
            dma((ens - 1,)),
            dma((ens - 1,)),
        ],
        compiler_params=params(collective_id=2, has_side_effects=True),
        name="gradient_terms",
    )(local_root, root, counts, lists, coefs, *shaped, index, static, pert)


def local(
    static_control,
    ensemble_control,
    perturbations,
    vertical_root,
    vertical_local,
    face_north,
    face_east,
    innovation,
    obs_weight,
    obs_slot,
    send_index,
    send_count,
):
    grid_rows = static_control.shape[1]
    ens = lax.axis_size("ens")
    member_scale = 1.0 / math.sqrt(ensemble_control.shape[0] * ens - 1)
    static = to_tiles(static_control)
    control = to_tiles(ensemble_control)
    pert = to_tiles(perturbations)
    lists, coefs = observer_lists(
        vertical_local,
        vertical_root,
        send_count,
        static,
        to_tiles(face_north),
        to_tiles(face_east),
        send_index,
        control,
        pert,
        ens,
        member_scale,
    )
    terms, static_grad = gradient_terms(
        vertical_local,
        vertical_root,
        send_count,
        lists,
        coefs,
        obs_slot,
        innovation,
        obs_weight,
        send_index,
        static,
        pert,
        ens,
        member_scale,
    )
    return (from_tiles(static_grad, grid_rows), from_tiles(control + terms, grid_rows))


def solution(mesh):
    placed = (
        P(None, "cols", None),
        P("ens", None, "cols", None),
        P("ens", None, "cols", None),
        P(),
        P(),
        P("cols", None),
        P("cols", None),
        P("cols"),
        P("cols"),
        P("cols"),
        P("cols", None),
        P("cols"),
    )
    return jax.shard_map(
        local,
        mesh=mesh,
        in_specs=placed,
        out_specs=(P(None, "cols", None), P("ens", None, "cols", None)),
        check_vma=False,
    )
```

time: 627 us -> 90.4 us (0.14)
  other arithmetic: 227 us -> 5.13 us
  matrix products: 149 us -> 0 us
  local copies, waits for them, and re-layouts: 121 us -> 7.9 us
  starting transfers between devices: 78.6 us -> 0 us
  Pallas kernels: 0 us -> 75.9 us
  waiting for transfers between devices: 34.6 us -> 0 us
  between operations: 14.6 us -> 0.72 us
    scatter-add x1 -> x0, other arithmetic: 195 us -> none  [spread(): return grid.at[(index // lanes).reshape(-1)].add(rows).reshape(-1)]
    dot_general x6 -> x0, matrix products: 149 us -> none  [the longest x1 84.3 us: local(): jnp.dot(row_onehot.T, weighted_rows, precision=precise)]
    gather x1 -> x0, local copies, waits for them, and re-layouts: 108 us -> none  [pick(): rows = jnp.take(grid, index // lanes, axis=0)]
    pallas_call x0 -> x2, Pallas kernels: none -> 75.9 us  [the longest x1 46.9 us: gradient_terms(): pl.pallas_call(functools.partial(gradient_kernel, scale), in_specs=[SMEM,...]
    ppermute x17 -> x0, starting transfers between devices: 64.5 us -> none  [the longest x8 44.9 us: with_halo(): lax.ppermute(head, axis, [((i + 1) % count, i) for i in range(ends)])]
    reduce_sum x1 -> x0, other arithmetic: 18 us -> none  [pick(): return jnp.sum(jnp.where(lane_select(index, lanes), rows, 0.0), axis=-1)]
    ppermute x17 -> x0, waiting for transfers between devices: 17.8 us -> none  [the longest x8 9.02 us: with_halo(): lax.ppermute(tail, axis, [(i, (i + 1) % count) for i in range(ends)])]
    all_to_all x2 -> x0, starting transfers between devices: 14 us -> none  [the longest x1 8.99 us: local(): lax.all_to_all(outgoing, 'cols', split_axis=0, concat_axis=0, tiled=True)]
  transfers between devices with their start and end apart: 20 -> 0, of which waited for: 13 -> 0; matrix products, arithmetic and copies ran while one was open for 6% -> 0% of each run, Pallas kernels for 0% -> 0%
where the time goes in v4:
time: 90.4 us; the launch traced here: 89.7 us
  Pallas kernels  75.9 us (84%)
  local copies, waits for them, and re-layouts  7.9 us (9%)
  other arithmetic  5.13 us (6%)
    pallas_call x1, Pallas kernels, gradient_terms(): pl.pallas_call(functools.partial(gradient_kernel, scale), in_specs=[SMEM,...  46.9 us
    pallas_call x1, Pallas kernels, observer_lists(): pl.pallas_call(functools.partial(observers_kernel, scale), in_specs=[SMEM...  29 us
    unnamed x27, local copies, waits for them, and re-layouts  7.9 us
    add x1, other arithmetic, local(): control + terms  5.13 us

profile of v4, /device:TPU:32, one launch (start us, length us, event | category | flops | bytes accessed | tf_op | source)
XLA Modules:
  0.0 89.7 jit_solution(8984654422547399959)
XLA Ops:
  0.6 0.0 copy-start
  0.6 1.6 %copy-done = bf16[8,16,2,4096]{3,2,1,0:T(2,128)(2,1)S(1)} copy-done((bf16[8,16,2,4096]{3,2,1,0:T(2,128)(2,1)S(1)}, bf16[8,16,2,4096]{3,2,1,0:T(2,128)(2,1)}, u32[]{:S(2)}) %copy-start) | copy-done | bytes 2097176
  2.2 0.0 copy-start.2
  2.2 1.0 %copy-done.2 = f32[16,2,4096]{2,1,0:T(2,128)S(1)} copy-done((f32[16,2,4096]{2,1,0:T(2,128)S(1)}, f32[16,2,4096]{2,1,0:T(2,128)}, u32[]{:S(2)}) %copy-start.2) | copy-done | bytes 524312
  3.3 0.0 copy-start.3
  3.3 0.9 %copy-done.3 = s32[32,1024]{1,0:T(8,128)S(1)} copy-done((s32[32,1024]{1,0:T(8,128)S(1)}, s32[32,1024]{1,0:T(8,128)}, u32[]{:S(2)}) %copy-start.3) | copy-done | bytes 131096
  4.2 0.0 copy-start.7
  4.2 0.8 copy-done.7
  4.9 0.0 copy-start.8
  4.9 0.8 copy-done.8
  5.7 0.7 copy-done.9
  6.4 0.0 copy-start.10
  6.4 0.7 copy-done.10
  7.1 0.7 copy-done.11
  7.8 0.0 copy-start.12
  7.8 29.0 %observer_lists.1 = (f32[8,8,128]{2,1,0:T(8,128)S(1)}, f32[10,64,128]{2,1,0:T(8,128)S(1)}) custom-call(f32[16,16]{1,0:T(8,128)S(1)} %copy-done.9, f32[16,16]{1,0:T(8,128)S(1)} %copy-done.10, s32[32]{0:T(128)S(1)} %copy-done.11, f32[16,64,128]{2,1,0:T(8,128)S(1)} %bitcast.40, f32[64,128]{1,0:T(8,128)S(1)} %bitcast.46, f32[64,128]{1,0:T(8,128)S(1)} %bitcast.47, ...), custom_call_target="tpu_custom_call" | custom-call | tf_op jit(solution)/shard_map/observer_lists/pallas_call | solution.py:485
  36.8 0.0 copy-done.1
  36.8 0.0 copy-done.4
  36.8 0.0 copy-done.5
  36.8 0.0 copy-done.6
  36.8 46.9 %gradient_terms.1 = (f32[8,16,64,128]{3,2,1,0:T(8,128)}, f32[16,64,128]{2,1,0:T(8,128)S(1)}) custom-call(f32[16,16]{1,0:T(8,128)S(1)} %copy-done.9, f32[16,16]{1,0:T(8,128)S(1)} %copy-done.10, s32[32]{0:T(128)S(1)} %copy-done.11, f32[8,8,128]{2,1,0:T(8,128)S(1)} %get-tuple-element.6.lists_ref, f32[10,64,128]{2,1,0:T(8,128)S(1)} %get-tuple-element.7.coef_ref, ...), custom_call_target="tpu_custom_call" | custom-call | tf_op jit(solution)/shard_map/gradient_terms/pallas_call | solution.py:723
  83.7 0.0 copy-done.12
  83.7 5.1 %add.3 = f32[8,16,64,128]{3,2,1,0:T(8,128)} add(f32[8,16,64,128]{3,2,1,0:T(8,128)S(1)} %bitcast.49, f32[8,16,64,128]{3,2,1,0:T(8,128)} %get-tuple-element.9) | non-fusion elementwise | flops 1048576 | bytes 12582912 | tf_op jit(solution)/shard_map/add | solution.py:804
  88.9 0.8 copy.22
  (6 shorter events, 0.0 us)
Async XLA Ops:
  0.6 1.6 %copy-start = (bf16[8,16,2,4096]{3,2,1,0:T(2,128)(2,1)S(1)}, bf16[8,16,2,4096]{3,2,1,0:T(2,128)(2,1)}, u32[]{:S(2)}) copy-start(bf16[8,16,2,4096]{3,2,1,0:T(2,128)(2,1)} %param.14) | copy-start | bytes 6291460
  2.2 1.0 %copy-start.2 = (f32[16,2,4096]{2,1,0:T(2,128)S(1)}, f32[16,2,4096]{2,1,0:T(2,128)}, u32[]{:S(2)}) copy-start(f32[16,2,4096]{2,1,0:T(2,128)} %param.12) | copy-start | bytes 1572868
  3.3 0.9 %copy-start.3 = (s32[32,1024]{1,0:T(8,128)S(1)}, s32[32,1024]{1,0:T(8,128)}, u32[]{:S(2)}) copy-start(s32[32,1024]{1,0:T(8,128)} %index_ref.3) | copy-start | bytes 393220
  4.2 0.8 copy-start.7
  4.9 0.8 copy-start.8
  5.7 0.7 copy-start.9
  6.4 0.7 copy-start.10
  7.1 0.7 copy-start.11
  7.7 29.0 %copy-start.1 = (bf16[8,16,2,4096]{3,2,1,0:T(2,128)(2,1)S(1)}, bf16[8,16,2,4096]{3,2,1,0:T(2,128)(2,1)}, u32[]{:S(2)}) copy-start(bf16[8,16,2,4096]{3,2,1,0:T(2,128)(2,1)} %param.14) | copy-start | bytes 6291460
  7.7 29.0 %copy-start.4 = (s32[65536]{0:T(1024)S(1)}, s32[65536]{0:T(1024)}, u32[]{:S(2)}) copy-start(s32[65536]{0:T(1024)} %param.21) | copy-start | bytes 786436
  7.7 29.1 %copy-start.5 = (f32[65536]{0:T(1024)S(1)}, f32[65536]{0:T(1024)}, u32[]{:S(2)}) copy-start(f32[65536]{0:T(1024)} %param.19) | copy-start | bytes 786436
  7.7 29.1 %copy-start.6 = (f32[65536]{0:T(1024)S(1)}, f32[65536]{0:T(1024)}, u32[]{:S(2)}) copy-start(f32[65536]{0:T(1024)} %param.20) | copy-start | bytes 786436
  7.8 76.0 %copy-start.12 = (f32[8,16,2,4096]{3,2,1,0:T(2,128)S(1)}, f32[8,16,2,4096]{3,2,1,0:T(2,128)}, u32[]{:S(2)}) copy-start(f32[8,16,2,4096]{3,2,1,0:T(2,128)} %param.13) | copy-start | bytes 12582916

commit v5 on v0

v5 whole, which is shorter than its diff:
```python
import functools
import math
import types

import jax
import jax.numpy as jnp
from jax import lax
from jax.experimental import pallas as pl
from jax.experimental.pallas import tpu as pltpu
from jax.sharding import PartitionSpec as P

NDIFF = 4
LANES = 128
VMEM_LIMIT = 52 * 1024 * 1024

precise = lax.Precision.HIGHEST

SMEM = pl.BlockSpec(memory_space=pltpu.SMEM)
VMEM = pl.BlockSpec(memory_space=pltpu.VMEM)


def params(**more):
    return pltpu.CompilerParams(vmem_limit_bytes=VMEM_LIMIT, **more)


def to_tiles(cells):
    lead = cells.shape[:-2]
    rows, length = cells.shape[-2:]
    split = cells.reshape(lead + (rows, length // LANES, LANES))
    return jnp.swapaxes(split, -3, -2).reshape(lead + (rows * length // LANES, LANES))


def from_tiles(tiles, rows):
    lead = tiles.shape[:-2]
    count = tiles.shape[-2] // rows
    split = tiles.reshape(lead + (count, rows, LANES))
    return jnp.swapaxes(split, -3, -2).reshape(lead + (rows, count * LANES))


def iota(shape, dim):
    return lax.broadcasted_iota(jnp.int32, shape, dim)


def small(ids):
    return ids.astype(jnp.float32).astype(jnp.bfloat16)


def one_hot(ids, count):
    width = ids.shape[1]
    hit = small(iota((count, width), 0)) == small(ids)
    return jnp.where(hit, jnp.bfloat16(1), jnp.bfloat16(0))


def table_parts(table, parts_ref):
    lanes = table.shape[1]
    high = table.astype(jnp.bfloat16).astype(jnp.float32)
    parts_ref[:lanes, :] = high.T.astype(jnp.bfloat16)
    parts_ref[lanes:, :] = (table - high).T.astype(jnp.bfloat16)


def look_up(parts_ref, hot, lane):
    lanes = parts_ref.shape[0] // 2
    found = jnp.dot(parts_ref[...], hot, preferred_element_type=jnp.float32)
    found = found[:lanes] + found[lanes:]
    found = jnp.where(iota(found.shape, 0) == lane, found, 0.0)
    return jnp.sum(found, axis=0, keepdims=True)


def sum_up(hot, lane, values, lanes):
    high = values.astype(jnp.bfloat16)
    low = (values - high.astype(jnp.float32)).astype(jnp.bfloat16)
    hit = small(iota((lanes, lane.shape[1]), 0)) == small(lane)
    zero = jnp.bfloat16(0)
    parts = jnp.concatenate([jnp.where(hit, high, zero), jnp.where(hit, low, zero)], axis=0)
    return lax.dot_general(hot, parts, (((1,), (1,)), ((), ())), preferred_element_type=jnp.float32)


def as_row(block):
    return jnp.concatenate([block[i : i + 1, :] for i in range(block.shape[0])], axis=1)


def cell_place(index, first_cell, cells):
    inside = index - first_cell
    level = inside >> 13
    row = (level << 6) + (((inside >> 7) & 31) << 1) + ((inside >> 12) & 1)
    mine = (inside >= 0) & (inside < cells)
    return jnp.where(mine, row, -1), inside & (LANES - 1)


MESH = pl.DeviceIdType.MESH


def spot(ens, cols):
    return {"ens": ens, "cols": cols}


def places():
    return (lax.axis_index("ens"), lax.axis_index("cols"), lax.axis_size("ens"), lax.axis_size("cols"))


def greet(barrier, target):
    pl.semaphore_signal(barrier, inc=1, device_id=target, device_id_type=MESH)


def send(source, landing, send_sem, recv_sem, target):
    copy = pltpu.make_async_remote_copy(
        src_ref=source,
        dst_ref=landing,
        send_sem=send_sem,
        recv_sem=recv_sem,
        device_id=target,
        device_id_type=MESH,
    )
    copy.start()
    return copy


def odd_rows():
    return (lax.broadcasted_iota(jnp.int32, (64, LANES), 0) & 1) == 1


def swapped(tile):
    return jnp.where(odd_rows(), pltpu.roll(tile, 1, 0), pltpu.roll(tile, 63, 0))


def east_of(tile):
    near = pltpu.roll(tile, LANES - 1, 1)
    lane = lax.broadcasted_iota(jnp.int32, (64, LANES), 1)
    return jnp.where(lane == LANES - 1, pltpu.roll(near, 62, 0), near)


def west_of(tile):
    near = pltpu.roll(tile, 1, 1)
    lane = lax.broadcasted_iota(jnp.int32, (64, LANES), 1)
    return jnp.where(lane == 0, pltpu.roll(near, 2, 0), near)


COEFS = 10


def make_coefs(coef_ref, north, east, north_up, east_up, north_down, east_down, has_up, has_down):
    odd = odd_rows()
    keep_up = has_up.astype(jnp.float32)
    keep_down = has_down.astype(jnp.float32)
    north_down = north_down * keep_down
    pair = jnp.where(odd, north, swapped(north))
    outer = jnp.where(odd, swapped(north_down), north)
    east_rim = jnp.where(odd, east_up, east_down)
    west = west_of(east)
    west_rim = west_of(east_rim)
    inner = swapped(outer)
    far = jnp.where(odd, north_up, swapped(north_down))
    coef_ref[0] = 1.0 - pair - outer - east - west
    coef_ref[1] = pair
    coef_ref[2] = outer * jnp.where(odd, keep_down, keep_up)
    coef_ref[3] = east
    coef_ref[4] = west
    coef_ref[5] = 1.0 - inner - far - east_rim - west_rim
    coef_ref[6] = inner
    coef_ref[7] = far
    coef_ref[8] = east_rim
    coef_ref[9] = west_rim


def two_steps(coef_ref, own, up, down):
    odd = odd_rows()
    rim = jnp.where(odd, up, down)
    far = jnp.where(odd, down, up)
    own_swap = swapped(own)
    first = (
        coef_ref[0] * own
        + coef_ref[1] * own_swap
        + coef_ref[2] * swapped(rim)
        + coef_ref[3] * east_of(own)
        + coef_ref[4] * west_of(own)
    )
    rim = (
        coef_ref[5] * rim
        + coef_ref[6] * own_swap
        + coef_ref[7] * swapped(far)
        + coef_ref[8] * east_of(rim)
        + coef_ref[9] * west_of(rim)
    )
    return (
        coef_ref[0] * first
        + coef_ref[1] * swapped(first)
        + coef_ref[2] * swapped(rim)
        + coef_ref[3] * east_of(first)
        + coef_ref[4] * west_of(first)
    )


def neighbours():
    e, c, ens, cols = places()
    return spot(e, (c + cols - 1) % cols), spot(e, (c + 1) % cols)


def tile_copies(source, landing, send_sems, recv_sems):
    upper, lower = neighbours()
    return [
        pltpu.make_async_remote_copy(
            src_ref=source,
            dst_ref=landing.at[side],
            send_sem=send_sems.at[side],
            recv_sem=recv_sems.at[side],
            device_id=target,
            device_id_type=MESH,
        )
        for side, target in ((0, lower), (1, upper))
    ]


def start_tiles(copies):
    e, c, ens, cols = places()

    @pl.when(c < cols - 1)
    def _():
        copies[0].start()

    @pl.when(c > 0)
    def _():
        copies[1].start()


def wait_tiles(copies):
    e, c, ens, cols = places()

    @pl.when(c < cols - 1)
    def _():
        copies[0].wait_send()
        copies[1].wait_recv()

    @pl.when(c > 0)
    def _():
        copies[1].wait_send()
        copies[0].wait_recv()


def clear_rims(refs):
    e, c, ens, cols = places()
    for ref in refs:

        @pl.when(c == 0)
        def _(ref=ref):
            ref[0] = jnp.zeros(ref.shape[1:], jnp.float32)

        @pl.when(c == cols - 1)
        def _(ref=ref):
            ref[1] = jnp.zeros(ref.shape[1:], jnp.float32)


def greet_neighbours(barrier):
    e, c, ens, cols = places()
    upper, lower = neighbours()

    @pl.when(c > 0)
    def _():
        greet(barrier, upper)

    @pl.when(c < cols - 1)
    def _():
        greet(barrier, lower)

    for d in range(1, ens):
        greet(barrier, spot((e + d) % ens, c))


def wait_barrier(barrier):
    e, c, ens, cols = places()
    has_upper = (c + cols - 1) // cols
    has_lower = 1 - (c + 1) // cols
    all_leave = ((e - c // (cols // ens) + ens) % ens + ens - 1) // ens
    pl.semaphore_wait(barrier, ens - 1 + has_upper + has_lower + 2 * (cols - 1 + all_leave))


def wait_sends(lists_ref, send_sem):
    e, c, ens, cols = places()
    few = lists_ref.at[pl.ds(0, cols - 1)]

    @pl.when(e == c // (cols // ens))
    def _():
        pltpu.make_async_copy(few, few, send_sem).wait()

    @pl.when(e != c // (cols // ens))
    def _():
        pltpu.make_async_copy(lists_ref, lists_ref, send_sem).wait()


HALF = 64
BLOCK = 32
ANY = pl.BlockSpec(memory_space=pl.ANY)


def greet_all(barrier):
    e, c, ens, cols = places()
    group = cols // ens
    z = c // group
    greet_neighbours(barrier)

    def senders(n, carry):
        e2 = n // group
        p = group * e + n % group

        @pl.when((e2 != e) | (p != c))
        def _():
            greet(barrier, spot(e2, p))

        return carry

    lax.fori_loop(0, cols, senders, 0)

    def returners(d, carry):
        greet(barrier, spot(z, (c + d) % cols))
        return carry

    lax.fori_loop(1, cols, returners, 0)

    @pl.when(z != e)
    def _():
        greet(barrier, spot(z, c))


def share(own_ref, whole_ref, send_sems, recv_sems):
    e, c, ens, cols = places()
    own = own_ref.shape[0]
    return [
        send(
            own_ref,
            whole_ref.at[pl.ds(e * own, own)],
            send_sems.at[d - 1],
            recv_sems.at[d - 1],
            spot((e + d) % ens, c),
        )
        for d in (2, 1, 3)
    ]


def level_part(r, peer, own, scale, loads):
    members, levels = r.control.shape[:2]
    first = peer * own

    def chunk(i, carry):
        rows = pl.ds(pl.multiple_of(i * 32, 32), 32)

        def member(k, totals):
            if loads is not None:

                @pl.when(i == 0)
                def _():
                    for load in loads(k):
                        load.wait()

            sums = [jnp.zeros((32, LANES), jnp.float32)] * own
            for m in range(levels):
                source = r.control[k, m, rows, :]
                sums = [sums[l] + r.local[first + l, m] * source for l in range(own)]
            return tuple(
                totals[l] + r.pert[k, first + l, rows, :].astype(jnp.float32) * sums[l] for l in range(own)
            )

        totals = lax.fori_loop(0, members, member, (jnp.zeros((32, LANES), jnp.float32),) * own)
        for l in range(own):
            r.part[first + l, rows, :] = totals[l] * scale
        return carry

    lax.fori_loop(0, 2, chunk, 0)


def picks(r):
    e, c, ens, cols = places()
    group = cols // ens
    z = c // group
    cell_rows = r.table.shape[0]
    cells = cell_rows * LANES
    capacity = r.index.shape[1]
    slots = iota((1, capacity), 1)
    place = r.landing.at[e, c % group]
    table_parts(r.table[...], r.cell_parts)

    def some(i, carry):
        for j in range(8):
            q = (c + 1 + i * 8 + j) % cols
            row, lane = cell_place(r.index[pl.ds(q, 1), :], e * cells, cells)
            row = jnp.where(slots < r.counts[q], row, -1)
            found = look_up(r.cell_parts, one_hot(row, cell_rows), lane)
            for t in range(capacity // LANES):
                r.picked[q, pl.ds(t, 1), :] = found[:, t * LANES : (t + 1) * LANES]
        for j in range(7):
            q = (c + 1 + i * 8 + j) % cols
            send(r.picked.at[q], place, r.list_send, r.list_recv, spot(z, q))
        q = (c + 8 + i * 8) % cols

        @pl.when((q != c) | (e != z))
        def _():
            send(r.picked.at[q], place, r.list_send, r.list_recv, spot(z, q))

        @pl.when((q == c) & (e == z))
        def _():
            pltpu.make_async_copy(r.picked.at[q], place, r.list_recv).start()

        return carry

    lax.fori_loop(0, cols // 8, some, 0)


def observe(r):
    e, c, ens, cols = places()
    total = r.landing[0]
    for n in range(1, ens):
        total = total + r.landing[n]
    half_rows = total.shape[0] * total.shape[1]
    table = total.reshape(half_rows, LANES)
    table_parts(jnp.concatenate([table[:, :HALF], table[:, HALF:]], axis=0), r.list_parts)
    r.seen[...] = jnp.zeros_like(r.seen)

    def some(i, carry):
        total = jnp.zeros(r.seen.shape, jnp.float32)
        for j in range(2):
            at = pl.ds(pl.multiple_of((i * 2 + j) * BLOCK, BLOCK), BLOCK)
            inside = as_row(r.slot[at, :]) - e * (half_rows * LANES)
            row = inside >> 7
            mine = (inside >= 0) & (row < half_rows)
            row = jnp.where(mine, row + ((inside >> 6) & 1) * half_rows, -1)
            lane = inside & (HALF - 1)
            hot = one_hot(row, 2 * half_rows)
            found = look_up(r.list_parts, hot, lane)
            weighted = as_row(r.weight[at, :]) * (found - as_row(r.innovation[at, :]))
            total = total + sum_up(hot, lane, jnp.where(mine, weighted, 0.0), HALF)
        r.seen[...] += total
        return carry

    lax.fori_loop(0, r.slot.shape[0] // (2 * BLOCK), some, 0)
    seen = r.seen[:, :HALF] + r.seen[:, HALF:]
    r.returned[...] = jnp.concatenate([seen[:half_rows], seen[half_rows:]], axis=1).reshape(r.returned.shape)


def give_back(r):
    e, c, ens, cols = places()
    group = cols // ens
    z = c // group
    last = cols - 1

    def step(n, carry):
        p = group * e + (c + 1 + n) % group
        e2 = (e + 1 + n // group) % ens
        send(r.returned.at[p % group], r.arrived.at[c], r.back_send, r.back_recv.at[z], spot(e2, p))
        return carry

    lax.fori_loop(0, last, step, 0)
    own = c % group
    p = group * e + own

    @pl.when(p != c)
    def _():
        send(r.returned.at[own], r.arrived.at[c], r.back_send, r.back_recv.at[z], spot(e, p))

    @pl.when(p == c)
    def _():
        pltpu.make_async_copy(r.returned.at[own], r.arrived.at[c], r.back_recv.at[z]).start()


def spread(r):
    e, c, ens, cols = places()
    group = cols // ens
    capacity = r.index.shape[1]
    slots = iota((1, capacity), 1)
    cell_rows = r.both.shape[0]
    cells = cell_rows * LANES
    r.both[...] = jnp.zeros_like(r.both)

    def some(i, carry):
        lists = r.arrived.at[pl.ds(i * group, group)]
        pltpu.make_async_copy(lists, lists, r.back_recv.at[i]).wait()
        total = jnp.zeros(r.both.shape, jnp.float32)
        for j in range(group):
            q = i * group + j
            row, lane = cell_place(r.index[pl.ds(q, 1), :], e * cells, cells)
            row = jnp.where(slots < r.counts[q], row, -1)
            total = total + sum_up(one_hot(row, cell_rows), lane, as_row(r.arrived[q]), LANES)
        r.both[...] += total
        return carry

    lax.fori_loop(0, ens, some, 0)
    r.adjoint[...] = (r.both[:, :LANES] + r.both[:, LANES:]).reshape(r.adjoint.shape)


def member_products(r, scale, first_member, last_member):
    levels = r.static.shape[0]

    def member(k, carry):
        def chunk(i, inner):
            rows = pl.ds(pl.multiple_of((i // 2) * 32, 32), 32)
            first = (i % 2) * 8
            totals = [jnp.zeros((32, LANES), jnp.float32)] * 8
            for m in range(levels):
                source = r.pert[k, m, rows, :].astype(jnp.float32) * r.whole[m, rows, :]
                totals = [totals[n] + r.local[m, first + n] * source for n in range(8)]
            for n in range(8):
                r.grad[k, first + n, rows, :] = r.control[k, first + n, rows, :] + totals[n] * scale
            return inner

        lax.fori_loop(0, 4, chunk, 0)
        return carry

    lax.fori_loop(first_member, last_member, member, 0)


def kernel(names, scale, *refs):
    r = types.SimpleNamespace(**dict(zip(names, refs)))
    e, c, ens, cols = places()
    levels = r.static.shape[0]
    members = r.control.shape[0]
    own = levels // ens

    def member_loads(k):
        return [
            pltpu.make_async_copy(r.control_hbm.at[k], r.control.at[k], r.control_load.at[k]),
            pltpu.make_async_copy(r.pert_hbm.at[k], r.pert.at[k], r.pert_load.at[k]),
        ]

    def load(name, n):
        return pltpu.make_async_copy(getattr(r, name + "_hbm"), getattr(r, name), r.load.at[n])

    early = [load("static", 0), load("north", 1), load("east", 2)]
    late = [load("index", 3), load("slot", 4), load("innovation", 5), load("weight", 6)]
    for one in early:
        one.start()

    def start_members(k, carry):
        for one in member_loads(k):
            one.start()
        return carry

    lax.fori_loop(0, members, start_members, 0)
    for one in late:
        one.start()
    barrier = pltpu.get_barrier_semaphore()
    greet_all(barrier)
    clear_rims([r.faces, r.halos.at[0], r.halos.at[1], r.halos.at[2], r.halos.at[3]])
    for one in early:
        one.wait()

    def product(i, carry):
        rows = pl.ds(pl.multiple_of(i * 32, 32), 32)
        totals = [jnp.zeros((32, LANES), jnp.float32)] * own
        for m in range(levels):
            source = r.static[m, rows, :]
            totals = [totals[l] + r.root[e * own + l, m] * source for l in range(own)]
        for l in range(own):
            r.fields[0, l, rows, :] = totals[l]
        return carry

    lax.fori_loop(0, 2, product, 0)
    wait_barrier(barrier)

    def halo_copies(field, n):
        return tile_copies(field, r.halos.at[n], r.halo_send.at[n], r.halo_recv.at[n])

    halo = halo_copies(r.fields.at[0], 0)
    start_tiles(halo)
    norths = tile_copies(r.north, r.faces.at[:, 0], r.face_send.at[0], r.face_recv.at[0])
    easts = tile_copies(r.east, r.faces.at[:, 1], r.face_send.at[1], r.face_recv.at[1])
    start_tiles(norths)
    start_tiles(easts)

    def send_part(d):
        peer = (e + d) % ens
        return send(
            r.part.at[pl.ds(peer * own, own)],
            r.terms.at[d - 1],
            r.term_send.at[d - 1],
            r.term_recv.at[d - 1],
            spot(peer, c),
        )

    level_part(r, (e + 2) % ens, own, scale, member_loads)
    sums = [send_part(2)]
    wait_tiles(norths)
    wait_tiles(easts)
    make_coefs(
        r.coefs,
        r.north[...],
        r.east[...],
        r.faces[0, 0],
        r.faces[0, 1],
        r.faces[1, 0],
        r.faces[1, 1],
        c > 0,
        c < cols - 1,
    )
    wait_tiles(halo)
    for l in range(own):
        r.fields[1, l] = two_steps(r.coefs, r.fields[0, l], r.halos[0, 0, l], r.halos[0, 1, l])
    halo = halo_copies(r.fields.at[1], 1)
    start_tiles(halo)
    level_part(r, (e + 1) % ens, own, scale, None)
    sums.append(send_part(1))
    level_part(r, (e + 3) % ens, own, scale, None)
    sums.append(send_part(3))
    level_part(r, e, own, scale, None)
    wait_tiles(halo)
    rows = r.table.shape[0] // own
    for l in range(own):
        total = two_steps(r.coefs, r.fields[1, l], r.halos[1, 0, l], r.halos[1, 1, l])
        r.table[l * rows : (l + 1) * rows, :] = total + r.part[e * own + l]
    for copy in sums:
        copy.wait()
    for l in range(own):
        total = r.table[l * rows : (l + 1) * rows, :]
        for d in range(ens - 1):
            total = total + r.terms[d, l]
        r.table[l * rows : (l + 1) * rows, :] = total
    for one in late:
        one.wait()
    picks(r)
    pltpu.make_async_copy(r.landing, r.landing, r.list_recv).wait()
    observe(r)
    give_back(r)
    wait_sends(r.picked, r.list_send)
    spread(r)

    halo = halo_copies(r.adjoint, 2)
    start_tiles(halo)
    wholes = share(r.adjoint, r.whole, r.whole_send, r.whole_recv)
    for l in range(own):
        r.whole[e * own + l] = r.adjoint[l]
    wait_sends(r.arrived, r.back_send)
    wait_tiles(halo)
    for l in range(own):
        r.fields[2, l] = two_steps(r.coefs, r.adjoint[l], r.halos[2, 0, l], r.halos[2, 1, l])
    halo = halo_copies(r.fields.at[2], 3)
    start_tiles(halo)
    for copy in wholes:
        copy.wait()
    member_products(r, scale, 0, 2)
    wait_tiles(halo)
    for l in range(own):
        r.fields[3, l] = two_steps(r.coefs, r.fields[2, l], r.halos[3, 0, l], r.halos[3, 1, l])
    smooths = share(r.fields.at[3], r.smooth, r.smooth_send, r.smooth_recv)
    for l in range(own):
        r.smooth[e * own + l] = r.fields[3, l]
    member_products(r, scale, 2, members)
    for copy in smooths:
        copy.wait()

    def static_product(i, carry):
        rows = pl.ds(pl.multiple_of((i // 2) * 32, 32), 32)
        first = (i % 2) * 8
        totals = [r.static[first + n, rows, :] for n in range(8)]
        for m in range(levels):
            source = r.smooth[m, rows, :]
            totals = [totals[n] + r.root[m, first + n] * source for n in range(8)]
        for n in range(8):
            r.static_grad[first + n, rows, :] = totals[n]
        return carry

    lax.fori_loop(0, 4, static_product, 0)


def store_kernel(static_ref, grad_ref, static_hbm, grad_hbm, static_sem, grad_sem):
    copies = [
        pltpu.make_async_copy(static_ref, static_hbm, static_sem),
        pltpu.make_async_copy(grad_ref, grad_hbm, grad_sem),
    ]
    for copy in copies:
        copy.start()
    for copy in copies:
        copy.wait()


def in_hbm(array):
    return pltpu.with_memory_space_constraint(array, pltpu.HBM)


def gradients(arrays, ens, scale):
    levels, rows, lanes = arrays["static"].shape
    own = levels // ens
    members = arrays["control"].shape[0]
    lists, capacity = arrays["index"].shape
    tiles = capacity // LANES
    half_rows = lists // ens * tiles
    f32, bf16 = jnp.float32, jnp.bfloat16
    dma = pltpu.SemaphoreType.DMA
    scalars = ("local", "root", "counts")
    loaded = ("static", "north", "east", "index", "slot", "innovation", "weight", "control", "pert")
    scratch = {name: pltpu.VMEM(arrays[name].shape, arrays[name].dtype) for name in loaded}
    scratch |= {
        "part": pltpu.VMEM((levels, rows, lanes), f32),
        "faces": pltpu.VMEM((2, 2, rows, lanes), f32),
        "coefs": pltpu.VMEM((COEFS, rows, lanes), f32),
        "fields": pltpu.VMEM((4, own, rows, lanes), f32),
        "halos": pltpu.VMEM((4, 2, own, rows, lanes), f32),
        "terms": pltpu.VMEM((ens - 1, own, rows, lanes), f32),
        "table": pltpu.VMEM((own * rows, lanes), f32),
        "cell_parts": pltpu.VMEM((2 * LANES, own * rows), bf16),
        "picked": pltpu.VMEM((lists, tiles, LANES), f32),
        "landing": pltpu.VMEM((ens, lists // ens, tiles, LANES), f32),
        "list_parts": pltpu.VMEM((2 * HALF, 2 * half_rows), bf16),
        "seen": pltpu.VMEM((2 * half_rows, 2 * HALF), f32),
        "returned": pltpu.VMEM((lists // ens, tiles, LANES), f32),
        "arrived": pltpu.VMEM((lists, tiles, LANES), f32),
        "both": pltpu.VMEM((own * rows, 2 * LANES), f32),
        "adjoint": pltpu.VMEM((own, rows, lanes), f32),
        "whole": pltpu.VMEM((levels, rows, lanes), f32),
        "smooth": pltpu.VMEM((levels, rows, lanes), f32),
        "load": dma((7,)),
        "control_load": dma((members,)),
        "pert_load": dma((members,)),
        "face_send": dma((2, 2)),
        "face_recv": dma((2, 2)),
        "halo_send": dma((4, 2)),
        "halo_recv": dma((4, 2)),
        "term_send": dma((ens - 1,)),
        "term_recv": dma((ens - 1,)),
        "list_send": dma,
        "list_recv": dma,
        "back_send": dma,
        "back_recv": dma((ens,)),
        "whole_send": dma((ens - 1,)),
        "whole_recv": dma((ens - 1,)),
        "smooth_send": dma((ens - 1,)),
        "smooth_recv": dma((ens - 1,)),
    }
    names = scalars + tuple(name + "_hbm" for name in loaded) + ("static_grad", "grad") + tuple(scratch)
    shapes = [arrays["static"].shape, arrays["control"].shape]
    static_grad, grad = pl.pallas_call(
        functools.partial(kernel, names, scale),
        in_specs=[SMEM] * len(scalars) + [ANY] * len(loaded),
        out_specs=[VMEM, VMEM],
        out_shape=[pltpu.VMEM(shape, f32) for shape in shapes],
        scratch_shapes=list(scratch.values()),
        compiler_params=params(collective_id=1, has_side_effects=True),
        name="gradients",
    )(*[arrays[name] for name in scalars], *[in_hbm(arrays[name]) for name in loaded])
    return pl.pallas_call(
        store_kernel,
        in_specs=[VMEM, VMEM],
        out_specs=[ANY, ANY],
        out_shape=[jax.ShapeDtypeStruct(shape, f32) for shape in shapes],
        scratch_shapes=[dma, dma],
        name="store",
    )(static_grad, grad)


def local(
    static_control,
    ensemble_control,
    perturbations,
    vertical_root,
    vertical_local,
    face_north,
    face_east,
    innovation,
    obs_weight,
    obs_slot,
    send_index,
    send_count,
):
    grid_rows = static_control.shape[1]
    ens = lax.axis_size("ens")
    arrays = {
        "local": vertical_local,
        "root": vertical_root,
        "counts": send_count,
        "static": to_tiles(static_control),
        "north": to_tiles(face_north),
        "east": to_tiles(face_east),
        "index": send_index,
        "slot": obs_slot.reshape(-1, LANES),
        "innovation": innovation.reshape(-1, LANES),
        "weight": obs_weight.reshape(-1, LANES),
        "control": to_tiles(ensemble_control),
        "pert": to_tiles(perturbations),
    }
    scale = 1.0 / math.sqrt(ensemble_control.shape[0] * ens - 1)
    static_grad, grad = gradients(arrays, ens, scale)
    return (from_tiles(static_grad, grid_rows), from_tiles(grad, grid_rows))


def solution(mesh):
    placed = (
        P(None, "cols", None),
        P("ens", None, "cols", None),
        P("ens", None, "cols", None),
        P(),
        P(),
        P("cols", None),
        P("cols", None),
        P("cols"),
        P("cols"),
        P("cols"),
        P("cols", None),
        P("cols"),
    )
    return jax.shard_map(
        local,
        mesh=mesh,
        in_specs=placed,
        out_specs=(P(None, "cols", None), P("ens", None, "cols", None)),
        check_vma=False,
    )
```

time: 627 us -> 82.1 us (0.13)
  other arithmetic: 227 us -> 0 us
  matrix products: 149 us -> 0 us
  local copies, waits for them, and re-layouts: 121 us -> 2.74 us
  starting transfers between devices: 78.6 us -> 0 us
  Pallas kernels: 0 us -> 77.8 us
  waiting for transfers between devices: 34.6 us -> 0 us
  between operations: 14.6 us -> 0.65 us
    scatter-add x1 -> x0, other arithmetic: 195 us -> none  [spread(): return grid.at[(index // lanes).reshape(-1)].add(rows).reshape(-1)]
    dot_general x6 -> x0, matrix products: 149 us -> none  [the longest x1 84.3 us: local(): jnp.dot(row_onehot.T, weighted_rows, precision=precise)]
    gather x1 -> x0, local copies, waits for them, and re-layouts: 108 us -> none  [pick(): rows = jnp.take(grid, index // lanes, axis=0)]
    pallas_call x0 -> x2, Pallas kernels: none -> 77.8 us  [the longest x1 73.2 us: gradients(): pl.pallas_call(functools.partial(kernel, names, scale), in_specs=[SMEM] *...]
    ppermute x17 -> x0, starting transfers between devices: 64.5 us -> none  [the longest x8 44.9 us: with_halo(): lax.ppermute(head, axis, [((i + 1) % count, i) for i in range(ends)])]
    reduce_sum x1 -> x0, other arithmetic: 18 us -> none  [pick(): return jnp.sum(jnp.where(lane_select(index, lanes), rows, 0.0), axis=-1)]
    ppermute x17 -> x0, waiting for transfers between devices: 17.8 us -> none  [the longest x8 9.02 us: with_halo(): lax.ppermute(tail, axis, [(i, (i + 1) % count) for i in range(ends)])]
    all_to_all x2 -> x0, starting transfers between devices: 14 us -> none  [the longest x1 8.99 us: local(): lax.all_to_all(outgoing, 'cols', split_axis=0, concat_axis=0, tiled=True)]
  transfers between devices with their start and end apart: 20 -> 0, of which waited for: 13 -> 0; matrix products, arithmetic and copies ran while one was open for 6% -> 0% of each run, Pallas kernels for 0% -> 0%
where the time goes in v5:
time: 82.1 us; the launch traced here: 81.2 us
  Pallas kernels  77.8 us (95%)
  local copies, waits for them, and re-layouts  2.74 us (3%)
    pallas_call x1, Pallas kernels, gradients(): pl.pallas_call(functools.partial(kernel, names, scale), in_specs=[SMEM] *...  73.2 us
    pallas_call x1, Pallas kernels, gradients(): pl.pallas_call(store_kernel, in_specs=[VMEM, VMEM], out_specs=[ANY, ANY],...  4.56 us
    unnamed x4, local copies, waits for them, and re-layouts  2.74 us

profile of v5, /device:TPU:32, one launch (start us, length us, event | category | flops | bytes accessed | tf_op | source)
XLA Modules:
  0.0 81.2 jit_solution(4560602381968345759)
XLA Ops:
  0.6 73.2 %gradients.1 = (f32[16,64,128]{2,1,0:T(8,128)S(1)}, f32[8,16,64,128]{3,2,1,0:T(8,128)S(1)}) custom-call(f32[16,16]{1,0:T(8,128)} %refs_0_.1, f32[16,16]{1,0:T(8,128)} %refs_1_.1, s32[32]{0:T(128)} %refs_2_.1, f32[16,64,128]{2,1,0:T(8,128)} %bitcast.40, f32[64,128]{1,0:T(8,128)} %bitcast.44, f32[64,128]{1,0:T(8,128)} %bitcast.45, s32[32,1024]{1,0:T(8,128)} %refs_6_.1, ...), custom_call_target="tpu_custom_call" | custom-call | tf_op jit(solution)/shard_map/gradients/pallas_call | solution.py:726
  73.9 0.0 copy-start
  73.9 1.9 %copy-done = f32[8,16,64,128]{3,2,1,0:T(8,128)} copy-done((f32[8,16,64,128]{3,2,1,0:T(8,128)}, f32[8,16,64,128]{3,2,1,0:T(8,128)S(1)}, u32[]{:S(2)}) %copy-start) | copy-done | bytes 4194328
  75.8 0.0 copy-start.1
  75.8 0.8 copy-done.1
  76.6 4.6 %store.1 = (f32[16,64,128]{2,1,0:T(8,128)}, f32[8,16,64,128]{3,2,1,0:T(8,128)}) custom-call(f32[16,64,128]{2,1,0:T(8,128)} %copy-done.1, f32[8,16,64,128]{3,2,1,0:T(8,128)} %copy-done), custom_call_target="tpu_custom_call" | custom-call | tf_op jit(solution)/shard_map/store/pallas_call | solution.py:735
Async XLA Ops:
  73.9 1.9 %copy-start = (f32[8,16,64,128]{3,2,1,0:T(8,128)}, f32[8,16,64,128]{3,2,1,0:T(8,128)S(1)}, u32[]{:S(2)}) copy-start(f32[8,16,64,128]{3,2,1,0:T(8,128)S(1)} %get-tuple-element.7.grad_ref) | copy-start | bytes 12582916
  75.8 0.8 copy-start.1

commit v6 on v5

--- a/solution.py
+++ b/solution.py
@@ -261,27 +261,40 @@
     def _():
         greet(barrier, lower)
 
-    for d in range(1, ens):
+    for d in (1, ens - 1):
         greet(barrier, spot((e + d) % ens, c))
+
+
+def list_home(c):
+    z, y, core = c // 8, (c // 2) % 4, c % 2
+    return (y + z + 2 * core) % 4, 2 * z + y // 2
+
+
+def column_of(home, place):
+    z = place // 2
+    y = (place % 2) * 2 + (home + z) % 2
+    return z * 8 + y * 2 + ((home + 8 - y - z) // 2) % 2
 
 
 def wait_barrier(barrier):
     e, c, ens, cols = places()
     has_upper = (c + cols - 1) // cols
     has_lower = 1 - (c + 1) // cols
-    all_leave = ((e - c // (cols // ens) + ens) % ens + ens - 1) // ens
-    pl.semaphore_wait(barrier, ens - 1 + has_upper + has_lower + 2 * (cols - 1 + all_leave))
+    home, place = list_home(c)
+    all_leave = ((e - home + ens) % ens + ens - 1) // ens
+    pl.semaphore_wait(barrier, 2 + has_upper + has_lower + cols - 1 + all_leave)
 
 
 def wait_sends(lists_ref, send_sem):
     e, c, ens, cols = places()
+    home, place = list_home(c)
     few = lists_ref.at[pl.ds(0, cols - 1)]
 
-    @pl.when(e == c // (cols // ens))
+    @pl.when(e == home)
     def _():
         pltpu.make_async_copy(few, few, send_sem).wait()
 
-    @pl.when(e != c // (cols // ens))
+    @pl.when(e != home)
     def _():
         pltpu.make_async_copy(lists_ref, lists_ref, send_sem).wait()
 
@@ -294,45 +307,51 @@
 def greet_all(barrier):
     e, c, ens, cols = places()
     group = cols // ens
-    z = c // group
+    home, place = list_home(c)
     greet_neighbours(barrier)
-
-    def senders(n, carry):
-        e2 = n // group
-        p = group * e + n % group
-
-        @pl.when((e2 != e) | (p != c))
-        def _():
-            greet(barrier, spot(e2, p))
-
-        return carry
-
-    lax.fori_loop(0, cols, senders, 0)
-
-    def returners(d, carry):
-        greet(barrier, spot(z, (c + d) % cols))
-        return carry
-
-    lax.fori_loop(1, cols, returners, 0)
-
-    @pl.when(z != e)
-    def _():
-        greet(barrier, spot(z, c))
-
-
-def share(own_ref, whole_ref, send_sems, recv_sems):
-    e, c, ens, cols = places()
-    own = own_ref.shape[0]
-    return [
-        send(
-            own_ref,
-            whole_ref.at[pl.ds(e * own, own)],
-            send_sems.at[d - 1],
-            recv_sems.at[d - 1],
-            spot((e + d) % ens, c),
-        )
-        for d in (2, 1, 3)
-    ]
+    for n in range(cols - 1):
+        greet(barrier, spot((e + 1 + n // group) % ens, column_of(e, (place + 1 + n) % group)))
+
+    @pl.when(e != home)
+    def _():
+        greet(barrier, spot(e, column_of(e, place)))
+
+
+def ring_neighbours():
+    e, c, ens, cols = places()
+    return spot((e + 1) % ens, c), spot((e + ens - 1) % ens, c)
+
+
+class Share:
+    def __init__(self, own_ref, whole_ref, send_sems, recv_sems):
+        self.own, self.whole = own_ref, whole_ref
+        self.send_sems, self.recv_sems = send_sems, recv_sems
+
+    def start(self):
+        e, c, ens, cols = places()
+        count = self.own.shape[0]
+        place = self.whole.at[pl.ds(e * count, count)]
+        self.first = [
+            send(self.own, place, self.send_sems.at[n], self.recv_sems.at[n], target)
+            for n, target in enumerate(ring_neighbours())
+        ]
+
+    def pass_on(self):
+        e, c, ens, cols = places()
+        count = self.own.shape[0]
+        half = count // 2
+        starts = (((e + ens - 1) % ens) * count, ((e + 1) % ens) * count + half)
+        self.second = []
+        for n, target in enumerate(ring_neighbours()):
+            self.first[n].wait_recv()
+            part = self.whole.at[pl.ds(starts[n], half)]
+            self.second.append(send(part, part, self.send_sems.at[2 + n], self.recv_sems.at[2 + n], target))
+
+    def finish(self):
+        for copy in self.first:
+            copy.wait_send()
+        for copy in self.second:
+            copy.wait()
 
 
 def level_part(r, peer, own, scale, loads):
@@ -368,13 +387,12 @@
 
 def picks(r):
     e, c, ens, cols = places()
-    group = cols // ens
-    z = c // group
+    home, at = list_home(c)
     cell_rows = r.table.shape[0]
     cells = cell_rows * LANES
     capacity = r.index.shape[1]
     slots = iota((1, capacity), 1)
-    place = r.landing.at[e, c % group]
+    place = r.landing.at[e, at]
     table_parts(r.table[...], r.cell_parts)
 
     def some(i, carry):
@@ -387,14 +405,14 @@
                 r.picked[q, pl.ds(t, 1), :] = found[:, t * LANES : (t + 1) * LANES]
         for j in range(7):
             q = (c + 1 + i * 8 + j) % cols
-            send(r.picked.at[q], place, r.list_send, r.list_recv, spot(z, q))
+            send(r.picked.at[q], place, r.list_send, r.list_recv, spot(home, q))
         q = (c + 8 + i * 8) % cols
 
-        @pl.when((q != c) | (e != z))
+        @pl.when((q != c) | (e != home))
         def _():
-            send(r.picked.at[q], place, r.list_send, r.list_recv, spot(z, q))
-
-        @pl.when((q == c) & (e == z))
+            send(r.picked.at[q], place, r.list_send, r.list_recv, spot(home, q))
+
+        @pl.when((q == c) & (e == home))
         def _():
             pltpu.make_async_copy(r.picked.at[q], place, r.list_recv).start()
 
@@ -417,15 +435,15 @@
         total = jnp.zeros(r.seen.shape, jnp.float32)
         for j in range(2):
             at = pl.ds(pl.multiple_of((i * 2 + j) * BLOCK, BLOCK), BLOCK)
-            inside = as_row(r.slot[at, :]) - e * (half_rows * LANES)
-            row = inside >> 7
-            mine = (inside >= 0) & (row < half_rows)
-            row = jnp.where(mine, row + ((inside >> 6) & 1) * half_rows, -1)
-            lane = inside & (HALF - 1)
-            hot = one_hot(row, 2 * half_rows)
+            slot = r.slot[at, :]
+            z, y, core = slot >> 13, (slot >> 11) & 3, (slot >> 10) & 1
+            mine = ((y + z + 2 * core) & 3) == e
+            row = (((z << 1) + (y >> 1)) << 3) + ((slot >> 7) & 7) + ((slot >> 6) & 1) * half_rows
+            lane = as_row(slot & (HALF - 1))
+            hot = one_hot(as_row(jnp.where(mine, row, -1)), 2 * half_rows)
             found = look_up(r.list_parts, hot, lane)
             weighted = as_row(r.weight[at, :]) * (found - as_row(r.innovation[at, :]))
-            total = total + sum_up(hot, lane, jnp.where(mine, weighted, 0.0), HALF)
+            total = total + sum_up(hot, lane, weighted, HALF)
         r.seen[...] += total
         return carry
 
@@ -438,25 +456,24 @@
     e, c, ens, cols = places()
     group = cols // ens
     z = c // group
-    last = cols - 1
+    home, at = list_home(c)
 
     def step(n, carry):
-        p = group * e + (c + 1 + n) % group
-        e2 = (e + 1 + n // group) % ens
-        send(r.returned.at[p % group], r.arrived.at[c], r.back_send, r.back_recv.at[z], spot(e2, p))
+        i = (at + 1 + n) % group
+        target = spot((e + 1 + n // group) % ens, column_of(e, i))
+        send(r.returned.at[i], r.arrived.at[c], r.back_send, r.back_recv.at[z], target)
         return carry
 
-    lax.fori_loop(0, last, step, 0)
-    own = c % group
-    p = group * e + own
-
-    @pl.when(p != c)
-    def _():
-        send(r.returned.at[own], r.arrived.at[c], r.back_send, r.back_recv.at[z], spot(e, p))
-
-    @pl.when(p == c)
-    def _():
-        pltpu.make_async_copy(r.returned.at[own], r.arrived.at[c], r.back_recv.at[z]).start()
+    lax.fori_loop(0, cols - 1, step, 0)
+
+    @pl.when(e != home)
+    def _():
+        target = spot(e, column_of(e, at))
+        send(r.returned.at[at], r.arrived.at[c], r.back_send, r.back_recv.at[z], target)
+
+    @pl.when(e == home)
+    def _():
+        pltpu.make_async_copy(r.returned.at[at], r.arrived.at[c], r.back_recv.at[z]).start()
 
 
 def spread(r):
@@ -563,18 +580,34 @@
     start_tiles(norths)
     start_tiles(easts)
 
-    def send_part(d):
-        peer = (e + d) % ens
+    right, left = (e + 1) % ens, (e + ens - 1) % ens
+    opposite = (e + 2) % ens
+    half = own // 2
+    ring = ring_neighbours()
+    level_part(r, opposite, own, scale, member_loads)
+    relays = [
+        send(
+            r.part.at[pl.ds(opposite * own + n * half, half)],
+            r.relayed.at[n],
+            r.term_send.at[n],
+            r.term_recv.at[n],
+            ring[n],
+        )
+        for n in range(2)
+    ]
+
+    def send_part(peer, n):
+        relays[n].wait_recv()
+        for l in range(half):
+            r.part[peer * own + n * half + l] += r.relayed[n, l]
         return send(
             r.part.at[pl.ds(peer * own, own)],
-            r.terms.at[d - 1],
-            r.term_send.at[d - 1],
-            r.term_recv.at[d - 1],
-            spot(peer, c),
+            r.terms.at[n],
+            r.term_send.at[2 + n],
+            r.term_recv.at[2 + n],
+            ring[n],
         )
 
-    level_part(r, (e + 2) % ens, own, scale, member_loads)
-    sums = [send_part(2)]
     wait_tiles(norths)
     wait_tiles(easts)
     make_coefs(
@@ -593,23 +626,23 @@
         r.fields[1, l] = two_steps(r.coefs, r.fields[0, l], r.halos[0, 0, l], r.halos[0, 1, l])
     halo = halo_copies(r.fields.at[1], 1)
     start_tiles(halo)
-    level_part(r, (e + 1) % ens, own, scale, None)
-    sums.append(send_part(1))
-    level_part(r, (e + 3) % ens, own, scale, None)
-    sums.append(send_part(3))
+    level_part(r, right, own, scale, None)
+    sums = [send_part(right, 0)]
+    level_part(r, left, own, scale, None)
+    sums.append(send_part(left, 1))
     level_part(r, e, own, scale, None)
     wait_tiles(halo)
     rows = r.table.shape[0] // own
     for l in range(own):
         total = two_steps(r.coefs, r.fields[1, l], r.halos[1, 0, l], r.halos[1, 1, l])
         r.table[l * rows : (l + 1) * rows, :] = total + r.part[e * own + l]
+    for copy in relays:
+        copy.wait_send()
     for copy in sums:
         copy.wait()
     for l in range(own):
-        total = r.table[l * rows : (l + 1) * rows, :]
-        for d in range(ens - 1):
-            total = total + r.terms[d, l]
-        r.table[l * rows : (l + 1) * rows, :] = total
+        at = slice(l * rows, (l + 1) * rows)
+        r.table[at, :] = r.table[at, :] + (r.terms[0, l] + r.terms[1, l])
     for one in late:
         one.wait()
     picks(r)
@@ -621,7 +654,8 @@
 
     halo = halo_copies(r.adjoint, 2)
     start_tiles(halo)
-    wholes = share(r.adjoint, r.whole, r.whole_send, r.whole_recv)
+    wholes = Share(r.adjoint, r.whole, r.whole_send, r.whole_recv)
+    wholes.start()
     for l in range(own):
         r.whole[e * own + l] = r.adjoint[l]
     wait_sends(r.arrived, r.back_send)
@@ -630,18 +664,20 @@
         r.fields[2, l] = two_steps(r.coefs, r.adjoint[l], r.halos[2, 0, l], r.halos[2, 1, l])
     halo = halo_copies(r.fields.at[2], 3)
     start_tiles(halo)
-    for copy in wholes:
-        copy.wait()
-    member_products(r, scale, 0, 2)
+    wholes.pass_on()
+    wholes.finish()
+    member_products(r, scale, 0, 1)
     wait_tiles(halo)
     for l in range(own):
         r.fields[3, l] = two_steps(r.coefs, r.fields[2, l], r.halos[3, 0, l], r.halos[3, 1, l])
-    smooths = share(r.fields.at[3], r.smooth, r.smooth_send, r.smooth_recv)
+    smooths = Share(r.fields.at[3], r.smooth, r.smooth_send, r.smooth_recv)
+    smooths.start()
     for l in range(own):
         r.smooth[e * own + l] = r.fields[3, l]
-    member_products(r, scale, 2, members)
-    for copy in smooths:
-        copy.wait()
+    member_products(r, scale, 1, 4)
+    smooths.pass_on()
+    member_products(r, scale, 4, members)
+    smooths.finish()
 
     def static_product(i, carry):
         rows = pl.ds(pl.multiple_of((i // 2) * 32, 32), 32)
@@ -655,17 +691,6 @@
         return carry
 
     lax.fori_loop(0, 4, static_product, 0)
-
-
-def store_kernel(static_ref, grad_ref, static_hbm, grad_hbm, static_sem, grad_sem):
-    copies = [
-        pltpu.make_async_copy(static_ref, static_hbm, static_sem),
-        pltpu.make_async_copy(grad_ref, grad_hbm, grad_sem),
-    ]
-    for copy in copies:
-        copy.start()
-    for copy in copies:
-        copy.wait()
 
 
 def in_hbm(array):
@@ -690,7 +715,8 @@
         "coefs": pltpu.VMEM((COEFS, rows, lanes), f32),
         "fields": pltpu.VMEM((4, own, rows, lanes), f32),
         "halos": pltpu.VMEM((4, 2, own, rows, lanes), f32),
-        "terms": pltpu.VMEM((ens - 1, own, rows, lanes), f32),
+        "relayed": pltpu.VMEM((2, own // 2, rows, lanes), f32),
+        "terms": pltpu.VMEM((2, own, rows, lanes), f32),
         "table": pltpu.VMEM((own * rows, lanes), f32),
         "cell_parts": pltpu.VMEM((2 * LANES, own * rows), bf16),
         "picked": pltpu.VMEM((lists, tiles, LANES), f32),
@@ -710,20 +736,20 @@
         "face_recv": dma((2, 2)),
         "halo_send": dma((4, 2)),
         "halo_recv": dma((4, 2)),
-        "term_send": dma((ens - 1,)),
-        "term_recv": dma((ens - 1,)),
+        "term_send": dma((4,)),
+        "term_recv": dma((4,)),
         "list_send": dma,
         "list_recv": dma,
         "back_send": dma,
         "back_recv": dma((ens,)),
-        "whole_send": dma((ens - 1,)),
-        "whole_recv": dma((ens - 1,)),
-        "smooth_send": dma((ens - 1,)),
-        "smooth_recv": dma((ens - 1,)),
+        "whole_send": dma((4,)),
+        "whole_recv": dma((4,)),
+        "smooth_send": dma((4,)),
+        "smooth_recv": dma((4,)),
     }
     names = scalars + tuple(name + "_hbm" for name in loaded) + ("static_grad", "grad") + tuple(scratch)
     shapes = [arrays["static"].shape, arrays["control"].shape]
-    static_grad, grad = pl.pallas_call(
+    return pl.pallas_call(
         functools.partial(kernel, names, scale),
         in_specs=[SMEM] * len(scalars) + [ANY] * len(loaded),
         out_specs=[VMEM, VMEM],
@@ -732,14 +758,6 @@
         compiler_params=params(collective_id=1, has_side_effects=True),
         name="gradients",
     )(*[arrays[name] for name in scalars], *[in_hbm(arrays[name]) for name in loaded])
-    return pl.pallas_call(
-        store_kernel,
-        in_specs=[VMEM, VMEM],
-        out_specs=[ANY, ANY],
-        out_shape=[jax.ShapeDtypeStruct(shape, f32) for shape in shapes],
-        scratch_shapes=[dma, dma],
-        name="store",
-    )(static_grad, grad)
 
 
 def local(

time: 82.1 us -> 78 us (0.950)
  Pallas kernels: 77.8 us -> 74.4 us
    pallas_call x1 -> x0, Pallas kernels: 4.56 us -> none  [gradients(): pl.pallas_call(store_kernel, in_specs=[VMEM, VMEM], out_specs=[ANY, ANY],...]
    pallas_call x1, Pallas kernels: 73.2 us -> 74.4 us  [gradients(): pl.pallas_call(functools.partial(kernel, names, scale), in_specs=[SMEM] *...]
    unnamed x4 -> x2, local copies, waits for them, and re-layouts: 2.74 us -> 2.81 us
where the time goes in v6:
time: 78 us; the launch traced here: 77.9 us
  Pallas kernels  74.4 us (95%)
  local copies, waits for them, and re-layouts  2.81 us (4%)
    pallas_call x1, Pallas kernels, gradients(): pl.pallas_call(functools.partial(kernel, names, scale), in_specs=[SMEM] *...  74.4 us
    unnamed x2, local copies, waits for them, and re-layouts  2.81 us

profile of v6, /device:TPU:32, one launch (start us, length us, event | category | flops | bytes accessed | tf_op | source)
XLA Modules:
  0.0 77.9 jit_solution(15104349879211975001)
XLA Ops:
  0.6 74.4 %gradients.1 = (f32[16,64,128]{2,1,0:T(8,128)S(1)}, f32[8,16,64,128]{3,2,1,0:T(8,128)S(1)}) custom-call(f32[16,16]{1,0:T(8,128)} %refs_0_.1, f32[16,16]{1,0:T(8,128)} %refs_1_.1, s32[32]{0:T(128)} %refs_2_.1, f32[16,64,128]{2,1,0:T(8,128)} %bitcast.42, f32[64,128]{1,0:T(8,128)} %bitcast.46, f32[64,128]{1,0:T(8,128)} %bitcast.47, s32[32,1024]{1,0:T(8,128)} %refs_6_.1, ...), custom_call_target="tpu_custom_call" | custom-call | tf_op jit(solution)/shard_map/gradients/pallas_call | solution.py:752
  75.1 0.8 %copy.23 = f32[16,2,4096]{2,1,0:T(2,128)} copy(f32[16,2,4096]{2,1,0:T(2,128)S(1)} %bitcast.39) | data formatting | bytes 1048576
  75.8 2.0 %copy.24 = f32[8,16,2,4096]{3,2,1,0:T(2,128)} copy(f32[8,16,2,4096]{3,2,1,0:T(2,128)S(1)} %bitcast.38) | data formatting | bytes 8388608

commit v7 on v5

v7 whole, which is shorter than its diff:
```python
import functools
import math
import types

import jax
import jax.numpy as jnp
from jax import lax
from jax.experimental import pallas as pl
from jax.experimental.pallas import tpu as pltpu
from jax.sharding import PartitionSpec as P

NDIFF = 4
LANES = 128
VMEM_LIMIT = 52 * 1024 * 1024

precise = lax.Precision.HIGHEST

SMEM = pl.BlockSpec(memory_space=pltpu.SMEM)
VMEM = pl.BlockSpec(memory_space=pltpu.VMEM)


def params(**more):
    return pltpu.CompilerParams(vmem_limit_bytes=VMEM_LIMIT, **more)


def to_tiles(cells):
    lead = cells.shape[:-2]
    rows, length = cells.shape[-2:]
    split = cells.reshape(lead + (rows, length // LANES, LANES))
    return jnp.swapaxes(split, -3, -2).reshape(lead + (rows * length // LANES, LANES))


def from_tiles(tiles, rows):
    lead = tiles.shape[:-2]
    count = tiles.shape[-2] // rows
    split = tiles.reshape(lead + (count, rows, LANES))
    return jnp.swapaxes(split, -3, -2).reshape(lead + (rows, count * LANES))


def iota(shape, dim):
    return lax.broadcasted_iota(jnp.int32, shape, dim)


def small(ids):
    return ids.astype(jnp.float32).astype(jnp.bfloat16)


def one_hot(ids, count):
    width = ids.shape[1]
    hit = small(iota((count, width), 0)) == small(ids)
    return jnp.where(hit, jnp.bfloat16(1), jnp.bfloat16(0))


def table_parts(table, parts_ref):
    lanes = table.shape[1]
    high = table.astype(jnp.bfloat16).astype(jnp.float32)
    parts_ref[:lanes, :] = high.T.astype(jnp.bfloat16)
    parts_ref[lanes:, :] = (table - high).T.astype(jnp.bfloat16)


def look_up(parts_ref, hot, lane):
    lanes = parts_ref.shape[0] // 2
    found = jnp.dot(parts_ref[...], hot, preferred_element_type=jnp.float32)
    found = found[:lanes] + found[lanes:]
    found = jnp.where(iota(found.shape, 0) == lane, found, 0.0)
    return jnp.sum(found, axis=0, keepdims=True)


def sum_up(hot, lane, values, lanes):
    high = values.astype(jnp.bfloat16)
    low = (values - high.astype(jnp.float32)).astype(jnp.bfloat16)
    hit = small(iota((lanes, lane.shape[1]), 0)) == small(lane)
    zero = jnp.bfloat16(0)
    parts = jnp.concatenate([jnp.where(hit, high, zero), jnp.where(hit, low, zero)], axis=0)
    return lax.dot_general(hot, parts, (((1,), (1,)), ((), ())), preferred_element_type=jnp.float32)


def as_row(block):
    return jnp.concatenate([block[i : i + 1, :] for i in range(block.shape[0])], axis=1)


def cell_place(index, first_cell, cells):
    inside = index - first_cell
    level = inside >> 13
    row = (level << 6) + (((inside >> 7) & 31) << 1) + ((inside >> 12) & 1)
    mine = (inside >= 0) & (inside < cells)
    return jnp.where(mine, row, -1), inside & (LANES - 1)


MESH = pl.DeviceIdType.MESH


def spot(ens, cols):
    return {"ens": ens, "cols": cols}


def places():
    return (lax.axis_index("ens"), lax.axis_index("cols"), lax.axis_size("ens"), lax.axis_size("cols"))


def greet(barrier, target):
    pl.semaphore_signal(barrier, inc=1, device_id=target, device_id_type=MESH)


def send(source, landing, send_sem, recv_sem, target):
    copy = pltpu.make_async_remote_copy(
        src_ref=source,
        dst_ref=landing,
        send_sem=send_sem,
        recv_sem=recv_sem,
        device_id=target,
        device_id_type=MESH,
    )
    copy.start()
    return copy


def odd_rows():
    return (iota((64, LANES), 0) & 1) == 1


def blend(odd, even):
    return jnp.where(odd_rows(), odd, even)


def swapped(tile):
    return blend(pltpu.roll(tile, 1, 0), pltpu.roll(tile, 63, 0))


def east_of(tile):
    near = pltpu.roll(tile, LANES - 1, 1)
    return jnp.where(iota((64, LANES), 1) == LANES - 1, pltpu.roll(near, 62, 0), near)


def west_of(tile):
    near = pltpu.roll(tile, 1, 1)
    return jnp.where(iota((64, LANES), 1) == 0, pltpu.roll(near, 2, 0), near)


SIDES = ((0, 2), (1, 1), (2, -1), (3, -2))
UP1, OWN, DOWN1, RIM2, RIM1 = range(5)


def make_coefs(coefs, own, faces):
    e, c, ens, cols = places()

    def keep(condition):
        return condition.astype(jnp.float32)

    up2, up1, down1, down2 = [faces[n, 0] for n in range(4)]
    norths = (up1, own[0], down1)
    belows = (own[0], down1, down2)
    easts = (faces[1, 1], own[1], faces[2, 1])
    keeps = (keep(c > 0), 1.0, keep(c < cols - 1))

    def put(t, pair, outer, east, kept):
        west = west_of(east)
        coefs[t, 0] = (1.0 - pair - outer - east - west) * kept
        coefs[t, 1] = pair * kept
        coefs[t, 2] = outer * kept
        coefs[t, 3] = east * kept
        coefs[t, 4] = west * kept

    for t in range(3):
        north = norths[t]
        put(t, blend(north, swapped(north)), blend(swapped(belows[t]), north), easts[t], keeps[t])
    put(
        RIM2,
        blend(up2, swapped(down2)),
        blend(swapped(up1), down2),
        blend(faces[0, 1], faces[3, 1]),
        blend(keep(c > 1), keep(c < cols - 2)),
    )
    for n in range(5):
        coefs[RIM1, n] = blend(coefs[UP1, n], coefs[DOWN1, n])


def step_tile(coefs, t, tile, beside, beyond):
    return (
        coefs[t, 0] * tile
        + coefs[t, 1] * swapped(beside)
        + coefs[t, 2] * swapped(beyond)
        + coefs[t, 3] * east_of(tile)
        + coefs[t, 4] * west_of(tile)
    )


def diffused(coefs, own, up2, up1, down1, down2):
    rim = step_tile(coefs, RIM2, blend(up2, down2), blend(down2, up2), blend(down1, up1))
    up, here, down = (
        step_tile(coefs, UP1, up1, up1, blend(up2, own)),
        step_tile(coefs, OWN, own, own, blend(up1, down1)),
        step_tile(coefs, DOWN1, down1, down1, blend(own, down2)),
    )
    up, here, down = (
        step_tile(coefs, UP1, up, up, blend(rim, here)),
        step_tile(coefs, OWN, here, here, blend(up, down)),
        step_tile(coefs, DOWN1, down, down, blend(here, rim)),
    )
    rim = blend(up, down)
    rim, here = (
        step_tile(coefs, RIM1, rim, blend(down, up), here),
        step_tile(coefs, OWN, here, here, rim),
    )
    return step_tile(coefs, OWN, here, here, rim)


def with_side(by, action):
    e, c, ens, cols = places()
    pl.when(c < cols - by if by > 0 else c >= -by)(action)


def tile_copies(source, landing, send_sems, recv_sems):
    e, c, ens, cols = places()
    return [
        pltpu.make_async_remote_copy(
            src_ref=source,
            dst_ref=landing.at[n],
            send_sem=send_sems.at[n],
            recv_sem=recv_sems.at[n],
            device_id=spot(e, (c + by + cols) % cols),
            device_id_type=MESH,
        )
        for n, by in SIDES
    ]


def start_tiles(copies):
    for n, by in SIDES:
        with_side(by, copies[n].start)


def wait_tiles(copies):
    for n, by in SIDES:
        with_side(by, copies[n].wait_send)
        with_side(-by, copies[n].wait_recv)


def clear_rims(refs):
    e, c, ens, cols = places()
    for ref in refs:
        for n, by in SIDES:

            @pl.when(c < by if by > 0 else c >= cols + by)
            def _(ref=ref, n=n):
                ref[n] = jnp.zeros(ref.shape[1:], jnp.float32)


def greet_neighbours(barrier):
    e, c, ens, cols = places()
    for n, by in SIDES:
        with_side(by, functools.partial(greet, barrier, spot(e, (c + by + cols) % cols)))
    for d in range(1, ens):
        greet(barrier, spot((e + d) % ens, c))


def column_of(place):
    e, c, ens, cols = places()
    return place * ens + (e - c + cols) % ens


def wait_barrier(barrier):
    e, c, ens, cols = places()
    around = 0
    for n, by in SIDES:
        around = around + (1 - (c + by) // cols if by > 0 else (c + cols + by) // cols)
    all_leave = ((e - 2 * c + 2 * cols) % ens + ens - 1) // ens
    pl.semaphore_wait(barrier, ens - 1 + around + cols - 1 + all_leave)


def wait_sends(lists_ref, send_sem):
    e, c, ens, cols = places()
    few = lists_ref.at[pl.ds(0, cols - 1)]

    @pl.when(e == (2 * c) % ens)
    def _():
        pltpu.make_async_copy(few, few, send_sem).wait()

    @pl.when(e != (2 * c) % ens)
    def _():
        pltpu.make_async_copy(lists_ref, lists_ref, send_sem).wait()


HALF = 64
BLOCK = 32
ANY = pl.BlockSpec(memory_space=pl.ANY)


def greet_all(barrier):
    e, c, ens, cols = places()
    group = cols // ens
    at = c // ens
    greet_neighbours(barrier)

    def senders(n, carry):
        greet(barrier, spot((e + 1 + n // group) % ens, column_of((at + 1 + n) % group)))
        return carry

    lax.fori_loop(0, cols - 1, senders, 0)

    @pl.when(e != (2 * c) % ens)
    def _():
        greet(barrier, spot(e, column_of(at)))


def share(own_ref, whole_ref, send_sems, recv_sems):
    e, c, ens, cols = places()
    count = own_ref.shape[0]
    return [
        send(
            own_ref,
            whole_ref.at[pl.ds(e * count, count)],
            send_sems.at[d - 1],
            recv_sems.at[d - 1],
            spot((e + d) % ens, c),
        )
        for d in (2, 1, 3)
    ]


def level_part(r, peer, own, scale, i, loads=None):
    members, levels = r.control.shape[:2]
    first = peer * own
    rows = pl.ds(i * 32, 32)

    def member(k, totals):
        if loads is not None:
            for load in loads(k):
                load.wait()
        sums = [jnp.zeros((32, LANES), jnp.float32)] * own
        for m in range(levels):
            source = r.control[k, m, rows, :]
            sums = [sums[l] + r.local[first + l, m] * source for l in range(own)]
        return tuple(
            totals[l] + r.pert[k, first + l, rows, :].astype(jnp.float32) * sums[l] for l in range(own)
        )

    totals = lax.fori_loop(0, members, member, (jnp.zeros((32, LANES), jnp.float32),) * own)
    for l in range(own):
        r.part[first + l, rows, :] = totals[l] * scale


def picks(r):
    e, c, ens, cols = places()
    cell_rows = r.table.shape[0]
    cells = cell_rows * LANES
    capacity = r.index.shape[1]
    slots = iota((1, capacity), 1)
    place = r.landing.at[e, c // ens]
    table_parts(r.table[...], r.cell_parts)

    def some(i, carry):
        for j in range(8):
            q = (c + 1 + i * 8 + j) % cols
            row, lane = cell_place(r.index[pl.ds(q, 1), :], e * cells, cells)
            row = jnp.where(slots < r.counts[q], row, -1)
            found = look_up(r.cell_parts, one_hot(row, cell_rows), lane)
            for t in range(capacity // LANES):
                r.picked[q, pl.ds(t, 1), :] = found[:, t * LANES : (t + 1) * LANES]
        for j in range(7):
            q = (c + 1 + i * 8 + j) % cols
            send(r.picked.at[q], place, r.list_send, r.list_recv, spot((c + q) % ens, q))
        q = (c + 8 + i * 8) % cols

        @pl.when((q != c) | (e != (2 * c) % ens))
        def _():
            send(r.picked.at[q], place, r.list_send, r.list_recv, spot((c + q) % ens, q))

        @pl.when((q == c) & (e == (2 * c) % ens))
        def _():
            pltpu.make_async_copy(r.picked.at[q], place, r.list_recv).start()

        return carry

    lax.fori_loop(0, cols // 8, some, 0)


def observe(r):
    e, c, ens, cols = places()
    total = r.landing[0]
    for n in range(1, ens):
        total = total + r.landing[n]
    half_rows = total.shape[0] * total.shape[1]
    table = total.reshape(half_rows, LANES)
    table_parts(jnp.concatenate([table[:, :HALF], table[:, HALF:]], axis=0), r.list_parts)
    r.seen[...] = jnp.zeros_like(r.seen)

    def some(i, carry):
        total = jnp.zeros(r.seen.shape, jnp.float32)
        for j in range(2):
            at = pl.ds(pl.multiple_of((i * 2 + j) * BLOCK, BLOCK), BLOCK)
            slot = r.slot[at, :]
            column = slot >> 10
            mine = ((column + c) & (ens - 1)) == e
            row = ((column >> 2) << 3) + ((slot >> 7) & 7) + ((slot >> 6) & 1) * half_rows
            lane = as_row(slot & (HALF - 1))
            hot = one_hot(as_row(jnp.where(mine, row, -1)), 2 * half_rows)
            found = look_up(r.list_parts, hot, lane)
            weighted = as_row(r.weight[at, :]) * (found - as_row(r.innovation[at, :]))
            total = total + sum_up(hot, lane, weighted, HALF)
        r.seen[...] += total
        return carry

    lax.fori_loop(0, r.slot.shape[0] // (2 * BLOCK), some, 0)
    seen = r.seen[:, :HALF] + r.seen[:, HALF:]
    r.returned[...] = jnp.concatenate([seen[:half_rows], seen[half_rows:]], axis=1).reshape(r.returned.shape)


def give_back(r):
    e, c, ens, cols = places()
    group = cols // ens
    at = c // ens
    recv = r.back_recv.at[c // group]

    def step(n, carry):
        i = (at + 1 + n) % group
        target = spot((e + 1 + n // group) % ens, column_of(i))
        send(r.returned.at[i], r.arrived.at[c], r.back_send, recv, target)
        return carry

    lax.fori_loop(0, cols - 1, step, 0)

    @pl.when(e != (2 * c) % ens)
    def _():
        send(r.returned.at[at], r.arrived.at[c], r.back_send, recv, spot(e, column_of(at)))

    @pl.when(e == (2 * c) % ens)
    def _():
        pltpu.make_async_copy(r.returned.at[at], r.arrived.at[c], recv).start()


def spread(r):
    e, c, ens, cols = places()
    group = cols // ens
    capacity = r.index.shape[1]
    slots = iota((1, capacity), 1)
    cell_rows = r.both.shape[0]
    cells = cell_rows * LANES
    r.both[...] = jnp.zeros_like(r.both)

    def some(i, carry):
        lists = r.arrived.at[pl.ds(i * group, group)]
        pltpu.make_async_copy(lists, lists, r.back_recv.at[i]).wait()
        total = jnp.zeros(r.both.shape, jnp.float32)
        for j in range(group):
            q = i * group + j
            row, lane = cell_place(r.index[pl.ds(q, 1), :], e * cells, cells)
            row = jnp.where(slots < r.counts[q], row, -1)
            total = total + sum_up(one_hot(row, cell_rows), lane, as_row(r.arrived[q]), LANES)
        r.both[...] += total
        return carry

    lax.fori_loop(0, ens, some, 0)
    r.adjoint[...] = (r.both[:, :LANES] + r.both[:, LANES:]).reshape(r.adjoint.shape)


def member_products(r, scale, first_member, last_member):
    levels = r.static.shape[0]

    def member(k, carry):
        def chunk(i, inner):
            rows = pl.ds(pl.multiple_of((i // 2) * 32, 32), 32)
            first = (i % 2) * 8
            totals = [jnp.zeros((32, LANES), jnp.float32)] * 8
            for m in range(levels):
                source = r.pert[k, m, rows, :].astype(jnp.float32) * r.whole[m, rows, :]
                totals = [totals[n] + r.local[m, first + n] * source for n in range(8)]
            for n in range(8):
                r.grad[k, first + n, rows, :] = r.control[k, first + n, rows, :] + totals[n] * scale
            return inner

        lax.fori_loop(0, 4, chunk, 0)
        return carry

    lax.fori_loop(first_member, last_member, member, 0)


def kernel(names, scale, *refs):
    r = types.SimpleNamespace(**dict(zip(names, refs)))
    e, c, ens, cols = places()
    levels = r.static.shape[0]
    members = r.control.shape[0]
    own = levels // ens

    def member_loads(k):
        return [
            pltpu.make_async_copy(r.control_hbm.at[k], r.control.at[k], r.control_load.at[k]),
            pltpu.make_async_copy(r.pert_hbm.at[k], r.pert.at[k], r.pert_load.at[k]),
        ]

    def load(name, n):
        return pltpu.make_async_copy(getattr(r, name + "_hbm"), getattr(r, name), r.load.at[n])

    early = [
        load("static", 0),
        pltpu.make_async_copy(r.north_hbm, r.own_faces.at[0], r.load.at[1]),
        pltpu.make_async_copy(r.east_hbm, r.own_faces.at[1], r.load.at[2]),
    ]
    late = [load("index", 3), load("slot", 4), load("innovation", 5), load("weight", 6)]
    for one in early:
        one.start()

    def start_members(k, carry):
        for one in member_loads(k):
            one.start()
        return carry

    lax.fori_loop(0, members, start_members, 0)
    for one in late:
        one.start()
    barrier = pltpu.get_barrier_semaphore()
    greet_all(barrier)
    clear_rims([r.faces, r.halos.at[0], r.halos.at[1]])
    for one in early:
        one.wait()

    def product(i, carry):
        rows = pl.ds(pl.multiple_of(i * 32, 32), 32)
        totals = [jnp.zeros((32, LANES), jnp.float32)] * own
        for m in range(levels):
            source = r.static[m, rows, :]
            totals = [totals[l] + r.root[e * own + l, m] * source for l in range(own)]
        for l in range(own):
            r.fields[0, l, rows, :] = totals[l]
        return carry

    lax.fori_loop(0, 2, product, 0)
    wait_barrier(barrier)

    def halo_copies(field, n):
        return tile_copies(field, r.halos.at[n], r.halo_send.at[n], r.halo_recv.at[n])

    halo = halo_copies(r.fields.at[0], 0)
    start_tiles(halo)
    faces = tile_copies(r.own_faces, r.faces, r.face_send, r.face_recv)
    start_tiles(faces)
    sums = []

    def send_part(d, i):
        peer = (e + d) % ens
        rows = pl.ds(i * 32, 32)
        sums.append(
            send(
                r.part.at[pl.ds(peer * own, own), rows],
                r.terms.at[d - 1, :, rows],
                r.term_send.at[d - 1, i],
                r.term_recv.at[d - 1, i],
                spot(peer, c),
            )
        )

    for n, (d, i) in enumerate(((2, 0), (2, 1), (1, 0), (3, 0), (1, 1), (3, 1))):
        level_part(r, (e + d) % ens, own, scale, i, member_loads if n == 0 else None)
        send_part(d, i)
    wait_tiles(faces)
    make_coefs(r.coefs, r.own_faces, r.faces)
    level_part(r, e, own, scale, 0)
    level_part(r, e, own, scale, 1)
    wait_tiles(halo)
    cell_rows = r.table.shape[0] // own

    def static_level(l, carry):
        around = [r.halos[0, n, l] for n in range(4)]
        total = diffused(r.coefs, r.fields[0, l], *around) + r.part[e * own + l]
        r.table[pl.ds(pl.multiple_of(l * cell_rows, cell_rows), cell_rows), :] = total
        return carry

    lax.fori_loop(0, own, static_level, 0)
    for copy in sums:
        copy.wait()
    for l in range(own):
        at = slice(l * cell_rows, (l + 1) * cell_rows)
        r.table[at, :] = r.table[at, :] + ((r.terms[0, l] + r.terms[1, l]) + r.terms[2, l])
    for one in late:
        one.wait()
    picks(r)
    pltpu.make_async_copy(r.landing, r.landing, r.list_recv).wait()
    observe(r)
    give_back(r)
    wait_sends(r.picked, r.list_send)
    spread(r)

    halo = halo_copies(r.adjoint, 1)
    start_tiles(halo)
    wholes = share(r.adjoint, r.whole, r.whole_send, r.whole_recv)
    for l in range(own):
        r.whole[e * own + l] = r.adjoint[l]
    wait_sends(r.arrived, r.back_send)
    wait_tiles(halo)

    def adjoint_level(l, carry):
        around = [r.halos[1, n, l] for n in range(4)]
        smoothed = diffused(r.coefs, r.adjoint[l], *around)
        r.fields[1, l] = smoothed
        r.smooth[e * own + l] = smoothed
        return carry

    lax.fori_loop(0, own, adjoint_level, 0)
    smooths = share(r.fields.at[1], r.smooth, r.smooth_send, r.smooth_recv)
    for copy in wholes:
        copy.wait()
    member_products(r, scale, 0, members)
    for copy in smooths:
        copy.wait()

    def static_product(i, carry):
        rows = pl.ds(pl.multiple_of((i // 2) * 32, 32), 32)
        first = (i % 2) * 8
        totals = [r.static[first + n, rows, :] for n in range(8)]
        for m in range(levels):
            source = r.smooth[m, rows, :]
            totals = [totals[n] + r.root[m, first + n] * source for n in range(8)]
        for n in range(8):
            r.static_grad[first + n, rows, :] = totals[n]
        return carry

    lax.fori_loop(0, 4, static_product, 0)


def in_hbm(array):
    return pltpu.with_memory_space_constraint(array, pltpu.HBM)


def gradients(arrays, ens, scale):
    levels, rows, lanes = arrays["static"].shape
    own = levels // ens
    members = arrays["control"].shape[0]
    lists, capacity = arrays["index"].shape
    tiles = capacity // LANES
    half_rows = lists // ens * tiles
    f32, bf16 = jnp.float32, jnp.bfloat16
    dma = pltpu.SemaphoreType.DMA
    scalars = ("local", "root", "counts")
    loaded = ("static", "north", "east", "index", "slot", "innovation", "weight", "control", "pert")
    scratch = {
        name: pltpu.VMEM(arrays[name].shape, arrays[name].dtype)
        for name in loaded
        if name not in ("north", "east")
    }
    scratch |= {
        "part": pltpu.VMEM((levels, rows, lanes), f32),
        "own_faces": pltpu.VMEM((2, rows, lanes), f32),
        "faces": pltpu.VMEM((4, 2, rows, lanes), f32),
        "coefs": pltpu.VMEM((5, 5, rows, lanes), f32),
        "fields": pltpu.VMEM((2, own, rows, lanes), f32),
        "halos": pltpu.VMEM((2, 4, own, rows, lanes), f32),
        "terms": pltpu.VMEM((ens - 1, own, rows, lanes), f32),
        "table": pltpu.VMEM((own * rows, lanes), f32),
        "cell_parts": pltpu.VMEM((2 * LANES, own * rows), bf16),
        "picked": pltpu.VMEM((lists, tiles, LANES), f32),
        "landing": pltpu.VMEM((ens, lists // ens, tiles, LANES), f32),
        "list_parts": pltpu.VMEM((2 * HALF, 2 * half_rows), bf16),
        "seen": pltpu.VMEM((2 * half_rows, 2 * HALF), f32),
        "returned": pltpu.VMEM((lists // ens, tiles, LANES), f32),
        "arrived": pltpu.VMEM((lists, tiles, LANES), f32),
        "both": pltpu.VMEM((own * rows, 2 * LANES), f32),
        "adjoint": pltpu.VMEM((own, rows, lanes), f32),
        "whole": pltpu.VMEM((levels, rows, lanes), f32),
        "smooth": pltpu.VMEM((levels, rows, lanes), f32),
        "load": dma((7,)),
        "control_load": dma((members,)),
        "pert_load": dma((members,)),
        "face_send": dma((4,)),
        "face_recv": dma((4,)),
        "halo_send": dma((2, 4)),
        "halo_recv": dma((2, 4)),
        "term_send": dma((ens - 1, 2)),
        "term_recv": dma((ens - 1, 2)),
        "list_send": dma,
        "list_recv": dma,
        "back_send": dma,
        "back_recv": dma((ens,)),
        "whole_send": dma((ens - 1,)),
        "whole_recv": dma((ens - 1,)),
        "smooth_send": dma((ens - 1,)),
        "smooth_recv": dma((ens - 1,)),
    }
    names = scalars + tuple(name + "_hbm" for name in loaded) + ("static_grad", "grad") + tuple(scratch)
    shapes = [arrays["static"].shape, arrays["control"].shape]
    return pl.pallas_call(
        functools.partial(kernel, names, scale),
        in_specs=[SMEM] * len(scalars) + [ANY] * len(loaded),
        out_specs=[VMEM, VMEM],
        out_shape=[pltpu.VMEM(shape, f32) for shape in shapes],
        scratch_shapes=list(scratch.values()),
        compiler_params=params(collective_id=1, has_side_effects=True),
        name="gradients",
    )(*[arrays[name] for name in scalars], *[in_hbm(arrays[name]) for name in loaded])


def local(
    static_control,
    ensemble_control,
    perturbations,
    vertical_root,
    vertical_local,
    face_north,
    face_east,
    innovation,
    obs_weight,
    obs_slot,
    send_index,
    send_count,
):
    grid_rows = static_control.shape[1]
    ens = lax.axis_size("ens")
    arrays = {
        "local": vertical_local,
        "root": vertical_root,
        "counts": send_count,
        "static": to_tiles(static_control),
        "north": to_tiles(face_north),
        "east": to_tiles(face_east),
        "index": send_index,
        "slot": obs_slot.reshape(-1, LANES),
        "innovation": innovation.reshape(-1, LANES),
        "weight": obs_weight.reshape(-1, LANES),
        "control": to_tiles(ensemble_control),
        "pert": to_tiles(perturbations),
    }
    scale = 1.0 / math.sqrt(ensemble_control.shape[0] * ens - 1)
    static_grad, grad = gradients(arrays, ens, scale)
    return (from_tiles(static_grad, grid_rows), from_tiles(grad, grid_rows))


def solution(mesh):
    placed = (
        P(None, "cols", None),
        P("ens", None, "cols", None),
        P("ens", None, "cols", None),
        P(),
        P(),
        P("cols", None),
        P("cols", None),
        P("cols"),
        P("cols"),
        P("cols"),
        P("cols", None),
        P("cols"),
    )
    return jax.shard_map(
        local,
        mesh=mesh,
        in_specs=placed,
        out_specs=(P(None, "cols", None), P("ens", None, "cols", None)),
        check_vma=False,
    )
```

time: 82.1 us -> 72.7 us (0.89)
  Pallas kernels: 77.8 us -> 67.9 us
    pallas_call x1, Pallas kernels: 73.2 us -> 67.9 us  [gradients(): pl.pallas_call(functools.partial(kernel, names, scale), in_specs=[SMEM] *...]
    pallas_call x1 -> x0, Pallas kernels: 4.56 us -> none  [gradients(): pl.pallas_call(store_kernel, in_specs=[VMEM, VMEM], out_specs=[ANY, ANY],...]
    unnamed x4 -> x2, local copies, waits for them, and re-layouts: 2.74 us -> 2.81 us
where the time goes in v7:
time: 72.7 us; the launch traced here: 71.4 us
  Pallas kernels  67.9 us (93%)
  local copies, waits for them, and re-layouts  2.81 us (4%)
    pallas_call x1, Pallas kernels, gradients(): pl.pallas_call(functools.partial(kernel, names, scale), in_specs=[SMEM] *...  67.9 us
    unnamed x2, local copies, waits for them, and re-layouts  2.81 us

profile of v7, /device:TPU:32, one launch (start us, length us, event | category | flops | bytes accessed | tf_op | source)
XLA Modules:
  0.0 71.4 jit_solution(8033740148382825510)
XLA Ops:
  0.6 67.9 %gradients.1 = (f32[16,64,128]{2,1,0:T(8,128)S(1)}, f32[8,16,64,128]{3,2,1,0:T(8,128)S(1)}) custom-call(f32[16,16]{1,0:T(8,128)} %refs_0_.1, f32[16,16]{1,0:T(8,128)} %refs_1_.1, s32[32]{0:T(128)} %refs_2_.1, f32[16,64,128]{2,1,0:T(8,128)} %bitcast.42, f32[64,128]{1,0:T(8,128)} %bitcast.46, f32[64,128]{1,0:T(8,128)} %bitcast.47, s32[32,1024]{1,0:T(8,128)} %refs_6_.1, ...), custom_call_target="tpu_custom_call" | custom-call | tf_op jit(solution)/shard_map/gradients/pallas_call | solution.py:680
  68.5 0.8 %copy.23 = f32[16,2,4096]{2,1,0:T(2,128)} copy(f32[16,2,4096]{2,1,0:T(2,128)S(1)} %bitcast.39) | data formatting | bytes 1048576
  69.3 2.0 %copy.24 = f32[8,16,2,4096]{3,2,1,0:T(2,128)} copy(f32[8,16,2,4096]{3,2,1,0:T(2,128)S(1)} %bitcast.38) | data formatting | bytes 8388608

commit v8 on v7

--- a/solution.py
+++ b/solution.py
@@ -282,7 +282,7 @@
 
 
 HALF = 64
-BLOCK = 32
+BLOCK = 64
 ANY = pl.BlockSpec(memory_space=pl.ANY)
 
 
@@ -318,15 +318,12 @@
     ]
 
 
-def level_part(r, peer, own, scale, i, loads=None):
+def level_part(r, peer, own, scale, i):
     members, levels = r.control.shape[:2]
     first = peer * own
     rows = pl.ds(i * 32, 32)
 
     def member(k, totals):
-        if loads is not None:
-            for load in loads(k):
-                load.wait()
         sums = [jnp.zeros((32, LANES), jnp.float32)] * own
         for m in range(levels):
             source = r.control[k, m, rows, :]
@@ -482,12 +479,6 @@
     members = r.control.shape[0]
     own = levels // ens
 
-    def member_loads(k):
-        return [
-            pltpu.make_async_copy(r.control_hbm.at[k], r.control.at[k], r.control_load.at[k]),
-            pltpu.make_async_copy(r.pert_hbm.at[k], r.pert.at[k], r.pert_load.at[k]),
-        ]
-
     def load(name, n):
         return pltpu.make_async_copy(getattr(r, name + "_hbm"), getattr(r, name), r.load.at[n])
 
@@ -496,17 +487,9 @@
         pltpu.make_async_copy(r.north_hbm, r.own_faces.at[0], r.load.at[1]),
         pltpu.make_async_copy(r.east_hbm, r.own_faces.at[1], r.load.at[2]),
     ]
-    late = [load("index", 3), load("slot", 4), load("innovation", 5), load("weight", 6)]
-    for one in early:
-        one.start()
-
-    def start_members(k, carry):
-        for one in member_loads(k):
-            one.start()
-        return carry
-
-    lax.fori_loop(0, members, start_members, 0)
-    for one in late:
+    members_loads = [load("control", 3), load("pert", 4)]
+    late = [load("index", 5), load("slot", 6), load("innovation", 7), load("weight", 8)]
+    for one in early + members_loads + late:
         one.start()
     barrier = pltpu.get_barrier_semaphore()
     greet_all(barrier)
@@ -525,6 +508,10 @@
         return carry
 
     lax.fori_loop(0, 2, product, 0)
+    for one in members_loads:
+        one.wait()
+    for i in range(2):
+        level_part(r, (e + 2) % ens, own, scale, i)
     wait_barrier(barrier)
 
     def halo_copies(field, n):
@@ -549,8 +536,10 @@
             )
         )
 
-    for n, (d, i) in enumerate(((2, 0), (2, 1), (1, 0), (3, 0), (1, 1), (3, 1))):
-        level_part(r, (e + d) % ens, own, scale, i, member_loads if n == 0 else None)
+    for i in range(2):
+        send_part(2, i)
+    for d, i in ((1, 0), (3, 0), (1, 1), (3, 1)):
+        level_part(r, (e + d) % ens, own, scale, i)
         send_part(d, i)
     wait_tiles(faces)
     make_coefs(r.coefs, r.own_faces, r.faces)
@@ -588,33 +577,47 @@
     wait_sends(r.arrived, r.back_send)
     wait_tiles(halo)
 
-    def adjoint_level(l, carry):
+    smooths = []
+    for l in range(own):
         around = [r.halos[1, n, l] for n in range(4)]
         smoothed = diffused(r.coefs, r.adjoint[l], *around)
         r.fields[1, l] = smoothed
         r.smooth[e * own + l] = smoothed
-        return carry
-
-    lax.fori_loop(0, own, adjoint_level, 0)
-    smooths = share(r.fields.at[1], r.smooth, r.smooth_send, r.smooth_recv)
+        for d in (2, 1, 3):
+            copy = send(
+                r.fields.at[1, l],
+                r.smooth.at[e * own + l],
+                r.smooth_send.at[d - 1, l],
+                r.smooth_recv.at[d - 1, l],
+                spot((e + d) % ens, c),
+            )
+            smooths.append((d, copy))
     for copy in wholes:
         copy.wait()
     member_products(r, scale, 0, members)
-    for copy in smooths:
-        copy.wait()
-
-    def static_product(i, carry):
-        rows = pl.ds(pl.multiple_of((i // 2) * 32, 32), 32)
-        first = (i % 2) * 8
-        totals = [r.static[first + n, rows, :] for n in range(8)]
-        for m in range(levels):
-            source = r.smooth[m, rows, :]
-            totals = [totals[n] + r.root[m, first + n] * source for n in range(8)]
-        for n in range(8):
-            r.static_grad[first + n, rows, :] = totals[n]
-        return carry
-
-    lax.fori_loop(0, 4, static_product, 0)
+
+    def add_levels(peer, source):
+        first = peer * own
+
+        def some(i, carry):
+            rows = pl.ds(pl.multiple_of((i // 2) * 32, 32), 32)
+            at = (i % 2) * 8
+            totals = [source[at + n, rows, :] for n in range(8)]
+            for m in range(own):
+                level = r.smooth[first + m, rows, :]
+                totals = [totals[n] + r.root[first + m, at + n] * level for n in range(8)]
+            for n in range(8):
+                r.static_grad[at + n, rows, :] = totals[n]
+            return carry
+
+        lax.fori_loop(0, 4, some, 0)
+
+    add_levels(e, r.static)
+    for d in (1, 3, 2):
+        for copy in smooths:
+            if copy[0] == d:
+                copy[1].wait()
+        add_levels((e + ens - d) % ens, r.static_grad)
 
 
 def in_hbm(array):
@@ -624,7 +627,6 @@
 def gradients(arrays, ens, scale):
     levels, rows, lanes = arrays["static"].shape
     own = levels // ens
-    members = arrays["control"].shape[0]
     lists, capacity = arrays["index"].shape
     tiles = capacity // LANES
     half_rows = lists // ens * tiles
@@ -657,9 +659,7 @@
         "adjoint": pltpu.VMEM((own, rows, lanes), f32),
         "whole": pltpu.VMEM((levels, rows, lanes), f32),
         "smooth": pltpu.VMEM((levels, rows, lanes), f32),
-        "load": dma((7,)),
-        "control_load": dma((members,)),
-        "pert_load": dma((members,)),
+        "load": dma((9,)),
         "face_send": dma((4,)),
         "face_recv": dma((4,)),
         "halo_send": dma((2, 4)),
@@ -672,8 +672,8 @@
         "back_recv": dma((ens,)),
         "whole_send": dma((ens - 1,)),
         "whole_recv": dma((ens - 1,)),
-        "smooth_send": dma((ens - 1,)),
-        "smooth_recv": dma((ens - 1,)),
+        "smooth_send": dma((ens - 1, own)),
+        "smooth_recv": dma((ens - 1, own)),
     }
     names = scalars + tuple(name + "_hbm" for name in loaded) + ("static_grad", "grad") + tuple(scratch)
     shapes = [arrays["static"].shape, arrays["control"].shape]

time: 72.7 us -> 71.8 us (0.988)
  Pallas kernels: 67.9 us -> 67.1 us
    pallas_call x1, Pallas kernels: 67.9 us -> 67.1 us  [gradients(): pl.pallas_call(functools.partial(kernel, names, scale), in_specs=[SMEM] *...]
where the time goes in v8:
time: 71.8 us; the launch traced here: 70.5 us
  Pallas kernels  67.1 us (93%)
  local copies, waits for them, and re-layouts  2.81 us (4%)
    pallas_call x1, Pallas kernels, gradients(): pl.pallas_call(functools.partial(kernel, names, scale), in_specs=[SMEM] *...  67.1 us
    unnamed x2, local copies, waits for them, and re-layouts  2.81 us

profile of v8, /device:TPU:32, one launch (start us, length us, event | category | flops | bytes accessed | tf_op | source)
XLA Modules:
  0.0 70.5 jit_solution(11291091804573795210)
XLA Ops:
  0.6 67.1 %gradients.1 = (f32[16,64,128]{2,1,0:T(8,128)S(1)}, f32[8,16,64,128]{3,2,1,0:T(8,128)S(1)}) custom-call(f32[16,16]{1,0:T(8,128)} %refs_0_.1, f32[16,16]{1,0:T(8,128)} %refs_1_.1, s32[32]{0:T(128)} %refs_2_.1, f32[16,64,128]{2,1,0:T(8,128)} %bitcast.42, f32[64,128]{1,0:T(8,128)} %bitcast.46, f32[64,128]{1,0:T(8,128)} %bitcast.47, s32[32,1024]{1,0:T(8,128)} %refs_6_.1, ...), custom_call_target="tpu_custom_call" | custom-call | tf_op jit(solution)/shard_map/gradients/pallas_call | solution.py:680
  67.7 0.8 %copy.23 = f32[16,2,4096]{2,1,0:T(2,128)} copy(f32[16,2,4096]{2,1,0:T(2,128)S(1)} %bitcast.39) | data formatting | bytes 1048576
  68.5 2.0 %copy.24 = f32[8,16,2,4096]{3,2,1,0:T(2,128)} copy(f32[8,16,2,4096]{3,2,1,0:T(2,128)S(1)} %bitcast.38) | data formatting | bytes 8388608

commit v9 on v8

--- a/solution.py
+++ b/solution.py
@@ -620,6 +620,17 @@
         add_levels((e + ens - d) % ens, r.static_grad)
 
 
+def store_kernel(static_ref, grad_ref, static_hbm, grad_hbm, sems):
+    members = grad_ref.shape[0]
+    copies = [pltpu.make_async_copy(static_ref, static_hbm, sems.at[members])]
+    for k in range(members):
+        copies.append(pltpu.make_async_copy(grad_ref.at[k], grad_hbm.at[k], sems.at[k]))
+    for copy in copies:
+        copy.start()
+    for copy in copies:
+        copy.wait()
+
+
 def in_hbm(array):
     return pltpu.with_memory_space_constraint(array, pltpu.HBM)
 
@@ -627,6 +638,7 @@
 def gradients(arrays, ens, scale):
     levels, rows, lanes = arrays["static"].shape
     own = levels // ens
+    members = arrays["control"].shape[0]
     lists, capacity = arrays["index"].shape
     tiles = capacity // LANES
     half_rows = lists // ens * tiles
@@ -677,7 +689,7 @@
     }
     names = scalars + tuple(name + "_hbm" for name in loaded) + ("static_grad", "grad") + tuple(scratch)
     shapes = [arrays["static"].shape, arrays["control"].shape]
-    return pl.pallas_call(
+    results = pl.pallas_call(
         functools.partial(kernel, names, scale),
         in_specs=[SMEM] * len(scalars) + [ANY] * len(loaded),
         out_specs=[VMEM, VMEM],
@@ -686,6 +698,15 @@
         compiler_params=params(collective_id=1, has_side_effects=True),
         name="gradients",
     )(*[arrays[name] for name in scalars], *[in_hbm(arrays[name]) for name in loaded])
+    return pl.pallas_call(
+        store_kernel,
+        in_specs=[VMEM, VMEM],
+        out_specs=[ANY, ANY],
+        out_shape=[pltpu.HBM(shape, f32) for shape in shapes],
+        scratch_shapes=[dma((members + 1,))],
+        compiler_params=pltpu.CompilerParams(vmem_limit_bytes=2**20),
+        name="store",
+    )(*[pltpu.with_memory_space_constraint(result, pltpu.VMEM) for result in results])
 
 
 def local(

time: 71.8 us -> 71.3 us (level)
  local copies, waits for them, and re-layouts: 2.81 us -> 0 us
  Pallas kernels: 67.1 us -> 69.3 us
    unnamed x2 -> x0, local copies, waits for them, and re-layouts: 2.81 us -> none
    pallas_call x0 -> x1, Pallas kernels: none -> 2.25 us  [gradients(): pl.pallas_call(store_kernel, in_specs=[VMEM, VMEM], out_specs=[ANY, ANY],...]
where the time goes in v9:
time: 71.3 us; the launch traced here: 70 us
  Pallas kernels  69.3 us (97%)
    pallas_call x1, Pallas kernels, gradients(): pl.pallas_call(functools.partial(kernel, names, scale), in_specs=[SMEM] *...  67.1 us
    pallas_call x1, Pallas kernels, gradients(): pl.pallas_call(store_kernel, in_specs=[VMEM, VMEM], out_specs=[ANY, ANY],...  2.25 us

profile of v9, /device:TPU:32, one launch (start us, length us, event | category | flops | bytes accessed | tf_op | source)
XLA Modules:
  0.0 70.0 jit_solution(13534774477278603961)
XLA Ops:
  0.6 67.1 %gradients.1 = (f32[16,64,128]{2,1,0:T(8,128)S(1)}, f32[8,16,64,128]{3,2,1,0:T(8,128)S(1)}) custom-call(f32[16,16]{1,0:T(8,128)} %refs_0_.1, f32[16,16]{1,0:T(8,128)} %refs_1_.1, s32[32]{0:T(128)} %refs_2_.1, f32[16,64,128]{2,1,0:T(8,128)} %bitcast.40, f32[64,128]{1,0:T(8,128)} %bitcast.44, f32[64,128]{1,0:T(8,128)} %bitcast.45, s32[32,1024]{1,0:T(8,128)} %refs_6_.1, ...), custom_call_target="tpu_custom_call" | custom-call | tf_op jit(solution)/shard_map/gradients/pallas_call | solution.py:692
  67.7 2.3 %store.1 = (f32[16,64,128]{2,1,0:T(8,128)}, f32[8,16,64,128]{3,2,1,0:T(8,128)}) custom-call(f32[16,64,128]{2,1,0:T(8,128)S(1)} %get-tuple-element.6.static_ref, f32[8,16,64,128]{3,2,1,0:T(8,128)S(1)} %get-tuple-element.7.grad_ref), custom_call_target="tpu_custom_call" | custom-call | tf_op jit(solution)/shard_map/store/pallas_call | solution.py:701
